TPU v7x, 128 devices: a whole 4x4x4 slice. The times are simulated.
128 devices in a mesh: along: 16 (over y, x), across: 8 (over z, core).
Axes of the slice: x: 4, y: 4, z: 4, core: 2. Of those that a mesh axis runs over, the one named last changes fastest.
Arguments:
- populations: float32 [19, 512, 256, 128], P(None, 'along', 'across')
- link_cell: int32 [16, 8, 8192], P('along', 'across'), may hold values from 0 to 131071, as said below
- link_dir: int32 [16, 8, 8192], P('along', 'across'), may hold values from 1 to 18
- link_floe: int32 [16, 8, 8192], P('along', 'across'), may hold values from -1 to 262143, as said below
- floe_place: float32 [3, 262144], P(None, ('along', 'across')), may hold values from 0 to 1
- floe_velocity: float32 [6, 262144], P(None, ('along', 'across')), may hold values from -1 to 1
- floe_response: float32 [2, 262144], P(None, ('along', 'across')), may hold values from 0.5 to 5
Outputs:
- relaxed: float32 [19, 512, 256, 128], P(None, 'along', 'across')
- floe_motion: float32 [6, 262144], P(None, ('along', 'across'))
Inputs may be any that keep to these rules, and one draw needn't show every extreme that they name: `link_cell`: within one block the cell numbers of all slots are distinct. `link_floe`: -1 marks an empty slot; a link's floe is owned by a block at most one block away along and across, counting around the ends; some block has no empty slot.
All inputs are finite; a program needn't handle non-finite values.
Results may differ from a plain program's by a relative error of at most 0.00005.
Values sent between devices are 32-bit elements; how exact they have to be, the bound alone decides.
No kernel may reach another device: no remote copies, remote signals or barrier semaphores. Data moves between devices by JAX's collectives and lax.ppermute only.
A program may use at most 256 MiB of HBM per device.

v0:
```python
import functools

import jax
import jax.numpy as jnp
from jax import lax
from jax.experimental import pallas as pl
from jax.experimental.pallas import tpu as pltpu
from jax.sharding import PartitionSpec as P

DIRECTIONS = [
    (0, 0, 0),
    (0, 0, 1),
    (0, 0, -1),
    (1, 0, 0),
    (-1, 0, 0),
    (0, 1, 0),
    (0, -1, 0),
    (1, 1, 0),
    (-1, -1, 0),
    (1, -1, 0),
    (-1, 1, 0),
    (1, 0, 1),
    (-1, 0, -1),
    (1, 0, -1),
    (-1, 0, 1),
    (0, 1, 1),
    (0, -1, -1),
    (0, 1, -1),
    (0, -1, 1),
]
WEIGHTS = [1.0 / 3.0] + [1.0 / 18.0] * 6 + [1.0 / 36.0] * 12
RELAXATION = 1.0 / 0.6
FLOW_SCALE = 0.02
LEVER_SCALE = 64.0

WX = 32
WY = 32
NZ = 128
COLUMNS = WX * WY
MEMBERS = 2048
GROUPS = MEMBERS // 128
STATE_ROWS = 6 * GROUPS
FACE = 5 * WX
EDGE_ROWS = 8
CHUNK = 1024

X_UP = [i for i in range(19) if DIRECTIONS[i][0] == 1]
X_DOWN = [i for i in range(19) if DIRECTIONS[i][0] == -1]
Y_UP = [i for i in range(19) if DIRECTIONS[i][1] == 1]
Y_DOWN = [i for i in range(19) if DIRECTIONS[i][1] == -1]

VMEM_LIMIT = 58 * 1024 * 1024


def opposite(i):
    if i == 0:
        return 0
    return i + 1 if i % 2 == 1 else i - 1


def params():
    return pltpu.CompilerParams(vmem_limit_bytes=VMEM_LIMIT)


def cost(flops, moved):
    return pl.CostEstimate(flops=flops, bytes_accessed=moved, transcendentals=0)


def whole():
    return pl.BlockSpec(memory_space=pltpu.VMEM)


def anywhere():
    return pl.BlockSpec(memory_space=pl.ANY)


def origin_terms(place, velocity):
    px = place[0:1] * float(WX)
    py = place[1:2] * float(WY)
    pz = place[2:3] * float(NZ)
    return px, py, pz


def prepare_kernel(place, velocity, pop, up, down, sem):
    copies = []
    for k in range(5):
        rows = pl.ds(STATE_ROWS + k * WY, WY)
        copies.append(pltpu.make_async_copy(pop.at[X_UP[k], WX - 1], up.at[rows, :], sem.at[0]))
        copies.append(pltpu.make_async_copy(pop.at[X_DOWN[k], 0], down.at[rows, :], sem.at[0]))
    for copy in copies:
        copy.start()
    px, py, pz = origin_terms(place, velocity)
    wx, wy, wz = velocity[3:4], velocity[4:5], velocity[5:6]
    scale = 1.0 / LEVER_SCALE
    values = [
        velocity[0:1] - (wy * pz - wz * py) * scale,
        velocity[1:2] - (wz * px - wx * pz) * scale,
        velocity[2:3] - (wx * py - wy * px) * scale,
        wx,
        wy,
        wz,
    ]
    for c in range(6):
        for b in range(GROUPS):
            row = values[c][:, b * 128 : (b + 1) * 128]
            up[c * GROUPS + b : c * GROUPS + b + 1, :] = row
            down[c * GROUPS + b : c * GROUPS + b + 1, :] = row
    for copy in copies:
        copy.wait()


def prepare(place, velocity, populations):
    shape = jax.ShapeDtypeStruct((STATE_ROWS + FACE, 128), jnp.float32)
    return pl.pallas_call(
        prepare_kernel,
        out_shape=(shape, shape),
        in_specs=[whole(), whole(), anywhere()],
        out_specs=(whole(), whole()),
        scratch_shapes=[pltpu.SemaphoreType.DMA((1,))],
        compiler_params=params(),
        cost_estimate=cost(100_000, 600_000),
        name="prepare",
    )(place, velocity, populations)


def column_hot(cell):
    low = jnp.bitwise_and(jnp.right_shift(cell, 7), 511)
    rows = lax.broadcasted_iota(jnp.int32, (512, cell.shape[1]), 0)
    return jnp.where(rows == low, 1.0, 0.0).astype(jnp.bfloat16)


def depth_mask(cell):
    depth = jnp.bitwise_or(
        jnp.left_shift(jnp.right_shift(cell, 16), 7), jnp.bitwise_and(cell, 127)
    )
    rows = lax.broadcasted_iota(jnp.int32, (256, cell.shape[1]), 0)
    return rows == depth


NT = (((1,), (1,)), ((), ()))
NN = (((1,), (0,)), ((), ()))


def product(a, b, dims):
    return lax.dot_general(a, b, dims, preferred_element_type=jnp.float32)


def pick_kernel(cell, heading, floe, pop_hbm, dense, picked, up, down, pop, chosen, sem):
    load = pltpu.make_async_copy(pop_hbm, pop, sem.at[0])
    load.start()
    chosen[...] = jnp.zeros_like(chosen)

    def scatter(step, carry):
        at = pl.ds(pl.multiple_of(step * CHUNK, CHUNK), CHUNK)
        own = cell[:, at]
        value = jnp.where(floe[:, at] >= 0, heading[:, at], 0).astype(jnp.float32)
        hot = column_hot(own)
        payload = jnp.where(depth_mask(own), value, 0.0).astype(jnp.bfloat16)
        chosen[...] += product(hot, payload, NT)
        return carry

    lax.fori_loop(0, cell.shape[1] // CHUNK, scatter, 0)
    dense[0:512] = chosen[:, 0:128]
    dense[512:1024] = chosen[:, 128:256]
    load.wait()

    def select(step, carry):
        rows = pl.ds(pl.multiple_of(step * 32, 32), 32)
        for half in range(2):
            where = chosen[rows, half * 128 : (half + 1) * 128]
            source = pl.ds(pl.multiple_of(step * 32, 32) + half * 512, 32)
            value = jnp.zeros((32, 128), jnp.float32)
            for i in range(1, 19):
                value = jnp.where(where == float(i), pop[i, source, :], value)
            chosen[rows, half * 128 : (half + 1) * 128] = value
        return carry

    lax.fori_loop(0, 16, select, 0)
    turned = jnp.transpose(chosen[...])
    high = turned.astype(jnp.bfloat16)
    picked[0:256] = high
    picked[256:512] = (turned - high.astype(jnp.float32)).astype(jnp.bfloat16)
    for k in range(5):
        up[k * WX : (k + 1) * WX, :] = pop[Y_UP[k], pl.ds(WY - 1, WX, stride=WY), :]
        down[k * WX : (k + 1) * WX, :] = pop[Y_DOWN[k], pl.ds(0, WX, stride=WY), :]


def pick(cell, heading, floe, columns):
    face = jax.ShapeDtypeStruct((FACE, 128), jnp.float32)
    return pl.pallas_call(
        pick_kernel,
        out_shape=(
            jax.ShapeDtypeStruct((COLUMNS, NZ), jnp.float32),
            jax.ShapeDtypeStruct((512, 512), jnp.bfloat16),
            face,
            face,
        ),
        in_specs=[whole(), whole(), whole(), anywhere()],
        out_specs=(whole(),) * 4,
        scratch_shapes=[
            pltpu.VMEM(columns.shape, jnp.float32),
            pltpu.VMEM((512, 256), jnp.float32),
            pltpu.SemaphoreType.DMA((1,)),
        ],
        compiler_params=params(),
        cost_estimate=cost(2_200_000_000, 12_000_000),
        name="pick",
    )(cell, heading, floe, columns)


def gather_kernel(cell, picked, out):
    def step(t, carry):
        at = pl.ds(pl.multiple_of(t * CHUNK, CHUNK), CHUNK)
        own = cell[:, at]
        values = product(picked[...], column_hot(own), NN)
        values = values[0:256] + values[256:512]
        out[:, at] = jnp.sum(jnp.where(depth_mask(own), values, 0.0), axis=0, keepdims=True)
        return carry

    lax.fori_loop(0, cell.shape[1] // CHUNK, step, 0)


def gather(cell, picked):
    return pl.pallas_call(
        gather_kernel,
        out_shape=jax.ShapeDtypeStruct(cell.shape, jnp.float32),
        in_specs=[whole(), whole()],
        out_specs=whole(),
        compiler_params=params(),
        cost_estimate=cost(4_300_000_000, 1_000_000),
        name="gather",
    )(cell, picked)


def bits(table, heading):
    word = 0
    for i in table:
        word |= 1 << i
    return jnp.bitwise_and(jnp.right_shift(jnp.full_like(heading, word), heading), 1)


def component(axis, heading):
    plus = [i for i in range(19) if DIRECTIONS[i][axis] == 1]
    minus = [i for i in range(19) if DIRECTIONS[i][axis] == -1]
    return (bits(plus, heading) - bits(minus, heading)).astype(jnp.float32)


def floe_kernel(
    sizes, place, cell, heading, floe, here, mine, low, high, left, right,
    taken, loads_left, loads_mid, loads_right, table, spread, payload, total,
):
    size_along, size_across = sizes
    a = place[0]
    b = place[1]
    links = cell.shape[1]
    for ra in range(3):
        for rb in range(3):
            if rb == 0:
                state = left[ra * STATE_ROWS : (ra + 1) * STATE_ROWS]
            elif rb == 2:
                state = right[ra * STATE_ROWS : (ra + 1) * STATE_ROWS]
            else:
                state = (low, mine, high)[ra][0:STATE_ROWS]
            region = ra * 3 + rb
            lanes = slice(region * 128, (region + 1) * 128)
            first = state.astype(jnp.bfloat16)
            table[0:STATE_ROWS, lanes] = first
            table[STATE_ROWS : 2 * STATE_ROWS, lanes] = (
                state - first.astype(jnp.float32)
            ).astype(jnp.bfloat16)
    total[...] = jnp.zeros_like(total)
    payload[...] = jnp.zeros_like(payload)

    def step(t, carry):
        at = pl.ds(pl.multiple_of(t * CHUNK, CHUNK), CHUNK)
        k = cell[:, at]
        d = heading[:, at]
        g = floe[:, at]
        active = g >= 0
        owner = jnp.right_shift(g, 11)
        ra = jnp.bitwise_and(owner // size_across - a + 1, size_along - 1)
        rb = jnp.bitwise_and(jnp.bitwise_and(owner, size_across - 1) - b + 1, size_across - 1)
        member = jnp.bitwise_and(g, MEMBERS - 1)
        group = jnp.where(active, jnp.right_shift(member, 7), -1)
        entry = (ra * 3 + rb) * 128 + jnp.bitwise_and(member, 127)
        rows = lax.broadcasted_iota(jnp.int32, (9 * 128, CHUNK), 0)
        pick_floe = jnp.where(rows == entry, 1.0, 0.0).astype(jnp.bfloat16)
        groups = lax.broadcasted_iota(jnp.int32, (GROUPS, CHUNK), 0)
        mask = jnp.where(groups == group, 1.0, 0.0)

        cx = component(0, d)
        cy = component(1, d)
        cz = component(2, d)
        weight = jnp.where(d <= 6, WEIGHTS[1], WEIGHTS[7])
        lx = jnp.right_shift(k, 12)
        ly = jnp.bitwise_and(jnp.right_shift(k, 7), 31)
        lz = jnp.bitwise_and(k, 127)
        rx = ((1 - ra) * WX + lx).astype(jnp.float32) + 0.5 * cx
        ry = ((1 - rb) * WY + ly).astype(jnp.float32) + 0.5 * cy
        rz = lz.astype(jnp.float32) + 0.5 * cz
        scale = 1.0 / LEVER_SCALE
        coefficients = [
            cx,
            cy,
            cz,
            (ry * cz - rz * cy) * scale,
            (rz * cx - rx * cz) * scale,
            (rx * cy - ry * cx) * scale,
        ]
        for c in range(6):
            spread[c * GROUPS : (c + 1) * GROUPS, :] = mask * coefficients[c]

        state = product(table[...], pick_floe, NN)
        state = state[0:STATE_ROWS] + state[STATE_ROWS : 2 * STATE_ROWS]
        weights = spread[...]
        speed = jnp.sum(state * weights, axis=0, keepdims=True)
        take = (6.0 * FLOW_SCALE) * weight * speed
        magnitude = 2.0 * here[:, at] - take
        taken[:, at] = take
        amount = weights * magnitude
        first = amount.astype(jnp.bfloat16)
        payload[0:STATE_ROWS, :] = first
        payload[128 : 128 + STATE_ROWS, :] = (amount - first.astype(jnp.float32)).astype(
            jnp.bfloat16
        )
        total[...] += product(pick_floe, payload[...], NT)
        return carry

    lax.fori_loop(0, links // CHUNK, step, 0)
    for ra in range(3):
        for rb in range(3):
            rows = slice((ra * 3 + rb) * 128, (ra * 3 + rb + 1) * 128)
            summed = total[rows, 0:128] + total[rows, 128:256]
            out = (loads_left, loads_mid, loads_right)[rb]
            out[ra * STATE_ROWS : (ra + 1) * STATE_ROWS] = jnp.transpose(summed)[0:STATE_ROWS]


def floes(sizes, place, cell, heading, floe, here, mine, low, high, left, right):
    loads = jax.ShapeDtypeStruct((3 * STATE_ROWS, 128), jnp.float32)
    return pl.pallas_call(
        functools.partial(floe_kernel, sizes),
        out_shape=(jax.ShapeDtypeStruct(cell.shape, jnp.float32), loads, loads, loads),
        in_specs=[pl.BlockSpec(memory_space=pltpu.SMEM)] + [whole()] * 9,
        out_specs=(whole(),) * 4,
        scratch_shapes=[
            pltpu.VMEM((2 * STATE_ROWS, 9 * 128), jnp.bfloat16),
            pltpu.VMEM((STATE_ROWS, CHUNK), jnp.float32),
            pltpu.VMEM((256, CHUNK), jnp.bfloat16),
            pltpu.VMEM((9 * 128, 256), jnp.float32),
        ],
        compiler_params=params(),
        cost_estimate=cost(8_000_000_000, 2_000_000),
        name="floes",
    )(place, cell, heading, floe, here, mine, low, high, left, right)


def spread_kernel(cell, taken, dense, total):
    total[...] = jnp.zeros_like(total)

    def step(t, carry):
        at = pl.ds(pl.multiple_of(t * CHUNK, CHUNK), CHUNK)
        own = cell[:, at]
        value = taken[:, at]
        first = value.astype(jnp.bfloat16).astype(jnp.float32)
        mask = depth_mask(own)
        payload = jnp.concatenate(
            [
                jnp.where(mask, first, 0.0).astype(jnp.bfloat16),
                jnp.where(mask, value - first, 0.0).astype(jnp.bfloat16),
            ],
            axis=0,
        )
        total[...] += product(column_hot(own), payload, NT)
        return carry

    lax.fori_loop(0, cell.shape[1] // CHUNK, step, 0)
    dense[0:512] = total[:, 0:128] + total[:, 256:384]
    dense[512:1024] = total[:, 128:256] + total[:, 384:512]


def spread_out(cell, taken):
    return pl.pallas_call(
        spread_kernel,
        out_shape=jax.ShapeDtypeStruct((COLUMNS, NZ), jnp.float32),
        in_specs=[whole(), whole()],
        out_specs=whole(),
        scratch_shapes=[pltpu.VMEM((512, 512), jnp.float32)],
        compiler_params=params(),
        cost_estimate=cost(4_300_000_000, 1_000_000),
        name="spread",
    )(cell, taken)


SLAB = 4
SLABS = WX // SLAB
TOP = 8


def collide_kernel(
    dense_dir, dense_take, low, high, left, right, pop_hbm, out_hbm, pop, out, load_sem, store_sem
):
    def loading(s):
        return pltpu.make_async_copy(
            pop_hbm.at[:, pl.ds(s * SLAB, SLAB)],
            pop.at[:, pl.ds(1 + s * SLAB, SLAB), pl.ds(TOP, WY), :],
            load_sem.at[s],
        )

    for s in range(SLABS):
        loading(s).start()
    for k in range(5):
        rows = slice(STATE_ROWS + k * WY, STATE_ROWS + (k + 1) * WY)
        pop[X_UP[k], 0, TOP : TOP + WY, :] = low[rows, :]
        pop[X_DOWN[k], WX + 1, TOP : TOP + WY, :] = high[rows, :]
    base = 3 * STATE_ROWS
    for k in range(5):
        for x in range(WX):
            row = base + k * WX + x
            pop[Y_UP[k], 1 + x, TOP - 1 : TOP, :] = left[row : row + 1, :]
            pop[Y_DOWN[k], 1 + x, TOP + WY : TOP + WY + 1, :] = right[row : row + 1, :]
    edge = base + FACE
    pop[7, 0, TOP - 1 : TOP, :] = left[edge : edge + 1, :]
    pop[10, WX + 1, TOP - 1 : TOP, :] = left[edge + 1 : edge + 2, :]
    pop[9, 0, TOP + WY : TOP + WY + 1, :] = right[edge : edge + 1, :]
    pop[8, WX + 1, TOP + WY : TOP + WY + 1, :] = right[edge + 1 : edge + 2, :]

    def storing(s, slot):
        return pltpu.make_async_copy(
            out.at[slot], out_hbm.at[:, pl.ds(s * SLAB, SLAB)], store_sem.at[slot]
        )

    lane = lax.broadcasted_iota(jnp.int32, (8, 128), 1)
    first_lane = lane == 0
    last_lane = lane == NZ - 1
    rest = 1.0 - RELAXATION

    def tile(x, j, slot, inner):
        row = pl.multiple_of(x * WY, WY) + j * 8
        where = dense_dir[pl.ds(row, 8), :]
        take = dense_take[pl.ds(row, 8), :]

        def plain(i):
            return pop[i, x + 1, TOP + j * 8 : TOP + j * 8 + 8, :]

        def bounded(i, back):
            step_x, step_y, step_z = DIRECTIONS[i]
            start = TOP + j * 8 - step_y
            value = pop[i, x + 1 - step_x, start : start + 8, :]
            if step_z == 1:
                value = jnp.where(first_lane, back, pltpu.roll(value, 1, 1))
            elif step_z == -1:
                value = jnp.where(last_lane, back, pltpu.roll(value, NZ - 1, 1))
            return jnp.where(where == float(opposite(i)), back - take, value)

        centre = plain(0)
        density = centre
        both = []
        apart = []
        for i in range(1, 19, 2):
            plus = bounded(i, plain(i + 1))
            minus = bounded(i + 1, plain(i))
            both.append((plus, minus))
            apart.append(plus - minus)
            density = density + (plus + minus)
        d1, d3, d5, d7, d9, d11, d13, d15, d17 = apart
        mx = (d3 + d7) + (d9 + d11) + d13
        my = (d5 + d7) + (d15 - d9) + d17
        mz = (d1 + d11) + (d15 - d13) - d17
        inverse = 1.0 / density
        ux = mx * inverse
        uy = my * inverse
        uz = mz * inverse
        scaled = density * RELAXATION
        flat = scaled * (1.0 - 1.5 * (ux * ux + uy * uy + uz * uz))
        linear = 3.0 * scaled
        square = 4.5 * scaled
        out[slot, 0, inner, j * 8 : j * 8 + 8, :] = rest * centre + WEIGHTS[0] * flat
        for n in range(9):
            i = 2 * n + 1
            step_x, step_y, step_z = DIRECTIONS[i]
            projection = None
            for step, u in ((step_x, ux), (step_y, uy), (step_z, uz)):
                if step == 0:
                    continue
                if projection is None:
                    projection = u
                else:
                    projection = projection + u if step == 1 else projection - u
            even = WEIGHTS[i] * (flat + square * (projection * projection))
            odd = WEIGHTS[i] * (linear * projection)
            plus, minus = both[n]
            out[slot, i, inner, j * 8 : j * 8 + 8, :] = rest * plus + (even + odd)
            out[slot, i + 1, inner, j * 8 : j * 8 + 8, :] = rest * minus + (even - odd)

    loading(0).wait()

    def slab(s, carry):
        slot = lax.rem(s, 2)

        @pl.when(s + 1 < SLABS)
        def _():
            loading(s + 1).wait()

        @pl.when(s >= 2)
        def _():
            storing(s - 2, slot).wait()

        def plane(inner, inside):
            for j in range(WY // 8):
                tile(s * SLAB + inner, j, slot, inner)
            return inside

        lax.fori_loop(0, SLAB, plane, 0)
        storing(s, slot).start()
        return carry

    lax.fori_loop(0, SLABS, slab, 0)
    storing(SLABS - 2, (SLABS - 2) % 2).wait()
    storing(SLABS - 1, (SLABS - 1) % 2).wait()


def collide(dense_dir, dense_take, low, high, left, right, populations):
    return pl.pallas_call(
        collide_kernel,
        out_shape=jax.ShapeDtypeStruct(populations.shape, jnp.float32),
        in_specs=[whole()] * 6 + [anywhere()],
        out_specs=anywhere(),
        scratch_shapes=[
            pltpu.VMEM((19, WX + 2, WY + 16, NZ), jnp.float32),
            pltpu.VMEM((2, 19, SLAB, WY, NZ), jnp.float32),
            pltpu.SemaphoreType.DMA((SLABS,)),
            pltpu.SemaphoreType.DMA((2,)),
        ],
        compiler_params=params(),
        cost_estimate=cost(40_000_000, 24_000_000),
        name="collide",
    )(dense_dir, dense_take, low, high, left, right, populations)


def motion_kernel(own, low, high, place, velocity, response, out):
    loads = own[...] + low[...] + high[...]
    px, py, pz = origin_terms(place, velocity)
    scale = 1.0 / LEVER_SCALE
    for b in range(GROUPS):
        lanes = slice(b * 128, (b + 1) * 128)

        def load(c):
            return loads[c * GROUPS + b : c * GROUPS + b + 1, :]

        fx, fy, fz = load(0), load(1), load(2)
        qx, qy, qz = px[:, lanes], py[:, lanes], pz[:, lanes]
        torques = [
            load(3) - (qy * fz - qz * fy) * scale,
            load(4) - (qz * fx - qx * fz) * scale,
            load(5) - (qx * fy - qy * fx) * scale,
        ]
        for c, value in enumerate((fx, fy, fz)):
            out[c : c + 1, lanes] = velocity[c : c + 1, lanes] + response[0:1, lanes] * value
        for c, value in enumerate(torques):
            out[c + 3 : c + 4, lanes] = (
                velocity[c + 3 : c + 4, lanes] + response[1:2, lanes] * value
            )


def motion(own, low, high, place, velocity, response):
    return pl.pallas_call(
        motion_kernel,
        out_shape=jax.ShapeDtypeStruct(velocity.shape, jnp.float32),
        in_specs=[whole()] * 6,
        out_specs=whole(),
        compiler_params=params(),
        cost_estimate=cost(200_000, 300_000),
        name="motion",
    )(own, low, high, place, velocity, response)


def shifted(value, axis, step):
    count = lax.axis_size(axis)
    return lax.ppermute(value, axis, [(i, (i + step) % count) for i in range(count)])


def body(populations, link_cell, link_dir, link_floe, floe_place, floe_velocity, floe_response):
    sizes = (lax.axis_size("along"), lax.axis_size("across"))
    where = jnp.stack([lax.axis_index("along"), lax.axis_index("across")]).astype(jnp.int32)
    links = link_cell.shape[-1]
    cell = link_cell.reshape(1, links)
    heading = link_dir.reshape(1, links)
    floe = link_floe.reshape(1, links)
    columns = populations.reshape(19, COLUMNS, NZ)

    up, down = prepare(floe_place, floe_velocity, populations)
    low = shifted(up, "along", 1)
    high = shifted(down, "along", -1)
    dense_dir, picked, face_up, face_down = pick(cell, heading, floe, columns)

    def rows(block, k, y):
        at = STATE_ROWS + k * WY + y
        return block[at : at + 1]

    states = [low[:STATE_ROWS], up[:STATE_ROWS], high[:STATE_ROWS]]
    filler = jnp.zeros((EDGE_ROWS - 2, 128), jnp.float32)
    to_up = jnp.concatenate(
        states + [face_up, rows(low, X_UP.index(7), WY - 1), rows(high, X_DOWN.index(10), WY - 1)]
        + [filler]
    )
    to_down = jnp.concatenate(
        states + [face_down, rows(low, X_UP.index(9), 0), rows(high, X_DOWN.index(8), 0), filler]
    )
    left = shifted(to_up, "across", 1)
    right = shifted(to_down, "across", -1)
    here = gather(cell, picked)
    taken, loads_left, loads_mid, loads_right = floes(
        sizes, where, cell, heading, floe, here, up, low, high, left, right
    )
    from_right = shifted(loads_left, "across", -1)
    from_left = shifted(loads_right, "across", 1)
    dense_take = spread_out(cell, taken)
    three = loads_mid + from_left + from_right
    from_high = shifted(three[:STATE_ROWS], "along", -1)
    from_low = shifted(three[2 * STATE_ROWS :], "along", 1)
    relaxed = collide(dense_dir, dense_take, low, high, left, right, populations)
    moved = motion(
        three[STATE_ROWS : 2 * STATE_ROWS],
        from_low,
        from_high,
        floe_place,
        floe_velocity,
        floe_response,
    )
    return relaxed, moved


def solution(mesh):
    placed = (
        P(None, "along", "across", None),
        P("along", "across", None),
        P("along", "across", None),
        P("along", "across", None),
        P(None, ("along", "across")),
        P(None, ("along", "across")),
        P(None, ("along", "across")),
    )
    return jax.shard_map(
        body,
        mesh=mesh,
        in_specs=placed,
        out_specs=(P(None, "along", "across", None), P(None, ("along", "across"))),
        check_vma=False,
    )
```

profile of v0, /device:TPU:0, one launch (start us, length us, event | category | flops | bytes accessed | tf_op | source)
XLA Modules:
  0.0 81.4 jit_solution(190182726737215456)
XLA Ops:
  0.6 2.4 %prepare.1 = (f32[256,128]{1,0:T(8,128)}, f32[256,128]{1,0:T(8,128)}) custom-call(f32[3,2048]{1,0:T(4,128)} %place.3, f32[6,2048]{1,0:T(8,128)} %velocity.3, f32[19,32,32,128]{3,2,1,0:T(8,128)} %pop_hbm.1), custom_call_target="tpu_custom_call" | custom-call | flops 100000 | bytes 600000 | tf_op jit(solution)/shard_map/prepare/pallas_call | solution.py:114
  3.1 5.4 %collective-permute-start.1 = (f32[256,128]{1,0:T(8,128)}, f32[256,128]{1,0:T(8,128)S(1)}, u32[]{:S(2)}, u32[]{:S(2)}) collective-permute-start(f32[256,128]{1,0:T(8,128)} %get-tuple-element.15), channel_id=1, source_target_pairs={{0,120},{8,0},{16,8},{24,16},{32,24},{40,32},{48,40},{56,48},{64,5... | collective-permute-start | bytes 393224 | tf_op jit(solution)/shard_map/ppermute | solution.py:579
  8.4 0.0 collective-permute-start
  8.4 0.8 %slice.31 = f32[96,128]{1,0:T(8,128)S(1)} slice(f32[256,128]{1,0:T(8,128)} %get-tuple-element.14.mine), slice={[0:96], [0:128]} | slice | bytes 98304 | tf_op jit(solution)/shard_map/slice | solution.py:600
  9.3 6.6 %pick.1 = (f32[1024,128]{1,0:T(8,128)}, bf16[512,512]{1,0:T(8,128)(2,1)}, f32[160,128]{1,0:T(8,128)}, f32[160,128]{1,0:T(8,128)}) custom-call(s32[1,8192]{1,0:T(1,128)} %bitcast.11, s32[1,8192]{1,0:T(1,128)} %bitcast.7, s32[1,8192]{1,0:T(1,128)} %bitcast.9, f32[19,1024,128]{2,1,0:T(8,128)} %bitcast.6), custom_call_target="tpu_custom_call" | custom-call | flops 2200000000 | bytes 12000000 | tf_op jit(solution)/shard_map/pick/pallas_call | solution.py:190
  15.9 0.0 collective-permute-done.1.high
  15.9 0.0 copy-start
  15.9 1.0 %collective-permute-done.low = f32[256,128]{1,0:T(8,128)S(1)} collective-permute-done((f32[256,128]{1,0:T(8,128)}, f32[256,128]{1,0:T(8,128)S(1)}, u32[]{:S(2)}, u32[]{:S(2)}) %collective-permute-start) | collective-permute-done | bytes 131104 | tf_op jit(solution)/shard_map/ppermute | solution.py:579
  16.9 0.0 copy-start.1
  17.0 1.0 %concatenate.7 = f32[456,128]{1,0:T(8,128)S(1)} concatenate(f32[96,128]{1,0:T(8,128)S(1)} %slice.40, f32[96,128]{1,0:T(8,128)S(1)} %slice.31, f32[96,128]{1,0:T(8,128)S(1)} %slice.41, f32[160,128]{1,0:T(8,128)} %get-tuple-element.17, f32[1,128]{1,0:T(1,128)S(1)} %get-tuple-element.27, f32[1,128]{1,0:T(1,128)S(1)} %get-tuple-element.25, f32[6,128]{1,0:T(8,128)S(1)} %broadcast_in_dim.3), dimensions={0} | concatenate | bytes 466944 | tf_op jit(solution)/shard_map/concatenate | solution.py:606
  17.9 2.2 %collective-permute-start.3 = (f32[456,128]{1,0:T(8,128)S(1)}, f32[456,128]{1,0:T(8,128)S(1)}, u32[]{:S(2)}, u32[]{:S(2)}) collective-permute-start(f32[456,128]{1,0:T(8,128)S(1)} %concatenate.7), channel_id=1, source_target_pairs={{0,7},{1,0},{2,1},{3,2},{4,3},{5,4},{6,5},{7,6},{8,15},{9,8},{10,9... | collective-permute-start | bytes 700424 | tf_op jit(solution)/shard_map/ppermute | solution.py:579
  20.1 0.9 %concatenate.6 = f32[456,128]{1,0:T(8,128)S(1)} concatenate(f32[96,128]{1,0:T(8,128)S(1)} %slice.40, f32[96,128]{1,0:T(8,128)S(1)} %slice.31, f32[96,128]{1,0:T(8,128)S(1)} %slice.41, f32[160,128]{1,0:T(8,128)} %get-tuple-element.16, f32[1,128]{1,0:T(1,128)S(1)} %get-tuple-element.28, f32[1,128]{1,0:T(1,128)S(1)} %get-tuple-element.26, f32[6,128]{1,0:T(8,128)S(1)} %broadcast_in_dim.3), dimensions={0} | concatenate | bytes 466944 | tf_op jit(solution)/shard_map/concatenate | solution.py:602
  21.0 0.0 collective-permute-start.2
  21.1 7.5 %gather.1.here = f32[1,8192]{1,0:T(1,128)} custom-call(s32[1,8192]{1,0:T(1,128)} %bitcast.12, bf16[512,512]{1,0:T(8,128)(2,1)} %get-tuple-element.13.picked), custom_call_target="tpu_custom_call" | custom-call | flops 4300000256 | bytes 1000000 | tf_op jit(solution)/shard_map/gather/pallas_call | solution.py:224
  28.6 0.6 pad_add_fusion.place
  29.2 0.0 collective-permute-done.3.right
  29.2 0.0 copy-start.2
  29.2 0.0 collective-permute-done.2.left
  29.2 0.0 copy-done
  29.2 0.0 copy-done.1
  29.2 0.7 copy-done.2
  29.9 0.0 copy-start.3
  29.9 0.7 copy-done.3
  30.6 16.9 %floes.1 = (f32[1,8192]{1,0:T(1,128)}, f32[288,128]{1,0:T(8,128)}, f32[288,128]{1,0:T(8,128)}, f32[288,128]{1,0:T(8,128)}) custom-call(s32[2]{0:T(128)} %pad_add_fusion.place, s32[1,8192]{1,0:T(1,128)} %bitcast.13, s32[1,8192]{1,0:T(1,128)} %bitcast.8, s32[1,8192]{1,0:T(1,128)} %bitcast.10, f32[1,8192]{1,0:T(1,128)} %gather.1.here, ...), custom_call_target="tpu_custom_call" | custom-call | flops 8000000000 | bytes 2000000 | tf_op jit(solution)/shard_map/floes/pallas_call | solution.py:340
  47.5 0.0 collective-permute-start.4
  47.5 3.0 %collective-permute-start.5 = (f32[288,128]{1,0:T(8,128)}, f32[288,128]{1,0:T(8,128)S(1)}, u32[]{:S(2)}, u32[]{:S(2)}) collective-permute-start(f32[288,128]{1,0:T(8,128)} %get-tuple-element.21), channel_id=1, source_target_pairs={{0,7},{1,0},{2,1},{3,2},{4,3},{5,4},{6,5},{7,6},{8,15},{9,8},{10,9... | collective-permute-start | bytes 442376 | tf_op jit(solution)/shard_map/ppermute | solution.py:579
  50.5 3.0 %collective-permute-done.4 = f32[288,128]{1,0:T(8,128)S(1)} collective-permute-done((f32[288,128]{1,0:T(8,128)}, f32[288,128]{1,0:T(8,128)S(1)}, u32[]{:S(2)}, u32[]{:S(2)}) %collective-permute-start.4) | collective-permute-done | bytes 147488 | tf_op jit(solution)/shard_map/ppermute | solution.py:579
  53.5 0.0 collective-permute-done.5
  53.5 0.9 %add_add_fusion = f32[288,128]{1,0:T(8,128)S(1)} fusion(f32[288,128]{1,0:T(8,128)S(1)} %collective-permute-done.5, f32[288,128]{1,0:T(8,128)} %get-tuple-element.19, f32[288,128]{1,0:T(8,128)S(1)} %collective-permute-done.4), kind=kLoop, calls=%fused_computation | loop fusion | flops 73728 | bytes 589824 | tf_op jit(solution)/shard_map/add | solution.py:618
  54.4 0.6 fusion
  55.1 5.1 %collective-permute-start.7 = (f32[96,128]{1,0:T(8,128)S(1)}, f32[96,128]{1,0:T(8,128)S(1)}, u32[]{:S(2)}, u32[]{:S(2)}) collective-permute-start(f32[96,128]{1,0:T(8,128)S(1)} %get-tuple-element.22), channel_id=1, source_target_pairs={{0,120},{8,0},{16,8},{24,16},{32,24},{40,32},{48,40},{56,48},{64,5... | collective-permute-start | bytes 147464 | tf_op jit(solution)/shard_map/ppermute | solution.py:579
  60.1 0.0 collective-permute-start.6
  60.1 7.8 %spread.1.dense_take = f32[1024,128]{1,0:T(8,128)} custom-call(s32[1,8192]{1,0:T(1,128)} %bitcast.14, f32[1,8192]{1,0:T(1,128)} %get-tuple-element.18.taken), custom_call_target="tpu_custom_call" | custom-call | flops 4300000256 | bytes 1000000 | tf_op jit(solution)/shard_map/spread/pallas_call | solution.py:382
  67.9 11.1 %collide.1 = f32[19,32,32,128]{3,2,1,0:T(8,128)} custom-call(f32[1024,128]{1,0:T(8,128)} %get-tuple-element.12.dense_dir, f32[1024,128]{1,0:T(8,128)} %spread.1.dense_take, f32[256,128]{1,0:T(8,128)} %copy-done.1, f32[256,128]{1,0:T(8,128)} %copy-done, f32[456,128]{1,0:T(8,128)} %copy-done.3, f32[456,128]{1,0:T(8,128)} %copy-done.2, f32[19,32,32,128]{3,2,1,0:T(8,128)} %pop_hbm.1), custom_call_target="tpu_custom_call" | custom-call | flops 40000000 | bytes 24000000 | tf_op jit(solution)/shard_map/collide/pallas_call | solution.py:523
  79.1 0.0 collective-permute-done.7.high
  79.1 0.0 copy-start.4
  79.1 0.0 collective-permute-done.6.low
  79.1 0.0 copy-start.5
  79.1 0.6 copy-done.4
  79.7 0.0 copy-done.5
  79.7 1.7 %motion.1 = f32[6,2048]{1,0:T(8,128)} custom-call(f32[96,128]{1,0:T(8,128)} %get-tuple-element.24.own, f32[96,128]{1,0:T(8,128)} %copy-done.5, f32[96,128]{1,0:T(8,128)} %copy-done.4, f32[3,2048]{1,0:T(4,128)} %place.3, f32[6,2048]{1,0:T(8,128)} %velocity.3, f32[2,2048]{1,0:T(2,128)} %response.1), custom_call_target="tpu_custom_call" | custom-call | flops 200000 | bytes 300000 | tf_op jit(solution)/shard_map/motion/pallas_call | solution.py:566
  (5 shorter events, 0.0 us)
Async XLA Ops:
  3.1 12.8 %collective-permute-start.1 = (f32[256,128]{1,0:T(8,128)}, f32[256,128]{1,0:T(8,128)S(1)}, u32[]{:S(2)}, u32[]{:S(2)}) collective-permute-start(f32[256,128]{1,0:T(8,128)} %get-tuple-element.15), channel_id=1, source_target_pairs={{0,120},{8,0},{16,8},{24,16},{32,24},{40,32},{48,40},{56,48},{64,5... | collective-permute-start | bytes 393224 | tf_op jit(solution)/shard_map/ppermute | solution.py:579
  8.4 8.5 %collective-permute-start = (f32[256,128]{1,0:T(8,128)}, f32[256,128]{1,0:T(8,128)S(1)}, u32[]{:S(2)}, u32[]{:S(2)}) collective-permute-start(f32[256,128]{1,0:T(8,128)} %get-tuple-element.14.mine), channel_id=1, source_target_pairs={{0,8},{8,16},{16,24},{24,32},{32,40},{40,48},{48,56},{56,64},{64,7... | collective-permute-start | bytes 393224 | tf_op jit(solution)/shard_map/ppermute | solution.py:579
  15.9 13.3 %copy-start = (f32[256,128]{1,0:T(8,128)}, f32[256,128]{1,0:T(8,128)S(1)}, u32[]{:S(2)}) copy-start(f32[256,128]{1,0:T(8,128)S(1)} %collective-permute-done.1.high) | copy-start | bytes 393220
  16.9 12.3 %copy-start.1 = (f32[256,128]{1,0:T(8,128)}, f32[256,128]{1,0:T(8,128)S(1)}, u32[]{:S(2)}) copy-start(f32[256,128]{1,0:T(8,128)S(1)} %collective-permute-done.low) | copy-start | bytes 393220
  17.9 11.3 %collective-permute-start.3 = (f32[456,128]{1,0:T(8,128)S(1)}, f32[456,128]{1,0:T(8,128)S(1)}, u32[]{:S(2)}, u32[]{:S(2)}) collective-permute-start(f32[456,128]{1,0:T(8,128)S(1)} %concatenate.7), channel_id=1, source_target_pairs={{0,7},{1,0},{2,1},{3,2},{4,3},{5,4},{6,5},{7,6},{8,15},{9,8},{10,9... | collective-permute-start | bytes 700424 | tf_op jit(solution)/shard_map/ppermute | solution.py:579
  21.0 8.1 %collective-permute-start.2 = (f32[456,128]{1,0:T(8,128)S(1)}, f32[456,128]{1,0:T(8,128)S(1)}, u32[]{:S(2)}, u32[]{:S(2)}) collective-permute-start(f32[456,128]{1,0:T(8,128)S(1)} %concatenate.6), channel_id=1, source_target_pairs={{0,1},{1,2},{2,3},{3,4},{4,5},{5,6},{6,7},{7,0},{8,9},{9,10},{10,1... | collective-permute-start | bytes 700424 | tf_op jit(solution)/shard_map/ppermute | solution.py:579
  29.2 0.7 copy-start.2
  29.9 0.7 copy-start.3
  47.5 6.0 %collective-permute-start.4 = (f32[288,128]{1,0:T(8,128)}, f32[288,128]{1,0:T(8,128)S(1)}, u32[]{:S(2)}, u32[]{:S(2)}) collective-permute-start(f32[288,128]{1,0:T(8,128)} %get-tuple-element.20), channel_id=1, source_target_pairs={{0,1},{1,2},{2,3},{3,4},{4,5},{5,6},{6,7},{7,0},{8,9},{9,10},{10,1... | collective-permute-start | bytes 442376 | tf_op jit(solution)/shard_map/ppermute | solution.py:579
  47.5 6.0 %collective-permute-start.5 = (f32[288,128]{1,0:T(8,128)}, f32[288,128]{1,0:T(8,128)S(1)}, u32[]{:S(2)}, u32[]{:S(2)}) collective-permute-start(f32[288,128]{1,0:T(8,128)} %get-tuple-element.21), channel_id=1, source_target_pairs={{0,7},{1,0},{2,1},{3,2},{4,3},{5,4},{6,5},{7,6},{8,15},{9,8},{10,9... | collective-permute-start | bytes 442376 | tf_op jit(solution)/shard_map/ppermute | solution.py:579
  55.1 24.0 %collective-permute-start.7 = (f32[96,128]{1,0:T(8,128)S(1)}, f32[96,128]{1,0:T(8,128)S(1)}, u32[]{:S(2)}, u32[]{:S(2)}) collective-permute-start(f32[96,128]{1,0:T(8,128)S(1)} %get-tuple-element.22), channel_id=1, source_target_pairs={{0,120},{8,0},{16,8},{24,16},{32,24},{40,32},{48,40},{56,48},{64,5... | collective-permute-start | bytes 147464 | tf_op jit(solution)/shard_map/ppermute | solution.py:579
  60.1 19.0 %collective-permute-start.6 = (f32[96,128]{1,0:T(8,128)S(1)}, f32[96,128]{1,0:T(8,128)S(1)}, u32[]{:S(2)}, u32[]{:S(2)}) collective-permute-start(f32[96,128]{1,0:T(8,128)S(1)} %get-tuple-element.23), channel_id=1, source_target_pairs={{0,8},{8,16},{16,24},{24,32},{32,40},{40,48},{48,56},{56,64},{64,7... | collective-permute-start | bytes 147464 | tf_op jit(solution)/shard_map/ppermute | solution.py:579
  79.1 0.6 copy-start.4
  79.1 0.6 copy-start.5
where the time goes:
time: 82.1 us; the launch traced here: 81.4 us
  Pallas kernels  54.1 us (66%)
  starting transfers between devices  15.6 us (19%)
  local copies, waits for them, and re-layouts  5.37 us (7%)
  waiting for transfers between devices  4.04 us (5%)
  other arithmetic  1.53 us (2%)
    pallas_call x1, Pallas kernels, floes(): pl.pallas_call(functools.partial(floe_kernel, sizes), out_shape=(jax.Shap...  16.9 us
    ppermute x8, starting transfers between devices, shifted(): lax.ppermute(value, axis, [(i, (i + step) % count) for i in range(count)])  15.6 us
    pallas_call x1, Pallas kernels, collide(): pl.pallas_call(collide_kernel, out_shape=jax.ShapeDtypeStruct(populations...  11.1 us
    pallas_call x1, Pallas kernels, spread_out(): pl.pallas_call(spread_kernel, out_shape=jax.ShapeDtypeStruct((COLUMNS, NZ...  7.79 us
    pallas_call x1, Pallas kernels, gather(): pl.pallas_call(gather_kernel, out_shape=jax.ShapeDtypeStruct(cell.shape,...  7.51 us
    pallas_call x1, Pallas kernels, pick(): pl.pallas_call(pick_kernel, out_shape=(jax.ShapeDtypeStruct((COLUMNS, NZ)...  6.61 us
    ppermute x8, waiting for transfers between devices, shifted(): lax.ppermute(value, axis, [(i, (i + step) % count) for i in range(count)])  4.04 us
    pallas_call x1, Pallas kernels, prepare(): pl.pallas_call(prepare_kernel, out_shape=(shape, shape), in_specs=[whole(...  2.43 us
  transfers between devices with their start and end apart: 8, of which 2 were waited for; matrix products, arithmetic and copies ran while one was open for 3% of the time, Pallas kernels for 41%

commit v1 on v0

--- a/solution.py
+++ b/solution.py
@@ -42,6 +42,8 @@
 STATE_ROWS = 6 * GROUPS
 FACE = 5 * WX
 EDGE_ROWS = 8
+WINDOW = 160
+PADDED_COLUMNS = COLUMNS + WINDOW
 CHUNK = 1024
 
 X_UP = [i for i in range(19) if DIRECTIONS[i][0] == 1]
@@ -81,13 +83,25 @@
     return px, py, pz
 
 
-def prepare_kernel(place, velocity, pop, up, down, sem):
+def prepare_kernel(
+    place, velocity, pop, up, down, face_up, face_down, ends_up, ends_down, sem, face_sem
+):
+    faces = []
+    for k in range(5):
+        faces.append(
+            pltpu.make_async_copy(
+                pop.at[Y_UP[k], :, pl.ds(WY - 8, 8), :], ends_up.at[k], face_sem.at[0]
+            )
+        )
+        faces.append(
+            pltpu.make_async_copy(pop.at[Y_DOWN[k], :, pl.ds(0, 8), :], ends_down.at[k], face_sem.at[0])
+        )
     copies = []
     for k in range(5):
         rows = pl.ds(STATE_ROWS + k * WY, WY)
         copies.append(pltpu.make_async_copy(pop.at[X_UP[k], WX - 1], up.at[rows, :], sem.at[0]))
         copies.append(pltpu.make_async_copy(pop.at[X_DOWN[k], 0], down.at[rows, :], sem.at[0]))
-    for copy in copies:
+    for copy in faces + copies:
         copy.start()
     px, py, pz = origin_terms(place, velocity)
     wx, wy, wz = velocity[3:4], velocity[4:5], velocity[5:6]
@@ -105,131 +119,269 @@
             row = values[c][:, b * 128 : (b + 1) * 128]
             up[c * GROUPS + b : c * GROUPS + b + 1, :] = row
             down[c * GROUPS + b : c * GROUPS + b + 1, :] = row
+    for copy in faces:
+        copy.wait()
+    for k in range(5):
+        face_up[k * WX : (k + 1) * WX, :] = ends_up[k, :, 7, :]
+        face_down[k * WX : (k + 1) * WX, :] = ends_down[k, :, 0, :]
     for copy in copies:
         copy.wait()
 
 
 def prepare(place, velocity, populations):
     shape = jax.ShapeDtypeStruct((STATE_ROWS + FACE, 128), jnp.float32)
+    face = jax.ShapeDtypeStruct((FACE, 128), jnp.float32)
     return pl.pallas_call(
         prepare_kernel,
-        out_shape=(shape, shape),
+        out_shape=(shape, shape, face, face),
         in_specs=[whole(), whole(), anywhere()],
-        out_specs=(whole(), whole()),
-        scratch_shapes=[pltpu.SemaphoreType.DMA((1,))],
-        compiler_params=params(),
-        cost_estimate=cost(100_000, 600_000),
-        name="prepare",
-    )(place, velocity, populations)
-
-
-def column_hot(cell):
-    low = jnp.bitwise_and(jnp.right_shift(cell, 7), 511)
-    rows = lax.broadcasted_iota(jnp.int32, (512, cell.shape[1]), 0)
-    return jnp.where(rows == low, 1.0, 0.0).astype(jnp.bfloat16)
-
-
-def depth_mask(cell):
-    depth = jnp.bitwise_or(
-        jnp.left_shift(jnp.right_shift(cell, 16), 7), jnp.bitwise_and(cell, 127)
-    )
-    rows = lax.broadcasted_iota(jnp.int32, (256, cell.shape[1]), 0)
-    return rows == depth
-
-
-NT = (((1,), (1,)), ((), ()))
-NN = (((1,), (0,)), ((), ()))
-
-
-def product(a, b, dims):
-    return lax.dot_general(a, b, dims, preferred_element_type=jnp.float32)
-
-
-def pick_kernel(cell, heading, floe, pop_hbm, dense, picked, up, down, pop, chosen, sem):
-    load = pltpu.make_async_copy(pop_hbm, pop, sem.at[0])
-    load.start()
-    chosen[...] = jnp.zeros_like(chosen)
-
-    def scatter(step, carry):
-        at = pl.ds(pl.multiple_of(step * CHUNK, CHUNK), CHUNK)
-        own = cell[:, at]
-        value = jnp.where(floe[:, at] >= 0, heading[:, at], 0).astype(jnp.float32)
-        hot = column_hot(own)
-        payload = jnp.where(depth_mask(own), value, 0.0).astype(jnp.bfloat16)
-        chosen[...] += product(hot, payload, NT)
-        return carry
-
-    lax.fori_loop(0, cell.shape[1] // CHUNK, scatter, 0)
-    dense[0:512] = chosen[:, 0:128]
-    dense[512:1024] = chosen[:, 128:256]
-    load.wait()
-
-    def select(step, carry):
-        rows = pl.ds(pl.multiple_of(step * 32, 32), 32)
-        for half in range(2):
-            where = chosen[rows, half * 128 : (half + 1) * 128]
-            source = pl.ds(pl.multiple_of(step * 32, 32) + half * 512, 32)
-            value = jnp.zeros((32, 128), jnp.float32)
-            for i in range(1, 19):
-                value = jnp.where(where == float(i), pop[i, source, :], value)
-            chosen[rows, half * 128 : (half + 1) * 128] = value
-        return carry
-
-    lax.fori_loop(0, 16, select, 0)
-    turned = jnp.transpose(chosen[...])
-    high = turned.astype(jnp.bfloat16)
-    picked[0:256] = high
-    picked[256:512] = (turned - high.astype(jnp.float32)).astype(jnp.bfloat16)
-    for k in range(5):
-        up[k * WX : (k + 1) * WX, :] = pop[Y_UP[k], pl.ds(WY - 1, WX, stride=WY), :]
-        down[k * WX : (k + 1) * WX, :] = pop[Y_DOWN[k], pl.ds(0, WX, stride=WY), :]
-
-
-def pick(cell, heading, floe, columns):
-    face = jax.ShapeDtypeStruct((FACE, 128), jnp.float32)
-    return pl.pallas_call(
-        pick_kernel,
-        out_shape=(
-            jax.ShapeDtypeStruct((COLUMNS, NZ), jnp.float32),
-            jax.ShapeDtypeStruct((512, 512), jnp.bfloat16),
-            face,
-            face,
-        ),
-        in_specs=[whole(), whole(), whole(), anywhere()],
         out_specs=(whole(),) * 4,
         scratch_shapes=[
-            pltpu.VMEM(columns.shape, jnp.float32),
-            pltpu.VMEM((512, 256), jnp.float32),
+            pltpu.VMEM((5, WX, 8, NZ), jnp.float32),
+            pltpu.VMEM((5, WX, 8, NZ), jnp.float32),
+            pltpu.SemaphoreType.DMA((1,)),
             pltpu.SemaphoreType.DMA((1,)),
         ],
         compiler_params=params(),
-        cost_estimate=cost(2_200_000_000, 12_000_000),
+        cost_estimate=cost(100_000, 2_600_000),
+        name="prepare",
+    )(place, velocity, populations)
+
+
+NT = (((1,), (1,)), ((), ()))
+NN = (((1,), (0,)), ((), ()))
+
+
+def product(a, b, dims):
+    return lax.dot_general(a, b, dims, preferred_element_type=jnp.float32)
+
+
+def column_hot(cell, start):
+    rows = lax.broadcasted_iota(jnp.int32, (WINDOW, cell.shape[1]), 0)
+    return jnp.where(rows == jnp.right_shift(cell, 7) - start, 1.0, 0.0).astype(jnp.bfloat16)
+
+
+def depth_mask(cell):
+    rows = lax.broadcasted_iota(jnp.int32, (NZ, cell.shape[1]), 0)
+    return rows == jnp.bitwise_and(cell, NZ - 1)
+
+
+def sorted_chunks(keys, values):
+    lane = lax.broadcasted_iota(jnp.int32, (8, 128), 1)
+    sublane = lax.broadcasted_iota(jnp.int32, (8, 128), 0)
+
+    def bit(position):
+        if position < 6:
+            return jnp.bitwise_and(jnp.right_shift(sublane, position - 3), 1)
+        return jnp.bitwise_and(jnp.right_shift(lane, position - 6), 1)
+
+    def partner(x, position):
+        axis = 0 if position < 6 else 1
+        extent = x.shape[axis]
+        distance = 1 << (position - (3 if position < 6 else 6))
+        if 2 * distance == extent:
+            return pltpu.roll(x, distance, axis)
+        return jnp.where(
+            bit(position) == 0,
+            pltpu.roll(x, extent - distance, axis),
+            pltpu.roll(x, distance, axis),
+        )
+
+    for merge in range(1, 14):
+        for position in range(merge - 1, -1, -1):
+            if merge == 13 and position < 10:
+                continue
+            if position < 3:
+                for v in range(8):
+                    u = v | (1 << position)
+                    if u == v:
+                        continue
+                    below = keys[u] < keys[v]
+                    if merge < 3:
+                        if (v >> merge) & 1:
+                            below = keys[u] > keys[v]
+                    elif merge < 13:
+                        below = jnp.logical_xor(below, bit(merge) == 1)
+                    keys[v], keys[u] = (
+                        jnp.where(below, keys[u], keys[v]),
+                        jnp.where(below, keys[v], keys[u]),
+                    )
+                    values[v], values[u] = (
+                        jnp.where(below, values[u], values[v]),
+                        jnp.where(below, values[v], values[u]),
+                    )
+                continue
+            if merge < 13:
+                least = bit(position) == bit(merge)
+            else:
+                least = bit(position) == 0
+            for v in range(8):
+                other = partner(keys[v], position)
+                carried = partner(values[v], position)
+                stay = jnp.logical_xor(other < keys[v], least)
+                keys[v] = jnp.where(stay, keys[v], other)
+                values[v] = jnp.where(stay, values[v], carried)
+    return keys, values
+
+
+def pick_kernel(sizes, place, cell, heading, floe, cells, words, work, dense, turned):
+    size_along, size_across = sizes
+    a = place[0]
+    b = place[1]
+    keys = []
+    values = []
+    for v in range(8):
+        rows = slice(v * 8, (v + 1) * 8)
+        g = floe[rows, :]
+        owner = jnp.right_shift(g, 11)
+        ra = jnp.bitwise_and(owner // size_across - a + 1, size_along - 1)
+        rb = jnp.bitwise_and(jnp.bitwise_and(owner, size_across - 1) - b + 1, size_across - 1)
+        entry = (ra * 3 + rb) * MEMBERS + jnp.bitwise_and(g, MEMBERS - 1)
+        word = jnp.left_shift(heading[rows, :], 15) + entry
+        keys.append(cell[rows, :])
+        values.append(jnp.where(g >= 0, word, 9 * MEMBERS))
+    keys, values = sorted_chunks(keys, values)
+    turned[...] = jnp.transpose(jnp.concatenate(keys + values, axis=0))
+    even = turned[pl.ds(0, 64, stride=2), :]
+    odd = turned[pl.ds(1, 64, stride=2), :]
+    left = lax.broadcasted_iota(jnp.int32, (64, 128), 1) < 64
+    key = jnp.where(left, even, pltpu.roll(odd, 64, 1))
+    value = jnp.where(left, pltpu.roll(even, 64, 1), odd)
+    for r in range(64):
+        cells[:, r * 128 : (r + 1) * 128] = key[r : r + 1, :]
+        words[:, r * 128 : (r + 1) * 128] = value[r : r + 1, :]
+    column = jnp.right_shift(key, 7)
+    count = jnp.int32(8)
+    for c in range(8):
+        part = column[c * 8 : (c + 1) * 8, :]
+        first = jnp.left_shift(jnp.right_shift(jnp.min(part), 3), 3)
+        last = jnp.max(part)
+        windows = (last - first) // WINDOW + 1
+        work[0, c] = c
+        work[1, c] = first
+
+        def enter(w, n, c=c, first=first):
+            work[0, n] = c
+            work[1, n] = first + w * WINDOW
+            return n + 1
+
+        count = lax.fori_loop(1, windows, enter, count)
+    work[2, 0] = count
+    dense[...] = jnp.zeros_like(dense)
+
+    def scatter(at, start):
+        own = cells[:, at]
+        kind = jnp.right_shift(words[:, at], 15).astype(jnp.float32)
+        payload = jnp.where(depth_mask(own), kind, 0.0).astype(jnp.bfloat16)
+        return product(column_hot(own, start), payload, NT)
+
+    over_windows(work, scatter, window_adder(dense))
+
+
+def window_adder(dense):
+    def add(at, start, value):
+        dense[pl.ds(start, WINDOW), :] += value
+
+    return add
+
+
+def over_windows(work, compute, apply):
+    for group in range(0, 8, 4):
+        results = []
+        for c in range(group, group + 4):
+            at = slice(c * 1024, (c + 1) * 1024)
+            start = pl.multiple_of(work[1, c], 8)
+            results.append((at, start, compute(at, start)))
+        for result in results:
+            apply(*result)
+
+    def step(n, carry):
+        at = pl.ds(pl.multiple_of(work[0, n] * 1024, 1024), 1024)
+        start = pl.multiple_of(work[1, n], 8)
+        apply(at, start, compute(at, start))
+        return carry
+
+    lax.fori_loop(8, work[2, 0], step, 0)
+
+
+def smem():
+    return pl.BlockSpec(memory_space=pltpu.SMEM)
+
+
+def pick(sizes, place, cell, heading, floe):
+    links = cell.shape[0] * cell.shape[1]
+    row = jax.ShapeDtypeStruct((1, links), jnp.int32)
+    return pl.pallas_call(
+        functools.partial(pick_kernel, sizes),
+        out_shape=(
+            row,
+            row,
+            jax.ShapeDtypeStruct((3, 32), jnp.int32),
+            jax.ShapeDtypeStruct((PADDED_COLUMNS, NZ), jnp.float32),
+        ),
+        in_specs=[smem(), whole(), whole(), whole()],
+        out_specs=(whole(), whole(), smem(), whole()),
+        scratch_shapes=[pltpu.VMEM((128, 128), jnp.int32)],
+        compiler_params=params(),
+        cost_estimate=cost(7_000_000_000, 1_000_000),
         name="pick",
-    )(cell, heading, floe, columns)
-
-
-def gather_kernel(cell, picked, out):
-    def step(t, carry):
-        at = pl.ds(pl.multiple_of(t * CHUNK, CHUNK), CHUNK)
+    )(place, cell, heading, floe)
+
+
+def gather_kernel(work, cell, dense, pop_hbm, out, pop, chosen, sem):
+    def loading(s):
+        return pltpu.make_async_copy(
+            pop_hbm.at[:, pl.ds(s * 128, 128)], pop.at[:, pl.ds(s * 128, 128)], sem.at[s]
+        )
+
+    for s in range(8):
+        loading(s).start()
+    chosen[COLUMNS:] = jnp.zeros((PADDED_COLUMNS - COLUMNS, NZ), jnp.float32)
+    out[...] = jnp.zeros_like(out)
+
+    def select(s, carry):
+        loading(s).wait()
+        for part in range(4):
+            rows = pl.ds(pl.multiple_of(s * 128, 128) + part * 32, 32)
+            where = dense[rows, :]
+            value = jnp.zeros((32, 128), jnp.float32)
+            for i in range(1, 19):
+                value = jnp.where(where == float(i), pop[i, rows, :], value)
+            chosen[rows, :] = value
+        return carry
+
+    lax.fori_loop(0, 8, select, 0)
+
+    def read(at, start):
         own = cell[:, at]
-        values = product(picked[...], column_hot(own), NN)
-        values = values[0:256] + values[256:512]
-        out[:, at] = jnp.sum(jnp.where(depth_mask(own), values, 0.0), axis=0, keepdims=True)
-        return carry
-
-    lax.fori_loop(0, cell.shape[1] // CHUNK, step, 0)
-
-
-def gather(cell, picked):
+        turned = jnp.transpose(chosen[pl.ds(start, WINDOW), :])
+        high = turned.astype(jnp.bfloat16)
+        low = (turned - high.astype(jnp.float32)).astype(jnp.bfloat16)
+        values = product(jnp.concatenate([high, low], axis=0), column_hot(own, start), NN)
+        values = values[0:NZ] + values[NZ : 2 * NZ]
+        return jnp.sum(jnp.where(depth_mask(own), values, 0.0), axis=0, keepdims=True)
+
+    def add(at, start, value):
+        out[:, at] += value
+
+    over_windows(work, read, add)
+
+
+def gather(work, cell, dense, columns):
     return pl.pallas_call(
         gather_kernel,
         out_shape=jax.ShapeDtypeStruct(cell.shape, jnp.float32),
-        in_specs=[whole(), whole()],
+        in_specs=[smem(), whole(), whole(), anywhere()],
         out_specs=whole(),
+        scratch_shapes=[
+            pltpu.VMEM(columns.shape, jnp.float32),
+            pltpu.VMEM((PADDED_COLUMNS, NZ), jnp.float32),
+            pltpu.SemaphoreType.DMA((8,)),
+        ],
         compiler_params=params(),
-        cost_estimate=cost(4_300_000_000, 1_000_000),
+        cost_estimate=cost(6_000_000_000, 12_000_000),
         name="gather",
-    )(cell, picked)
+    )(work, cell, dense, columns)
 
 
 def bits(table, heading):
@@ -246,12 +398,9 @@
 
 
 def floe_kernel(
-    sizes, place, cell, heading, floe, here, mine, low, high, left, right,
-    taken, loads_left, loads_mid, loads_right, table, spread, payload, total,
+    cell, words, here, mine, low, high, left, right,
+    taken, loads_left, loads_mid, loads_right, table, hot, spread, payload, total,
 ):
-    size_along, size_across = sizes
-    a = place[0]
-    b = place[1]
     links = cell.shape[1]
     for ra in range(3):
         for rb in range(3):
@@ -268,21 +417,20 @@
             table[STATE_ROWS : 2 * STATE_ROWS, lanes] = (
                 state - first.astype(jnp.float32)
             ).astype(jnp.bfloat16)
-    total[...] = jnp.zeros_like(total)
     payload[...] = jnp.zeros_like(payload)
 
-    def step(t, carry):
-        at = pl.ds(pl.multiple_of(t * CHUNK, CHUNK), CHUNK)
+    def first_half(t):
+        slot = t % 2
+        at = slice(t * CHUNK, (t + 1) * CHUNK)
         k = cell[:, at]
-        d = heading[:, at]
-        g = floe[:, at]
-        active = g >= 0
-        owner = jnp.right_shift(g, 11)
-        ra = jnp.bitwise_and(owner // size_across - a + 1, size_along - 1)
-        rb = jnp.bitwise_and(jnp.bitwise_and(owner, size_across - 1) - b + 1, size_across - 1)
-        member = jnp.bitwise_and(g, MEMBERS - 1)
-        group = jnp.where(active, jnp.right_shift(member, 7), -1)
-        entry = (ra * 3 + rb) * 128 + jnp.bitwise_and(member, 127)
+        word = words[:, at]
+        d = jnp.right_shift(word, 15)
+        place = jnp.bitwise_and(word, 32767)
+        region = jnp.right_shift(place, 11)
+        ra = jnp.right_shift(region * 11, 5)
+        rb = region - 3 * ra
+        group = jnp.bitwise_and(jnp.right_shift(place, 7), GROUPS - 1)
+        entry = region * 128 + jnp.bitwise_and(place, 127)
         rows = lax.broadcasted_iota(jnp.int32, (9 * 128, CHUNK), 0)
         pick_floe = jnp.where(rows == entry, 1.0, 0.0).astype(jnp.bfloat16)
         groups = lax.broadcasted_iota(jnp.int32, (GROUPS, CHUNK), 0)
@@ -308,25 +456,36 @@
             (rx * cy - ry * cx) * scale,
         ]
         for c in range(6):
-            spread[c * GROUPS : (c + 1) * GROUPS, :] = mask * coefficients[c]
+            spread[slot, c * GROUPS : (c + 1) * GROUPS, :] = mask * coefficients[c]
+        hot[slot] = pick_floe
 
         state = product(table[...], pick_floe, NN)
         state = state[0:STATE_ROWS] + state[STATE_ROWS : 2 * STATE_ROWS]
-        weights = spread[...]
+        weights = spread[slot]
         speed = jnp.sum(state * weights, axis=0, keepdims=True)
         take = (6.0 * FLOW_SCALE) * weight * speed
         magnitude = 2.0 * here[:, at] - take
         taken[:, at] = take
         amount = weights * magnitude
         first = amount.astype(jnp.bfloat16)
-        payload[0:STATE_ROWS, :] = first
-        payload[128 : 128 + STATE_ROWS, :] = (amount - first.astype(jnp.float32)).astype(
+        payload[slot, 0:STATE_ROWS, :] = first
+        payload[slot, 128 : 128 + STATE_ROWS, :] = (amount - first.astype(jnp.float32)).astype(
             jnp.bfloat16
         )
-        total[...] += product(pick_floe, payload[...], NT)
-        return carry
-
-    lax.fori_loop(0, links // CHUNK, step, 0)
+
+    def second_half(t):
+        value = product(hot[t % 2], payload[t % 2], NT)
+        if t == 0:
+            total[...] = value
+        else:
+            total[...] += value
+
+    steps = links // CHUNK
+    first_half(0)
+    for t in range(1, steps):
+        first_half(t)
+        second_half(t - 1)
+    second_half(steps - 1)
     for ra in range(3):
         for rb in range(3):
             rows = slice((ra * 3 + rb) * 128, (ra * 3 + rb + 1) * 128)
@@ -335,30 +494,30 @@
             out[ra * STATE_ROWS : (ra + 1) * STATE_ROWS] = jnp.transpose(summed)[0:STATE_ROWS]
 
 
-def floes(sizes, place, cell, heading, floe, here, mine, low, high, left, right):
+def floes(cell, words, here, mine, low, high, left, right):
     loads = jax.ShapeDtypeStruct((3 * STATE_ROWS, 128), jnp.float32)
     return pl.pallas_call(
-        functools.partial(floe_kernel, sizes),
+        floe_kernel,
         out_shape=(jax.ShapeDtypeStruct(cell.shape, jnp.float32), loads, loads, loads),
-        in_specs=[pl.BlockSpec(memory_space=pltpu.SMEM)] + [whole()] * 9,
+        in_specs=[whole()] * 8,
         out_specs=(whole(),) * 4,
         scratch_shapes=[
             pltpu.VMEM((2 * STATE_ROWS, 9 * 128), jnp.bfloat16),
-            pltpu.VMEM((STATE_ROWS, CHUNK), jnp.float32),
-            pltpu.VMEM((256, CHUNK), jnp.bfloat16),
+            pltpu.VMEM((2, 9 * 128, CHUNK), jnp.bfloat16),
+            pltpu.VMEM((2, STATE_ROWS, CHUNK), jnp.float32),
+            pltpu.VMEM((2, 256, CHUNK), jnp.bfloat16),
             pltpu.VMEM((9 * 128, 256), jnp.float32),
         ],
         compiler_params=params(),
         cost_estimate=cost(8_000_000_000, 2_000_000),
         name="floes",
-    )(place, cell, heading, floe, here, mine, low, high, left, right)
-
-
-def spread_kernel(cell, taken, dense, total):
-    total[...] = jnp.zeros_like(total)
-
-    def step(t, carry):
-        at = pl.ds(pl.multiple_of(t * CHUNK, CHUNK), CHUNK)
+    )(cell, words, here, mine, low, high, left, right)
+
+
+def spread_kernel(work, cell, taken, dense):
+    dense[...] = jnp.zeros_like(dense)
+
+    def scatter(at, start):
         own = cell[:, at]
         value = taken[:, at]
         first = value.astype(jnp.bfloat16).astype(jnp.float32)
@@ -370,25 +529,22 @@
             ],
             axis=0,
         )
-        total[...] += product(column_hot(own), payload, NT)
-        return carry
-
-    lax.fori_loop(0, cell.shape[1] // CHUNK, step, 0)
-    dense[0:512] = total[:, 0:128] + total[:, 256:384]
-    dense[512:1024] = total[:, 128:256] + total[:, 384:512]
-
-
-def spread_out(cell, taken):
+        both = product(column_hot(own, start), payload, NT)
+        return both[:, :NZ] + both[:, NZ:]
+
+    over_windows(work, scatter, window_adder(dense))
+
+
+def spread_out(work, cell, taken):
     return pl.pallas_call(
         spread_kernel,
-        out_shape=jax.ShapeDtypeStruct((COLUMNS, NZ), jnp.float32),
-        in_specs=[whole(), whole()],
+        out_shape=jax.ShapeDtypeStruct((PADDED_COLUMNS, NZ), jnp.float32),
+        in_specs=[smem(), whole(), whole()],
         out_specs=whole(),
-        scratch_shapes=[pltpu.VMEM((512, 512), jnp.float32)],
         compiler_params=params(),
-        cost_estimate=cost(4_300_000_000, 1_000_000),
+        cost_estimate=cost(3_000_000_000, 1_000_000),
         name="spread",
-    )(cell, taken)
+    )(work, cell, taken)
 
 
 SLAB = 4
@@ -583,15 +739,15 @@
     sizes = (lax.axis_size("along"), lax.axis_size("across"))
     where = jnp.stack([lax.axis_index("along"), lax.axis_index("across")]).astype(jnp.int32)
     links = link_cell.shape[-1]
-    cell = link_cell.reshape(1, links)
-    heading = link_dir.reshape(1, links)
-    floe = link_floe.reshape(1, links)
+    cell = link_cell.reshape(links // 128, 128)
+    heading = link_dir.reshape(links // 128, 128)
+    floe = link_floe.reshape(links // 128, 128)
     columns = populations.reshape(19, COLUMNS, NZ)
 
-    up, down = prepare(floe_place, floe_velocity, populations)
+    up, down, face_up, face_down = prepare(floe_place, floe_velocity, populations)
     low = shifted(up, "along", 1)
     high = shifted(down, "along", -1)
-    dense_dir, picked, face_up, face_down = pick(cell, heading, floe, columns)
+    cells, words, work, dense_dir = pick(sizes, where, cell, heading, floe)
 
     def rows(block, k, y):
         at = STATE_ROWS + k * WY + y
@@ -608,13 +764,13 @@
     )
     left = shifted(to_up, "across", 1)
     right = shifted(to_down, "across", -1)
-    here = gather(cell, picked)
+    here = gather(work, cells, dense_dir, columns)
     taken, loads_left, loads_mid, loads_right = floes(
-        sizes, where, cell, heading, floe, here, up, low, high, left, right
+        cells, words, here, up, low, high, left, right
     )
     from_right = shifted(loads_left, "across", -1)
     from_left = shifted(loads_right, "across", 1)
-    dense_take = spread_out(cell, taken)
+    dense_take = spread_out(work, cells, taken)
     three = loads_mid + from_left + from_right
     from_high = shifted(three[:STATE_ROWS], "along", -1)
     from_low = shifted(three[2 * STATE_ROWS :], "along", 1)

time: 82.1 us -> 74.7 us (0.910)
  Pallas kernels: 54.1 us -> 48.6 us
  local copies, waits for them, and re-layouts: 5.37 us -> 2.92 us
  starting transfers between devices: 15.6 us -> 16.5 us
  waiting for transfers between devices: 4.04 us -> 3.21 us
    pallas_call x4, Pallas kernels: 33.8 us -> 28.1 us  [the longest x1 14.7 us: floes(): pl.pallas_call(floe_kernel, out_shape=(jax.ShapeDtypeStruct(cell.shape, j...]
    concatenate x1, local copies, waits for them, and re-layouts: 0.96 us -> 0.04 us  [body(): jnp.concatenate(states + [face_down, rows(low, X_UP.index(9), 0), rows(hi...]
    concatenate x1, local copies, waits for them, and re-layouts: 0.92 us -> 0.04 us  [body(): jnp.concatenate(states + [face_up, rows(low, X_UP.index(7), WY - 1), rows...]
    ppermute x8, starting transfers between devices: 15.6 us -> 16.5 us  [shifted(): lax.ppermute(value, axis, [(i, (i + step) % count) for i in range(count)])]
    ppermute x8, waiting for transfers between devices: 4.04 us -> 3.21 us  [shifted(): lax.ppermute(value, axis, [(i, (i + step) % count) for i in range(count)])]
    unnamed x12 -> x16, local copies, waits for them, and re-layouts: 1.99 us -> 1.39 us
  transfers between devices with their start and end apart: 8 -> 8, of which waited for: 2 -> 2; matrix products, arithmetic and copies ran while one was open for 3% -> 2% of each run, Pallas kernels for 41% -> 39%
where the time goes in v1:
time: 74.7 us; the launch traced here: 73.6 us
  Pallas kernels  48.6 us (65%)
  starting transfers between devices  16.5 us (22%)
  waiting for transfers between devices  3.21 us (4%)
  local copies, waits for them, and re-layouts  2.92 us (4%)
  other arithmetic  1.59 us (2%)
  between operations  0.81 us (1%)
    ppermute x8, starting transfers between devices, shifted(): lax.ppermute(value, axis, [(i, (i + step) % count) for i in range(count)])  16.5 us
    pallas_call x1, Pallas kernels, floes(): pl.pallas_call(floe_kernel, out_shape=(jax.ShapeDtypeStruct(cell.shape, j...  14.7 us
    pallas_call x1, Pallas kernels, collide(): pl.pallas_call(collide_kernel, out_shape=jax.ShapeDtypeStruct(populations...  11.2 us
    pallas_call x1, Pallas kernels, gather(): pl.pallas_call(gather_kernel, out_shape=jax.ShapeDtypeStruct(cell.shape,...  7.65 us
    pallas_call x1, Pallas kernels, pick(): pl.pallas_call(functools.partial(pick_kernel, sizes), out_shape=(row, row...  6.83 us
    pallas_call x1, Pallas kernels, spread_out(): pl.pallas_call(spread_kernel, out_shape=jax.ShapeDtypeStruct((PADDED_COLU...  3.36 us
    ppermute x8, waiting for transfers between devices, shifted(): lax.ppermute(value, axis, [(i, (i + step) % count) for i in range(count)])  3.21 us
    pallas_call x1, Pallas kernels, prepare(): pl.pallas_call(prepare_kernel, out_shape=(shape, shape, face, face), in_s...  3.2 us
  transfers between devices with their start and end apart: 8, of which 2 were waited for; matrix products, arithmetic and copies ran while one was open for 2% of the time, Pallas kernels for 39%

profile of v1, /device:TPU:0, one launch (start us, length us, event | category | flops | bytes accessed | tf_op | source)
XLA Modules:
  0.0 73.6 jit_solution(15594509684049360526)
XLA Ops:
  0.6 3.2 %prepare.1 = (f32[256,128]{1,0:T(8,128)}, f32[256,128]{1,0:T(8,128)}, f32[160,128]{1,0:T(8,128)}, f32[160,128]{1,0:T(8,128)}) custom-call(f32[3,2048]{1,0:T(4,128)} %place.3, f32[6,2048]{1,0:T(8,128)} %velocity.3, f32[19,32,32,128]{3,2,1,0:T(8,128)} %pop_hbm.1), custom_call_target="tpu_custom_call" | custom-call | flops 100000 | bytes 2600000 | tf_op jit(solution)/shard_map/prepare/pallas_call | solution.py:134
  3.8 5.4 %collective-permute-start.1 = (f32[256,128]{1,0:T(8,128)}, f32[256,128]{1,0:T(8,128)S(1)}, u32[]{:S(2)}, u32[]{:S(2)}) collective-permute-start(f32[256,128]{1,0:T(8,128)} %get-tuple-element.19), channel_id=1, source_target_pairs={{0,120},{8,0},{16,8},{24,16},{32,24},{40,32},{48,40},{56,48},{64,5... | collective-permute-start | bytes 393224 | tf_op jit(solution)/shard_map/ppermute | solution.py:735
  9.2 0.0 collective-permute-start
  9.2 0.7 pad_add_fusion.place
  9.9 0.0 copy-start.5
  9.9 0.0 copy-start.4
  9.9 6.8 %pick.1 = (s32[1,8192]{1,0:T(1,128)}, s32[1,8192]{1,0:T(1,128)}, s32[3,32]{1,0:T(4,128)}, f32[1184,128]{1,0:T(8,128)}) custom-call(s32[2]{0:T(128)} %pad_add_fusion.place, s32[64,128]{1,0:T(8,128)} %bitcast.7, s32[64,128]{1,0:T(8,128)} %bitcast.8, s32[64,128]{1,0:T(8,128)} %bitcast.9), custom_call_target="tpu_custom_call" | custom-call | flops 7000000000 | bytes 1000000 | tf_op jit(solution)/shard_map/pick/pallas_call | solution.py:314
  16.7 0.8 %slice.31 = f32[96,128]{1,0:T(8,128)S(1)} slice(f32[256,128]{1,0:T(8,128)} %get-tuple-element.18.mine), slice={[0:96], [0:128]} | slice | bytes 98304 | tf_op jit(solution)/shard_map/slice | solution.py:756
  17.5 0.0 collective-permute-done.1.high
  17.5 0.0 copy-start
  17.5 0.2 collective-permute-done.low
  17.7 0.0 copy-start.1
  17.7 0.0 copy-done.5
  17.8 0.0 collective-permute-start.2
  17.8 0.0 copy-done.4
  17.8 3.1 %collective-permute-start.3 = (f32[456,128]{1,0:T(8,128)S(1)}, f32[456,128]{1,0:T(8,128)S(1)}, u32[]{:S(2)}, u32[]{:S(2)}) collective-permute-start(f32[456,128]{1,0:T(8,128)S(1)} %concatenate.7), channel_id=1, source_target_pairs={{0,7},{1,0},{2,1},{3,2},{4,3},{5,4},{6,5},{7,6},{8,15},{9,8},{10,9... | collective-permute-start | bytes 700424 | tf_op jit(solution)/shard_map/ppermute | solution.py:735
  20.9 7.7 %gather.1.here = f32[1,8192]{1,0:T(1,128)} custom-call(s32[3,32]{1,0:T(4,128)} %get-tuple-element.15.work, s32[1,8192]{1,0:T(1,128)} %get-tuple-element.16.cell, f32[1184,128]{1,0:T(8,128)} %get-tuple-element.14.dense.dense_dir, f32[19,1024,128]{2,1,0:T(8,128)} %bitcast.6), custom_call_target="tpu_custom_call" | custom-call | flops 6000000000 | bytes 12000000 | tf_op jit(solution)/shard_map/gather/pallas_call | solution.py:371
  28.6 0.0 copy-done
  28.6 0.0 copy-done.1
  28.6 0.0 collective-permute-done.2.left
  28.6 0.0 copy-start.2
  28.6 0.0 collective-permute-done.3.right
  28.6 0.0 copy-start.3
  28.6 0.7 copy-done.2
  29.3 0.1 copy-done.3
  29.4 14.7 %floes.1 = (f32[1,8192]{1,0:T(1,128)}, f32[288,128]{1,0:T(8,128)}, f32[288,128]{1,0:T(8,128)}, f32[288,128]{1,0:T(8,128)}) custom-call(s32[1,8192]{1,0:T(1,128)} %get-tuple-element.16.cell, s32[1,8192]{1,0:T(1,128)} %get-tuple-element.17.words, f32[1,8192]{1,0:T(1,128)} %gather.1.here, f32[256,128]{1,0:T(8,128)} %get-tuple-element.18.mine, ...), custom_call_target="tpu_custom_call" | custom-call | flops 8000000000 | bytes 2000000 | tf_op jit(solution)/shard_map/floes/pallas_call | solution.py:499
  44.1 0.0 collective-permute-start.4
  44.1 3.0 %collective-permute-start.5 = (f32[288,128]{1,0:T(8,128)}, f32[288,128]{1,0:T(8,128)S(1)}, u32[]{:S(2)}, u32[]{:S(2)}) collective-permute-start(f32[288,128]{1,0:T(8,128)} %get-tuple-element.25), channel_id=1, source_target_pairs={{0,7},{1,0},{2,1},{3,2},{4,3},{5,4},{6,5},{7,6},{8,15},{9,8},{10,9... | collective-permute-start | bytes 442376 | tf_op jit(solution)/shard_map/ppermute | solution.py:735
  47.1 3.0 %collective-permute-done.4 = f32[288,128]{1,0:T(8,128)S(1)} collective-permute-done((f32[288,128]{1,0:T(8,128)}, f32[288,128]{1,0:T(8,128)S(1)}, u32[]{:S(2)}, u32[]{:S(2)}) %collective-permute-start.4) | collective-permute-done | bytes 147488 | tf_op jit(solution)/shard_map/ppermute | solution.py:735
  50.1 0.0 collective-permute-done.5
  50.1 0.9 %add_add_fusion = f32[288,128]{1,0:T(8,128)S(1)} fusion(f32[288,128]{1,0:T(8,128)S(1)} %collective-permute-done.5, f32[288,128]{1,0:T(8,128)} %get-tuple-element.23, f32[288,128]{1,0:T(8,128)S(1)} %collective-permute-done.4), kind=kLoop, calls=%fused_computation | loop fusion | flops 73728 | bytes 589824 | tf_op jit(solution)/shard_map/add | solution.py:774
  51.0 0.6 fusion
  51.7 5.1 %collective-permute-start.7 = (f32[96,128]{1,0:T(8,128)S(1)}, f32[96,128]{1,0:T(8,128)S(1)}, u32[]{:S(2)}, u32[]{:S(2)}) collective-permute-start(f32[96,128]{1,0:T(8,128)S(1)} %get-tuple-element.26), channel_id=1, source_target_pairs={{0,120},{8,0},{16,8},{24,16},{32,24},{40,32},{48,40},{56,48},{64,5... | collective-permute-start | bytes 147464 | tf_op jit(solution)/shard_map/ppermute | solution.py:735
  56.7 0.0 collective-permute-start.6
  56.7 3.4 %spread.1.dense_take = f32[1184,128]{1,0:T(8,128)} custom-call(s32[3,32]{1,0:T(4,128)} %get-tuple-element.15.work, s32[1,8192]{1,0:T(1,128)} %get-tuple-element.16.cell, f32[1,8192]{1,0:T(1,128)} %get-tuple-element.22.taken), custom_call_target="tpu_custom_call" | custom-call | flops 3000000000 | bytes 1000000 | tf_op jit(solution)/shard_map/spread/pallas_call | solution.py:539
  60.1 11.2 %collide.1 = f32[19,32,32,128]{3,2,1,0:T(8,128)} custom-call(f32[1184,128]{1,0:T(8,128)} %get-tuple-element.14.dense.dense_dir, f32[1184,128]{1,0:T(8,128)} %spread.1.dense_take, f32[256,128]{1,0:T(8,128)} %copy-done.1, f32[256,128]{1,0:T(8,128)} %copy-done, f32[456,128]{1,0:T(8,128)} %copy-done.2, f32[456,128]{1,0:T(8,128)} %copy-done.3, ...), custom_call_target="tpu_custom_call" | custom-call | flops 40000000 | bytes 24000000 | tf_op jit(solution)/shard_map/collide/pallas_call | solution.py:679
  71.3 0.0 collective-permute-done.7.high
  71.3 0.0 copy-start.6
  71.3 0.0 collective-permute-done.6.low
  71.3 0.0 copy-start.7
  71.3 0.6 copy-done.6
  71.9 0.0 copy-done.7
  71.9 1.7 %motion.1 = f32[6,2048]{1,0:T(8,128)} custom-call(f32[96,128]{1,0:T(8,128)} %get-tuple-element.28.own, f32[96,128]{1,0:T(8,128)} %copy-done.7, f32[96,128]{1,0:T(8,128)} %copy-done.6, f32[3,2048]{1,0:T(4,128)} %place.3, f32[6,2048]{1,0:T(8,128)} %velocity.3, f32[2,2048]{1,0:T(2,128)} %response.1), custom_call_target="tpu_custom_call" | custom-call | flops 200000 | bytes 300000 | tf_op jit(solution)/shard_map/motion/pallas_call | solution.py:722
  (7 shorter events, 0.1 us)
Async XLA Ops:
  3.8 13.7 %collective-permute-start.1 = (f32[256,128]{1,0:T(8,128)}, f32[256,128]{1,0:T(8,128)S(1)}, u32[]{:S(2)}, u32[]{:S(2)}) collective-permute-start(f32[256,128]{1,0:T(8,128)} %get-tuple-element.19), channel_id=1, source_target_pairs={{0,120},{8,0},{16,8},{24,16},{32,24},{40,32},{48,40},{56,48},{64,5... | collective-permute-start | bytes 393224 | tf_op jit(solution)/shard_map/ppermute | solution.py:735
  9.2 8.5 %collective-permute-start = (f32[256,128]{1,0:T(8,128)}, f32[256,128]{1,0:T(8,128)S(1)}, u32[]{:S(2)}, u32[]{:S(2)}) collective-permute-start(f32[256,128]{1,0:T(8,128)} %get-tuple-element.18.mine), channel_id=1, source_target_pairs={{0,8},{8,16},{16,24},{24,32},{32,40},{40,48},{48,56},{56,64},{64,7... | collective-permute-start | bytes 393224 | tf_op jit(solution)/shard_map/ppermute | solution.py:735
  9.9 7.9 %copy-start.5 = (f32[160,128]{1,0:T(8,128)S(1)}, f32[160,128]{1,0:T(8,128)}, u32[]{:S(2)}) copy-start(f32[160,128]{1,0:T(8,128)} %get-tuple-element.20) | copy-start | bytes 245764
  9.9 7.9 %copy-start.4 = (f32[160,128]{1,0:T(8,128)S(1)}, f32[160,128]{1,0:T(8,128)}, u32[]{:S(2)}) copy-start(f32[160,128]{1,0:T(8,128)} %get-tuple-element.21) | copy-start | bytes 245764
  17.5 11.1 %copy-start = (f32[256,128]{1,0:T(8,128)}, f32[256,128]{1,0:T(8,128)S(1)}, u32[]{:S(2)}) copy-start(f32[256,128]{1,0:T(8,128)S(1)} %collective-permute-done.1.high) | copy-start | bytes 393220
  17.7 10.9 %copy-start.1 = (f32[256,128]{1,0:T(8,128)}, f32[256,128]{1,0:T(8,128)S(1)}, u32[]{:S(2)}) copy-start(f32[256,128]{1,0:T(8,128)S(1)} %collective-permute-done.low) | copy-start | bytes 393220
  17.8 10.8 %collective-permute-start.2 = (f32[456,128]{1,0:T(8,128)S(1)}, f32[456,128]{1,0:T(8,128)S(1)}, u32[]{:S(2)}, u32[]{:S(2)}) collective-permute-start(f32[456,128]{1,0:T(8,128)S(1)} %concatenate.6), channel_id=1, source_target_pairs={{0,1},{1,2},{2,3},{3,4},{4,5},{5,6},{6,7},{7,0},{8,9},{9,10},{10,1... | collective-permute-start | bytes 700424 | tf_op jit(solution)/shard_map/ppermute | solution.py:735
  17.8 10.8 %collective-permute-start.3 = (f32[456,128]{1,0:T(8,128)S(1)}, f32[456,128]{1,0:T(8,128)S(1)}, u32[]{:S(2)}, u32[]{:S(2)}) collective-permute-start(f32[456,128]{1,0:T(8,128)S(1)} %concatenate.7), channel_id=1, source_target_pairs={{0,7},{1,0},{2,1},{3,2},{4,3},{5,4},{6,5},{7,6},{8,15},{9,8},{10,9... | collective-permute-start | bytes 700424 | tf_op jit(solution)/shard_map/ppermute | solution.py:735
  28.6 0.7 copy-start.2
  28.6 0.8 %copy-start.3 = (f32[456,128]{1,0:T(8,128)}, f32[456,128]{1,0:T(8,128)S(1)}, u32[]{:S(2)}) copy-start(f32[456,128]{1,0:T(8,128)S(1)} %collective-permute-done.3.right) | copy-start | bytes 700420
  44.1 6.0 %collective-permute-start.4 = (f32[288,128]{1,0:T(8,128)}, f32[288,128]{1,0:T(8,128)S(1)}, u32[]{:S(2)}, u32[]{:S(2)}) collective-permute-start(f32[288,128]{1,0:T(8,128)} %get-tuple-element.24), channel_id=1, source_target_pairs={{0,1},{1,2},{2,3},{3,4},{4,5},{5,6},{6,7},{7,0},{8,9},{9,10},{10,1... | collective-permute-start | bytes 442376 | tf_op jit(solution)/shard_map/ppermute | solution.py:735
  44.1 6.0 %collective-permute-start.5 = (f32[288,128]{1,0:T(8,128)}, f32[288,128]{1,0:T(8,128)S(1)}, u32[]{:S(2)}, u32[]{:S(2)}) collective-permute-start(f32[288,128]{1,0:T(8,128)} %get-tuple-element.25), channel_id=1, source_target_pairs={{0,7},{1,0},{2,1},{3,2},{4,3},{5,4},{6,5},{7,6},{8,15},{9,8},{10,9... | collective-permute-start | bytes 442376 | tf_op jit(solution)/shard_map/ppermute | solution.py:735
  51.7 19.6 %collective-permute-start.7 = (f32[96,128]{1,0:T(8,128)S(1)}, f32[96,128]{1,0:T(8,128)S(1)}, u32[]{:S(2)}, u32[]{:S(2)}) collective-permute-start(f32[96,128]{1,0:T(8,128)S(1)} %get-tuple-element.26), channel_id=1, source_target_pairs={{0,120},{8,0},{16,8},{24,16},{32,24},{40,32},{48,40},{56,48},{64,5... | collective-permute-start | bytes 147464 | tf_op jit(solution)/shard_map/ppermute | solution.py:735
  56.7 14.6 %collective-permute-start.6 = (f32[96,128]{1,0:T(8,128)S(1)}, f32[96,128]{1,0:T(8,128)S(1)}, u32[]{:S(2)}, u32[]{:S(2)}) collective-permute-start(f32[96,128]{1,0:T(8,128)S(1)} %get-tuple-element.27), channel_id=1, source_target_pairs={{0,8},{8,16},{16,24},{24,32},{32,40},{40,48},{48,56},{56,64},{64,7... | collective-permute-start | bytes 147464 | tf_op jit(solution)/shard_map/ppermute | solution.py:735
  71.3 0.6 copy-start.6
  71.3 0.6 copy-start.7

commit v2 on v1

--- a/solution.py
+++ b/solution.py
@@ -51,8 +51,6 @@
 Y_UP = [i for i in range(19) if DIRECTIONS[i][1] == 1]
 Y_DOWN = [i for i in range(19) if DIRECTIONS[i][1] == -1]
 
-VMEM_LIMIT = 58 * 1024 * 1024
-
 
 def opposite(i):
     if i == 0:
@@ -60,8 +58,8 @@
     return i + 1 if i % 2 == 1 else i - 1
 
 
-def params():
-    return pltpu.CompilerParams(vmem_limit_bytes=VMEM_LIMIT)
+def params(mebibytes):
+    return pltpu.CompilerParams(vmem_limit_bytes=mebibytes * 1024 * 1024)
 
 
 def cost(flops, moved):
@@ -84,24 +82,14 @@
 
 
 def prepare_kernel(
-    place, velocity, pop, up, down, face_up, face_down, ends_up, ends_down, sem, face_sem
+    place, velocity, pop, up, down, sem
 ):
-    faces = []
-    for k in range(5):
-        faces.append(
-            pltpu.make_async_copy(
-                pop.at[Y_UP[k], :, pl.ds(WY - 8, 8), :], ends_up.at[k], face_sem.at[0]
-            )
-        )
-        faces.append(
-            pltpu.make_async_copy(pop.at[Y_DOWN[k], :, pl.ds(0, 8), :], ends_down.at[k], face_sem.at[0])
-        )
     copies = []
     for k in range(5):
         rows = pl.ds(STATE_ROWS + k * WY, WY)
         copies.append(pltpu.make_async_copy(pop.at[X_UP[k], WX - 1], up.at[rows, :], sem.at[0]))
         copies.append(pltpu.make_async_copy(pop.at[X_DOWN[k], 0], down.at[rows, :], sem.at[0]))
-    for copy in faces + copies:
+    for copy in copies:
         copy.start()
     px, py, pz = origin_terms(place, velocity)
     wx, wy, wz = velocity[3:4], velocity[4:5], velocity[5:6]
@@ -119,30 +107,19 @@
             row = values[c][:, b * 128 : (b + 1) * 128]
             up[c * GROUPS + b : c * GROUPS + b + 1, :] = row
             down[c * GROUPS + b : c * GROUPS + b + 1, :] = row
-    for copy in faces:
-        copy.wait()
-    for k in range(5):
-        face_up[k * WX : (k + 1) * WX, :] = ends_up[k, :, 7, :]
-        face_down[k * WX : (k + 1) * WX, :] = ends_down[k, :, 0, :]
     for copy in copies:
         copy.wait()
 
 
 def prepare(place, velocity, populations):
     shape = jax.ShapeDtypeStruct((STATE_ROWS + FACE, 128), jnp.float32)
-    face = jax.ShapeDtypeStruct((FACE, 128), jnp.float32)
     return pl.pallas_call(
         prepare_kernel,
-        out_shape=(shape, shape, face, face),
-        in_specs=[whole(), whole(), anywhere()],
-        out_specs=(whole(),) * 4,
-        scratch_shapes=[
-            pltpu.VMEM((5, WX, 8, NZ), jnp.float32),
-            pltpu.VMEM((5, WX, 8, NZ), jnp.float32),
-            pltpu.SemaphoreType.DMA((1,)),
-            pltpu.SemaphoreType.DMA((1,)),
-        ],
-        compiler_params=params(),
+        out_shape=(shape, shape),
+        in_specs=[whole(), whole(), hbm()],
+        out_specs=(whole(),) * 2,
+        scratch_shapes=[pltpu.SemaphoreType.DMA((1,))],
+        compiler_params=params(48),
         cost_estimate=cost(100_000, 2_600_000),
         name="prepare",
     )(place, velocity, populations)
@@ -224,10 +201,15 @@
     return keys, values
 
 
-def pick_kernel(sizes, place, cell, heading, floe, cells, words, work, dense, turned):
+def pick_kernel(
+    sizes, cell, heading, floe, pop, cells, words, work, dense, chosen, face_up, face_down,
+    turned, resident, sem,
+):
+    load = pltpu.make_async_copy(pop, resident, sem.at[0])
+    load.start()
     size_along, size_across = sizes
-    a = place[0]
-    b = place[1]
+    a = lax.axis_index("along")
+    b = lax.axis_index("across")
     keys = []
     values = []
     for v in range(8):
@@ -276,6 +258,22 @@
         return product(column_hot(own, start), payload, NT)
 
     over_windows(work, scatter, window_adder(dense))
+    load.wait()
+    for k in range(5):
+        face_up[k * WX : (k + 1) * WX, :] = resident[Y_UP[k], :, WY - 1, :]
+        face_down[k * WX : (k + 1) * WX, :] = resident[Y_DOWN[k], :, 0, :]
+    chosen[COLUMNS:] = jnp.zeros((PADDED_COLUMNS - COLUMNS, NZ), jnp.float32)
+
+    def select(x, carry):
+        rows = pl.ds(pl.multiple_of(x * WY, WY), WY)
+        where = dense[rows, :]
+        value = jnp.zeros((WY, NZ), jnp.float32)
+        for i in range(1, 19):
+            value = jnp.where(where == float(i), resident[i, x], value)
+        chosen[rows, :] = value
+        return carry
+
+    lax.fori_loop(0, WX, select, 0, unroll=2)
 
 
 def window_adder(dense):
@@ -304,12 +302,17 @@
     lax.fori_loop(8, work[2, 0], step, 0)
 
 
+def hbm():
+    return pl.BlockSpec(memory_space=pltpu.HBM)
+
+
 def smem():
     return pl.BlockSpec(memory_space=pltpu.SMEM)
 
 
-def pick(sizes, place, cell, heading, floe):
+def pick(sizes, cell, heading, floe, populations):
     links = cell.shape[0] * cell.shape[1]
+    face = jax.ShapeDtypeStruct((FACE, 128), jnp.float32)
     row = jax.ShapeDtypeStruct((1, links), jnp.int32)
     return pl.pallas_call(
         functools.partial(pick_kernel, sizes),
@@ -318,39 +321,25 @@
             row,
             jax.ShapeDtypeStruct((3, 32), jnp.int32),
             jax.ShapeDtypeStruct((PADDED_COLUMNS, NZ), jnp.float32),
+            jax.ShapeDtypeStruct((PADDED_COLUMNS, NZ), jnp.float32),
+            face,
+            face,
         ),
-        in_specs=[smem(), whole(), whole(), whole()],
-        out_specs=(whole(), whole(), smem(), whole()),
-        scratch_shapes=[pltpu.VMEM((128, 128), jnp.int32)],
-        compiler_params=params(),
+        in_specs=[whole(), whole(), whole(), hbm()],
+        out_specs=(whole(), whole(), smem(), whole(), whole(), whole(), whole()),
+        scratch_shapes=[
+            pltpu.VMEM((128, 128), jnp.int32),
+            pltpu.VMEM(populations.shape, jnp.float32),
+            pltpu.SemaphoreType.DMA((1,)),
+        ],
+        compiler_params=params(48),
         cost_estimate=cost(7_000_000_000, 1_000_000),
         name="pick",
-    )(place, cell, heading, floe)
-
-
-def gather_kernel(work, cell, dense, pop_hbm, out, pop, chosen, sem):
-    def loading(s):
-        return pltpu.make_async_copy(
-            pop_hbm.at[:, pl.ds(s * 128, 128)], pop.at[:, pl.ds(s * 128, 128)], sem.at[s]
-        )
-
-    for s in range(8):
-        loading(s).start()
-    chosen[COLUMNS:] = jnp.zeros((PADDED_COLUMNS - COLUMNS, NZ), jnp.float32)
+    )(cell, heading, floe, populations)
+
+
+def gather_kernel(work, cell, chosen, out):
     out[...] = jnp.zeros_like(out)
-
-    def select(s, carry):
-        loading(s).wait()
-        for part in range(4):
-            rows = pl.ds(pl.multiple_of(s * 128, 128) + part * 32, 32)
-            where = dense[rows, :]
-            value = jnp.zeros((32, 128), jnp.float32)
-            for i in range(1, 19):
-                value = jnp.where(where == float(i), pop[i, rows, :], value)
-            chosen[rows, :] = value
-        return carry
-
-    lax.fori_loop(0, 8, select, 0)
 
     def read(at, start):
         own = cell[:, at]
@@ -367,21 +356,16 @@
     over_windows(work, read, add)
 
 
-def gather(work, cell, dense, columns):
+def gather(work, cell, chosen):
     return pl.pallas_call(
         gather_kernel,
         out_shape=jax.ShapeDtypeStruct(cell.shape, jnp.float32),
-        in_specs=[smem(), whole(), whole(), anywhere()],
+        in_specs=[smem(), whole(), whole()],
         out_specs=whole(),
-        scratch_shapes=[
-            pltpu.VMEM(columns.shape, jnp.float32),
-            pltpu.VMEM((PADDED_COLUMNS, NZ), jnp.float32),
-            pltpu.SemaphoreType.DMA((8,)),
-        ],
-        compiler_params=params(),
-        cost_estimate=cost(6_000_000_000, 12_000_000),
+        compiler_params=params(12),
+        cost_estimate=cost(6_000_000_000, 2_000_000),
         name="gather",
-    )(work, cell, dense, columns)
+    )(work, cell, chosen)
 
 
 def bits(table, heading):
@@ -508,7 +492,7 @@
             pltpu.VMEM((2, 256, CHUNK), jnp.bfloat16),
             pltpu.VMEM((9 * 128, 256), jnp.float32),
         ],
-        compiler_params=params(),
+        compiler_params=params(18),
         cost_estimate=cost(8_000_000_000, 2_000_000),
         name="floes",
     )(cell, words, here, mine, low, high, left, right)
@@ -541,13 +525,14 @@
         out_shape=jax.ShapeDtypeStruct((PADDED_COLUMNS, NZ), jnp.float32),
         in_specs=[smem(), whole(), whole()],
         out_specs=whole(),
-        compiler_params=params(),
+        compiler_params=params(8),
         cost_estimate=cost(3_000_000_000, 1_000_000),
         name="spread",
     )(work, cell, taken)
 
 
-SLAB = 4
+SLAB = 2
+SLOTS = 4
 SLABS = WX // SLAB
 TOP = 8
 
@@ -651,15 +636,15 @@
     loading(0).wait()
 
     def slab(s, carry):
-        slot = lax.rem(s, 2)
+        slot = lax.rem(s, SLOTS)
 
         @pl.when(s + 1 < SLABS)
         def _():
             loading(s + 1).wait()
 
-        @pl.when(s >= 2)
+        @pl.when(s >= SLOTS)
         def _():
-            storing(s - 2, slot).wait()
+            storing(s - SLOTS, slot).wait()
 
         def plane(inner, inside):
             for j in range(WY // 8):
@@ -671,8 +656,8 @@
         return carry
 
     lax.fori_loop(0, SLABS, slab, 0)
-    storing(SLABS - 2, (SLABS - 2) % 2).wait()
-    storing(SLABS - 1, (SLABS - 1) % 2).wait()
+    for s in range(SLABS - SLOTS, SLABS):
+        storing(s, s % SLOTS).wait()
 
 
 def collide(dense_dir, dense_take, low, high, left, right, populations):
@@ -683,14 +668,37 @@
         out_specs=anywhere(),
         scratch_shapes=[
             pltpu.VMEM((19, WX + 2, WY + 16, NZ), jnp.float32),
-            pltpu.VMEM((2, 19, SLAB, WY, NZ), jnp.float32),
+            pltpu.VMEM((SLOTS, 19, SLAB, WY, NZ), jnp.float32),
             pltpu.SemaphoreType.DMA((SLABS,)),
-            pltpu.SemaphoreType.DMA((2,)),
+            pltpu.SemaphoreType.DMA((SLOTS,)),
         ],
-        compiler_params=params(),
+        compiler_params=params(30),
         cost_estimate=cost(40_000_000, 24_000_000),
         name="collide",
     )(dense_dir, dense_take, low, high, left, right, populations)
+
+
+def fold_kernel(dense, mid, left, right, own, to_low, to_high):
+    def total(k):
+        rows = slice(k * STATE_ROWS, (k + 1) * STATE_ROWS)
+        return mid[rows] + (left[rows] + right[rows])
+
+    to_low[...] = total(0)
+    own[...] = total(1)
+    to_high[...] = total(2)
+
+
+def fold(dense, mid, left, right):
+    shape = jax.ShapeDtypeStruct((STATE_ROWS, 128), jnp.float32)
+    return pl.pallas_call(
+        fold_kernel,
+        out_shape=(shape,) * 3,
+        in_specs=[anywhere(), whole(), whole(), whole()],
+        out_specs=(whole(),) * 3,
+        compiler_params=params(4),
+        cost_estimate=cost(100_000, 600_000),
+        name="fold",
+    )(dense, mid, left, right)
 
 
 def motion_kernel(own, low, high, place, velocity, response, out):
@@ -724,7 +732,7 @@
         out_shape=jax.ShapeDtypeStruct(velocity.shape, jnp.float32),
         in_specs=[whole()] * 6,
         out_specs=whole(),
-        compiler_params=params(),
+        compiler_params=params(4),
         cost_estimate=cost(200_000, 300_000),
         name="motion",
     )(own, low, high, place, velocity, response)
@@ -737,17 +745,17 @@
 
 def body(populations, link_cell, link_dir, link_floe, floe_place, floe_velocity, floe_response):
     sizes = (lax.axis_size("along"), lax.axis_size("across"))
-    where = jnp.stack([lax.axis_index("along"), lax.axis_index("across")]).astype(jnp.int32)
     links = link_cell.shape[-1]
     cell = link_cell.reshape(links // 128, 128)
     heading = link_dir.reshape(links // 128, 128)
     floe = link_floe.reshape(links // 128, 128)
-    columns = populations.reshape(19, COLUMNS, NZ)
-
-    up, down, face_up, face_down = prepare(floe_place, floe_velocity, populations)
+
+    up, down = prepare(floe_place, floe_velocity, populations)
     low = shifted(up, "along", 1)
     high = shifted(down, "along", -1)
-    cells, words, work, dense_dir = pick(sizes, where, cell, heading, floe)
+    cells, words, work, dense_dir, chosen, face_up, face_down = pick(
+        sizes, cell, heading, floe, populations
+    )
 
     def rows(block, k, y):
         at = STATE_ROWS + k * WY + y
@@ -764,19 +772,19 @@
     )
     left = shifted(to_up, "across", 1)
     right = shifted(to_down, "across", -1)
-    here = gather(work, cells, dense_dir, columns)
+    here = gather(work, cells, chosen)
     taken, loads_left, loads_mid, loads_right = floes(
         cells, words, here, up, low, high, left, right
     )
     from_right = shifted(loads_left, "across", -1)
     from_left = shifted(loads_right, "across", 1)
     dense_take = spread_out(work, cells, taken)
-    three = loads_mid + from_left + from_right
-    from_high = shifted(three[:STATE_ROWS], "along", -1)
-    from_low = shifted(three[2 * STATE_ROWS :], "along", 1)
+    own, to_low, to_high = fold(dense_take, loads_mid, from_left, from_right)
+    from_high = shifted(to_low, "along", -1)
+    from_low = shifted(to_high, "along", 1)
     relaxed = collide(dense_dir, dense_take, low, high, left, right, populations)
     moved = motion(
-        three[STATE_ROWS : 2 * STATE_ROWS],
+        own,
         from_low,
         from_high,
         floe_place,

time: 74.7 us -> 58.9 us (0.79)
  Pallas kernels: 48.6 us -> 34.2 us
  waiting for transfers between devices: 3.21 us -> 5.99 us
  other arithmetic: 1.59 us -> 0.01 us
  local copies, waits for them, and re-layouts: 2.92 us -> 1.74 us
    pallas_call x1, Pallas kernels: 7.65 us -> 2.5 us  [gather(): pl.pallas_call(gather_kernel, out_shape=jax.ShapeDtypeStruct(cell.shape,...]
    pallas_call x1, Pallas kernels: 11.2 us -> 8.11 us  [collide(): pl.pallas_call(collide_kernel, out_shape=jax.ShapeDtypeStruct(populations...]
    ppermute x8, waiting for transfers between devices: 3.21 us -> 5.99 us  [shifted(): lax.ppermute(value, axis, [(i, (i + step) % count) for i in range(count)])]
    pallas_call x1 -> x2, Pallas kernels: 3.2 us -> 0.87 us  [the longest x1 0.84 us: prepare(): pl.pallas_call(prepare_kernel, out_shape=(shape, shape), in_specs=[whole(...]
    pallas_call x1, Pallas kernels: 14.7 us -> 12.7 us  [floes(): pl.pallas_call(floe_kernel, out_shape=(jax.ShapeDtypeStruct(cell.shape, j...]
    pallas_call x1, Pallas kernels: 3.36 us -> 2.29 us  [spread_out(): pl.pallas_call(spread_kernel, out_shape=jax.ShapeDtypeStruct((PADDED_COLU...]
    add x1 -> x0, other arithmetic: 0.94 us -> none  [body(): three = loads_mid + from_left + from_right]
    pallas_call x1, Pallas kernels: 1.68 us -> 0.75 us  [motion(): pl.pallas_call(motion_kernel, out_shape=jax.ShapeDtypeStruct(velocity.sha...]
  transfers between devices with their start and end apart: 8 -> 8, of which waited for: 2 -> 4; matrix products, arithmetic and copies ran while one was open for 2% -> 0% of each run, Pallas kernels for 39% -> 34%
where the time goes in v2:
time: 58.9 us; the launch traced here: 58.5 us
  Pallas kernels  34.2 us (58%)
  starting transfers between devices  15.8 us (27%)
  waiting for transfers between devices  5.99 us (10%)
  local copies, waits for them, and re-layouts  1.74 us (3%)
  between operations  0.84 us (1%)
    ppermute x8, starting transfers between devices, shifted(): lax.ppermute(value, axis, [(i, (i + step) % count) for i in range(count)])  15.8 us
    pallas_call x1, Pallas kernels, floes(): pl.pallas_call(floe_kernel, out_shape=(jax.ShapeDtypeStruct(cell.shape, j...  12.7 us
    pallas_call x1, Pallas kernels, collide(): pl.pallas_call(collide_kernel, out_shape=jax.ShapeDtypeStruct(populations...  8.11 us
    pallas_call x1, Pallas kernels, pick(): pl.pallas_call(functools.partial(pick_kernel, sizes), out_shape=(row, row...  6.94 us
    ppermute x8, waiting for transfers between devices, shifted(): lax.ppermute(value, axis, [(i, (i + step) % count) for i in range(count)])  5.99 us
    pallas_call x1, Pallas kernels, gather(): pl.pallas_call(gather_kernel, out_shape=jax.ShapeDtypeStruct(cell.shape,...  2.5 us
    pallas_call x1, Pallas kernels, spread_out(): pl.pallas_call(spread_kernel, out_shape=jax.ShapeDtypeStruct((PADDED_COLU...  2.29 us
    unnamed x22, local copies, waits for them, and re-layouts  1.63 us
  transfers between devices with their start and end apart: 8, of which 4 were waited for; matrix products, arithmetic and copies ran while one was open for 0% of the time, Pallas kernels for 34%

profile of v2, /device:TPU:0, one launch (start us, length us, event | category | flops | bytes accessed | tf_op | source)
XLA Modules:
  0.0 58.5 jit_solution(2764293123427818048)
XLA Ops:
  0.6 0.0 copy-start
  0.6 0.8 %copy-done = f32[6,2048]{1,0:T(8,128)S(1)} copy-done((f32[6,2048]{1,0:T(8,128)S(1)}, f32[6,2048]{1,0:T(8,128)}, u32[]{:S(2)}) %copy-start) | copy-done | bytes 49176
  1.5 0.0 copy-start.2
  1.5 0.8 %copy-done.2 = f32[3,2048]{1,0:T(4,128)S(1)} copy-done((f32[3,2048]{1,0:T(4,128)S(1)}, f32[3,2048]{1,0:T(4,128)}, u32[]{:S(2)}) %copy-start.2) | copy-done | bytes 24600
  2.2 0.0 copy-start.5
  2.2 0.0 copy-start.6
  2.2 0.0 copy-start.7
  2.2 0.8 %prepare.1 = (f32[256,128]{1,0:T(8,128)S(1)}, f32[256,128]{1,0:T(8,128)S(1)}) custom-call(f32[3,2048]{1,0:T(4,128)S(1)} %copy-done.2, f32[6,2048]{1,0:T(8,128)S(1)} %copy-done, f32[19,32,32,128]{3,2,1,0:T(8,128)} %pop_hbm.1), custom_call_target="tpu_custom_call" | custom-call | flops 100000 | bytes 2600000 | tf_op jit(solution)/shard_map/prepare/pallas_call | solution.py:116
  3.1 5.4 %collective-permute-start.1 = (f32[256,128]{1,0:T(8,128)S(1)}, f32[256,128]{1,0:T(8,128)S(1)}, u32[]{:S(2)}, u32[]{:S(2)}) collective-permute-start(f32[256,128]{1,0:T(8,128)S(1)} %get-tuple-element.24), channel_id=1, source_target_pairs={{0,120},{8,0},{16,8},{24,16},{32,24},{40,32},{48,40},{56,48},{64,5... | collective-permute-start | bytes 393224 | tf_op jit(solution)/shard_map/ppermute | solution.py:743
  8.5 0.0 collective-permute-start
  8.5 0.0 copy-done.5
  8.5 0.0 copy-done.6
  8.5 0.0 copy-done.7
  8.5 6.9 %pick.1 = (s32[1,8192]{1,0:T(1,128)S(1)}, s32[1,8192]{1,0:T(1,128)S(1)}, s32[3,32]{1,0:T(4,128)S(1)}, f32[1184,128]{1,0:T(8,128)S(1)}, f32[1184,128]{1,0:T(8,128...) custom-call(s32[64,128]{1,0:T(8,128)S(1)} %bitcast.5, s32[64,128]{1,0:T(8,128)S(1)} %bitcast.6, ...), custom_call_target="tpu_custom_call" | custom-call | flops 7000000000 | bytes 1000000 | tf_op jit(solution)/shard_map/pick/pallas_call | solution.py:317
  15.4 0.0 collective-permute-done.1.high
  15.5 1.3 %collective-permute-done.low = f32[256,128]{1,0:T(8,128)S(1)} collective-permute-done((f32[256,128]{1,0:T(8,128)S(1)}, f32[256,128]{1,0:T(8,128)S(1)}, u32[]{:S(2)}, u32[]{:S(2)}) %collective-permute-start) | collective-permute-done | bytes 131104 | tf_op jit(solution)/shard_map/ppermute | solution.py:743
  16.8 2.1 %collective-permute-start.3 = (f32[456,128]{1,0:T(8,128)S(1)}, f32[456,128]{1,0:T(8,128)S(1)}, u32[]{:S(2)}, u32[]{:S(2)}) collective-permute-start(f32[456,128]{1,0:T(8,128)S(1)} %concatenate.7), channel_id=1, source_target_pairs={{0,7},{1,0},{2,1},{3,2},{4,3},{5,4},{6,5},{7,6},{8,15},{9,8},{10,9... | collective-permute-start | bytes 700424 | tf_op jit(solution)/shard_map/ppermute | solution.py:743
  18.9 0.0 collective-permute-start.2
  18.9 2.5 %gather.1.here = f32[1,8192]{1,0:T(1,128)S(1)} custom-call(s32[3,32]{1,0:T(4,128)S(1)} %get-tuple-element.19.work, s32[1,8192]{1,0:T(1,128)S(1)} %get-tuple-element.20.cell, f32[1184,128]{1,0:T(8,128)S(1)} %get-tuple-element.22.chosen), custom_call_target="tpu_custom_call" | custom-call | flops 6000000000 | bytes 2000000 | tf_op jit(solution)/shard_map/gather/pallas_call | solution.py:360
  21.4 1.0 %collective-permute-done.3.right = f32[456,128]{1,0:T(8,128)S(1)} collective-permute-done((f32[456,128]{1,0:T(8,128)S(1)}, f32[456,128]{1,0:T(8,128)S(1)}, u32[]{:S(2)}, u32[]{:S(2)}) %collective-permute-start.3) | collective-permute-done | bytes 233504 | tf_op jit(solution)/shard_map/ppermute | solution.py:743
  22.4 3.2 %collective-permute-done.2.left = f32[456,128]{1,0:T(8,128)S(1)} collective-permute-done((f32[456,128]{1,0:T(8,128)S(1)}, f32[456,128]{1,0:T(8,128)S(1)}, u32[]{:S(2)}, u32[]{:S(2)}) %collective-permute-start.2) | collective-permute-done | bytes 233504 | tf_op jit(solution)/shard_map/ppermute | solution.py:743
  25.6 0.0 slice-start
  25.6 0.0 slice-start.1
  25.6 0.0 slice-start.2
  25.6 12.7 %floes.1 = (f32[1,8192]{1,0:T(1,128)S(1)}, f32[288,128]{1,0:T(8,128)S(1)}, f32[288,128]{1,0:T(8,128)S(1)}, f32[288,128]{1,0:T(8,128)S(1)}) custom-call(s32[1,8192]{1,0:T(1,128)S(1)} %get-tuple-element.20.cell, s32[1,8192]{1,0:T(1,128)S(1)} %get-tuple-element.21.words, f32[1,8192]{1,0:T(1,128)S(1)} %gather.1.here, f32[256,128]{1,0:T(8,128)S(1)} %get-tuple-element.23.mine, ...), custom_call_target="tpu_custom_call" | custom-call | flops 8000000000 | bytes 2000000 | tf_op jit(solution)/shard_map/floes/pallas_call | solution.py:483
  38.3 0.0 collective-permute-start.4
  38.4 2.9 %collective-permute-start.5 = (f32[288,128]{1,0:T(8,128)S(1)}, f32[288,128]{1,0:T(8,128)S(1)}, u32[]{:S(2)}, u32[]{:S(2)}) collective-permute-start(f32[288,128]{1,0:T(8,128)S(1)} %get-tuple-element.30), channel_id=1, source_target_pairs={{0,7},{1,0},{2,1},{3,2},{4,3},{5,4},{6,5},{7,6},{8,15},{9,8},{10,9... | collective-permute-start | bytes 442376 | tf_op jit(solution)/shard_map/ppermute | solution.py:743
  41.3 2.3 %spread.1.dense_take.dense = f32[1184,128]{1,0:T(8,128)S(1)} custom-call(s32[3,32]{1,0:T(4,128)S(1)} %get-tuple-element.19.work, s32[1,8192]{1,0:T(1,128)S(1)} %get-tuple-element.20.cell, f32[1,8192]{1,0:T(1,128)S(1)} %get-tuple-element.27.taken), custom_call_target="tpu_custom_call" | custom-call | flops 3000000000 | bytes 1000000 | tf_op jit(solution)/shard_map/spread/pallas_call | solution.py:523
  43.6 0.5 collective-permute-done.4.left
  44.1 0.0 collective-permute-done.5.right
  44.2 0.1 collective-permute-start.6
  44.2 5.3 %collective-permute-start.7 = (f32[96,128]{1,0:T(8,128)S(1)}, f32[96,128]{1,0:T(8,128)S(1)}, u32[]{:S(2)}, u32[]{:S(2)}) collective-permute-start(f32[96,128]{1,0:T(8,128)S(1)} %get-tuple-element.33), channel_id=1, source_target_pairs={{0,120},{8,0},{16,8},{24,16},{32,24},{40,32},{48,40},{56,48},{64,5... | collective-permute-start | bytes 147464 | tf_op jit(solution)/shard_map/ppermute | solution.py:743
  49.6 0.0 slice-done
  49.6 0.0 slice-done.1
  49.6 0.0 slice-done.2
  49.6 0.0 copy-start.1
  49.6 0.0 copy-start.3
  49.6 0.0 copy-start.4
  49.6 8.1 %collide.1 = f32[19,32,32,128]{3,2,1,0:T(8,128)} custom-call(f32[1184,128]{1,0:T(8,128)S(1)} %get-tuple-element.18.dense_dir, f32[1184,128]{1,0:T(8,128)S(1)} %spread.1.dense_take.dense, f32[256,128]{1,0:T(8,128)S(1)} %collective-permute-done.low, f32[256,128]{1,0:T(8,128)S(1)} %collective-permute-done.1.high, f32[456,128]{1,0:T(8,128)S(1)} %collective-permute-done.2.left, ...), custom_call_target="tpu_custom_call" | custom-call | flops 40000000 | bytes 24000000 | tf_op jit(solution)/shard_map/collide/pallas_call | solution.py:664
  57.7 0.0 collective-permute-done.6.low
  57.8 0.0 collective-permute-done.7.high
  57.8 0.0 copy-done.1
  57.8 0.0 copy-done.3
  57.8 0.0 copy-done.4
  57.8 0.7 %motion.1 = f32[6,2048]{1,0:T(8,128)} custom-call(f32[96,128]{1,0:T(8,128)S(1)} %get-tuple-element.31.own, f32[96,128]{1,0:T(8,128)S(1)} %collective-permute-done.6.low, f32[96,128]{1,0:T(8,128)S(1)} %collective-permute-done.7.high, f32[3,2048]{1,0:T(4,128)S(1)} %copy-done.3, f32[6,2048]{1,0:T(8,128)S(1)} %copy-done.1, f32[2,2048]{1,0:T(2,128)S(1)} %copy-done.4), custom_call_target="tpu_custom_call" | custom-call | flops 200000 | bytes 300000 | tf_op jit(solution)/shard_map/motion/pallas_call | solution.py:730
  (10 shorter events, 0.1 us)
Async XLA Ops:
  0.6 0.8 %copy-start = (f32[6,2048]{1,0:T(8,128)S(1)}, f32[6,2048]{1,0:T(8,128)}, u32[]{:S(2)}) copy-start(f32[6,2048]{1,0:T(8,128)} %velocity.3) | copy-start | bytes 147460
  1.5 0.8 %copy-start.2 = (f32[3,2048]{1,0:T(4,128)S(1)}, f32[3,2048]{1,0:T(4,128)}, u32[]{:S(2)}) copy-start(f32[3,2048]{1,0:T(4,128)} %place.3) | copy-start | bytes 73732
  2.2 6.2 %copy-start.5 = (s32[1,1,8192]{2,1,0:T(1,128)S(1)}, s32[1,1,8192]{2,1,0:T(1,128)}, u32[]{:S(2)}) copy-start(s32[1,1,8192]{2,1,0:T(1,128)} %param.8) | copy-start | bytes 98308
  2.2 6.2 %copy-start.6 = (s32[1,1,8192]{2,1,0:T(1,128)S(1)}, s32[1,1,8192]{2,1,0:T(1,128)}, u32[]{:S(2)}) copy-start(s32[1,1,8192]{2,1,0:T(1,128)} %param.9) | copy-start | bytes 98308
  2.2 6.2 %copy-start.7 = (s32[1,1,8192]{2,1,0:T(1,128)S(1)}, s32[1,1,8192]{2,1,0:T(1,128)}, u32[]{:S(2)}) copy-start(s32[1,1,8192]{2,1,0:T(1,128)} %param.10) | copy-start | bytes 98308
  3.1 12.3 %collective-permute-start.1 = (f32[256,128]{1,0:T(8,128)S(1)}, f32[256,128]{1,0:T(8,128)S(1)}, u32[]{:S(2)}, u32[]{:S(2)}) collective-permute-start(f32[256,128]{1,0:T(8,128)S(1)} %get-tuple-element.24), channel_id=1, source_target_pairs={{0,120},{8,0},{16,8},{24,16},{32,24},{40,32},{48,40},{56,48},{64,5... | collective-permute-start | bytes 393224 | tf_op jit(solution)/shard_map/ppermute | solution.py:743
  8.5 8.3 %collective-permute-start = (f32[256,128]{1,0:T(8,128)S(1)}, f32[256,128]{1,0:T(8,128)S(1)}, u32[]{:S(2)}, u32[]{:S(2)}) collective-permute-start(f32[256,128]{1,0:T(8,128)S(1)} %get-tuple-element.23.mine), channel_id=1, source_target_pairs={{0,8},{8,16},{16,24},{24,32},{32,40},{40,48},{48,56},{56,64},{64,7... | collective-permute-start | bytes 393224 | tf_op jit(solution)/shard_map/ppermute | solution.py:743
  16.8 5.6 %collective-permute-start.3 = (f32[456,128]{1,0:T(8,128)S(1)}, f32[456,128]{1,0:T(8,128)S(1)}, u32[]{:S(2)}, u32[]{:S(2)}) collective-permute-start(f32[456,128]{1,0:T(8,128)S(1)} %concatenate.7), channel_id=1, source_target_pairs={{0,7},{1,0},{2,1},{3,2},{4,3},{5,4},{6,5},{7,6},{8,15},{9,8},{10,9... | collective-permute-start | bytes 700424 | tf_op jit(solution)/shard_map/ppermute | solution.py:743
  18.9 6.7 %collective-permute-start.2 = (f32[456,128]{1,0:T(8,128)S(1)}, f32[456,128]{1,0:T(8,128)S(1)}, u32[]{:S(2)}, u32[]{:S(2)}) collective-permute-start(f32[456,128]{1,0:T(8,128)S(1)} %concatenate.6), channel_id=1, source_target_pairs={{0,1},{1,2},{2,3},{3,4},{4,5},{5,6},{6,7},{7,0},{8,9},{9,10},{10,1... | collective-permute-start | bytes 700424 | tf_op jit(solution)/shard_map/ppermute | solution.py:743
  25.6 24.0 %slice-start = ((s8[9961472]{0:T(1024)(128)(4,1)}), s8[4194304]{0:T(1024)(128)(4,1)S(1)}, s32[]{:S(2)}) async-start(s8[9961472]{0:T(1024)(128)(4,1)} %bitcast.3), calls=%async_computation | async-start | bytes 8388608
  25.6 24.0 %slice-start.1 = ((s8[9961472]{0:T(1024)(128)(4,1)}), s8[4194304]{0:T(1024)(128)(4,1)S(1)}, s32[]{:S(2)}) async-start(s8[9961472]{0:T(1024)(128)(4,1)} %bitcast.3), calls=%async_computation.1 | async-start | bytes 8388608
  25.6 24.0 %slice-start.2 = ((s8[9961472]{0:T(1024)(128)(4,1)}), s8[1572864]{0:T(1024)(128)(4,1)S(1)}, s32[]{:S(2)}) async-start(s8[9961472]{0:T(1024)(128)(4,1)} %bitcast.3), calls=%async_computation.2 | async-start | bytes 3145728
  38.3 5.8 %collective-permute-start.4 = (f32[288,128]{1,0:T(8,128)S(1)}, f32[288,128]{1,0:T(8,128)S(1)}, u32[]{:S(2)}, u32[]{:S(2)}) collective-permute-start(f32[288,128]{1,0:T(8,128)S(1)} %get-tuple-element.29), channel_id=1, source_target_pairs={{0,1},{1,2},{2,3},{3,4},{4,5},{5,6},{6,7},{7,0},{8,9},{9,10},{10,1... | collective-permute-start | bytes 442376 | tf_op jit(solution)/shard_map/ppermute | solution.py:743
  38.4 5.8 %collective-permute-start.5 = (f32[288,128]{1,0:T(8,128)S(1)}, f32[288,128]{1,0:T(8,128)S(1)}, u32[]{:S(2)}, u32[]{:S(2)}) collective-permute-start(f32[288,128]{1,0:T(8,128)S(1)} %get-tuple-element.30), channel_id=1, source_target_pairs={{0,7},{1,0},{2,1},{3,2},{4,3},{5,4},{6,5},{7,6},{8,15},{9,8},{10,9... | collective-permute-start | bytes 442376 | tf_op jit(solution)/shard_map/ppermute | solution.py:743
  44.2 13.6 %collective-permute-start.6 = (f32[96,128]{1,0:T(8,128)S(1)}, f32[96,128]{1,0:T(8,128)S(1)}, u32[]{:S(2)}, u32[]{:S(2)}) collective-permute-start(f32[96,128]{1,0:T(8,128)S(1)} %get-tuple-element.32), channel_id=1, source_target_pairs={{0,8},{8,16},{16,24},{24,32},{32,40},{40,48},{48,56},{56,64},{64,7... | collective-permute-start | bytes 147464 | tf_op jit(solution)/shard_map/ppermute | solution.py:743
  44.2 13.5 %collective-permute-start.7 = (f32[96,128]{1,0:T(8,128)S(1)}, f32[96,128]{1,0:T(8,128)S(1)}, u32[]{:S(2)}, u32[]{:S(2)}) collective-permute-start(f32[96,128]{1,0:T(8,128)S(1)} %get-tuple-element.33), channel_id=1, source_target_pairs={{0,120},{8,0},{16,8},{24,16},{32,24},{40,32},{48,40},{56,48},{64,5... | collective-permute-start | bytes 147464 | tf_op jit(solution)/shard_map/ppermute | solution.py:743
  49.6 8.2 %copy-start.1 = (f32[6,2048]{1,0:T(8,128)S(1)}, f32[6,2048]{1,0:T(8,128)}, u32[]{:S(2)}) copy-start(f32[6,2048]{1,0:T(8,128)} %velocity.3) | copy-start | bytes 147460
  49.6 8.2 %copy-start.3 = (f32[3,2048]{1,0:T(4,128)S(1)}, f32[3,2048]{1,0:T(4,128)}, u32[]{:S(2)}) copy-start(f32[3,2048]{1,0:T(4,128)} %place.3) | copy-start | bytes 73732
  49.6 8.2 %copy-start.4 = (f32[2,2048]{1,0:T(2,128)S(1)}, f32[2,2048]{1,0:T(2,128)}, u32[]{:S(2)}) copy-start(f32[2,2048]{1,0:T(2,128)} %response.1) | copy-start | bytes 49156

commit v3 on v2

--- a/solution.py
+++ b/solution.py
@@ -82,8 +82,14 @@
 
 
 def prepare_kernel(
-    place, velocity, pop, up, down, sem
+    place_hbm, velocity_hbm, pop, up, down, place, velocity, sem, small_sem
 ):
+    small = [
+        pltpu.make_async_copy(place_hbm, place, small_sem.at[0]),
+        pltpu.make_async_copy(velocity_hbm, velocity, small_sem.at[1]),
+    ]
+    for copy in small:
+        copy.start()
     copies = []
     for k in range(5):
         rows = pl.ds(STATE_ROWS + k * WY, WY)
@@ -91,6 +97,8 @@
         copies.append(pltpu.make_async_copy(pop.at[X_DOWN[k], 0], down.at[rows, :], sem.at[0]))
     for copy in copies:
         copy.start()
+    for copy in small:
+        copy.wait()
     px, py, pz = origin_terms(place, velocity)
     wx, wy, wz = velocity[3:4], velocity[4:5], velocity[5:6]
     scale = 1.0 / LEVER_SCALE
@@ -116,10 +124,15 @@
     return pl.pallas_call(
         prepare_kernel,
         out_shape=(shape, shape),
-        in_specs=[whole(), whole(), hbm()],
+        in_specs=[hbm(), hbm(), hbm()],
         out_specs=(whole(),) * 2,
-        scratch_shapes=[pltpu.SemaphoreType.DMA((1,))],
-        compiler_params=params(48),
+        scratch_shapes=[
+            pltpu.VMEM(place.shape, jnp.float32),
+            pltpu.VMEM(velocity.shape, jnp.float32),
+            pltpu.SemaphoreType.DMA((1,)),
+            pltpu.SemaphoreType.DMA((2,)),
+        ],
+        compiler_params=params(58),
         cost_estimate=cost(100_000, 2_600_000),
         name="prepare",
     )(place, velocity, populations)
@@ -401,8 +414,6 @@
             table[STATE_ROWS : 2 * STATE_ROWS, lanes] = (
                 state - first.astype(jnp.float32)
             ).astype(jnp.bfloat16)
-    payload[...] = jnp.zeros_like(payload)
-
     def first_half(t):
         slot = t % 2
         at = slice(t * CHUNK, (t + 1) * CHUNK)
@@ -453,12 +464,12 @@
         amount = weights * magnitude
         first = amount.astype(jnp.bfloat16)
         payload[slot, 0:STATE_ROWS, :] = first
-        payload[slot, 128 : 128 + STATE_ROWS, :] = (amount - first.astype(jnp.float32)).astype(
+        payload[slot, STATE_ROWS : 2 * STATE_ROWS, :] = (amount - first.astype(jnp.float32)).astype(
             jnp.bfloat16
         )
 
     def second_half(t):
-        value = product(hot[t % 2], payload[t % 2], NT)
+        value = product(payload[t % 2], hot[t % 2], NT)
         if t == 0:
             total[...] = value
         else:
@@ -472,10 +483,10 @@
     second_half(steps - 1)
     for ra in range(3):
         for rb in range(3):
-            rows = slice((ra * 3 + rb) * 128, (ra * 3 + rb + 1) * 128)
-            summed = total[rows, 0:128] + total[rows, 128:256]
+            lanes = slice((ra * 3 + rb) * 128, (ra * 3 + rb + 1) * 128)
+            summed = total[0:STATE_ROWS, lanes] + total[STATE_ROWS : 2 * STATE_ROWS, lanes]
             out = (loads_left, loads_mid, loads_right)[rb]
-            out[ra * STATE_ROWS : (ra + 1) * STATE_ROWS] = jnp.transpose(summed)[0:STATE_ROWS]
+            out[ra * STATE_ROWS : (ra + 1) * STATE_ROWS] = summed
 
 
 def floes(cell, words, here, mine, low, high, left, right):
@@ -489,8 +500,8 @@
             pltpu.VMEM((2 * STATE_ROWS, 9 * 128), jnp.bfloat16),
             pltpu.VMEM((2, 9 * 128, CHUNK), jnp.bfloat16),
             pltpu.VMEM((2, STATE_ROWS, CHUNK), jnp.float32),
-            pltpu.VMEM((2, 256, CHUNK), jnp.bfloat16),
-            pltpu.VMEM((9 * 128, 256), jnp.float32),
+            pltpu.VMEM((2, 2 * STATE_ROWS, CHUNK), jnp.bfloat16),
+            pltpu.VMEM((2 * STATE_ROWS, 9 * 128), jnp.float32),
         ],
         compiler_params=params(18),
         cost_estimate=cost(8_000_000_000, 2_000_000),
@@ -607,28 +618,27 @@
         mx = (d3 + d7) + (d9 + d11) + d13
         my = (d5 + d7) + (d15 - d9) + d17
         mz = (d1 + d11) + (d15 - d13) - d17
-        inverse = 1.0 / density
+        inverse = 1.5 / density
         ux = mx * inverse
         uy = my * inverse
         uz = mz * inverse
         scaled = density * RELAXATION
-        flat = scaled * (1.0 - 1.5 * (ux * ux + uy * uy + uz * uz))
-        linear = 3.0 * scaled
-        square = 4.5 * scaled
+        flat = scaled - (2.0 / 3.0) * scaled * (ux * ux + uy * uy + uz * uz)
+        parts = {w: (flat * w, scaled * (2.0 * w)) for w in (WEIGHTS[1], WEIGHTS[7])}
         out[slot, 0, inner, j * 8 : j * 8 + 8, :] = rest * centre + WEIGHTS[0] * flat
         for n in range(9):
             i = 2 * n + 1
-            step_x, step_y, step_z = DIRECTIONS[i]
             projection = None
-            for step, u in ((step_x, ux), (step_y, uy), (step_z, uz)):
+            for step, u in zip(DIRECTIONS[i], (ux, uy, uz)):
                 if step == 0:
                     continue
                 if projection is None:
                     projection = u
                 else:
                     projection = projection + u if step == 1 else projection - u
-            even = WEIGHTS[i] * (flat + square * (projection * projection))
-            odd = WEIGHTS[i] * (linear * projection)
+            level, slope = parts[WEIGHTS[i]]
+            odd = slope * projection
+            even = level + odd * projection
             plus, minus = both[n]
             out[slot, i, inner, j * 8 : j * 8 + 8, :] = rest * plus + (even + odd)
             out[slot, i + 1, inner, j * 8 : j * 8 + 8, :] = rest * minus + (even - odd)
@@ -651,7 +661,7 @@
                 tile(s * SLAB + inner, j, slot, inner)
             return inside
 
-        lax.fori_loop(0, SLAB, plane, 0)
+        lax.fori_loop(0, SLAB, plane, 0, unroll=True)
         storing(s, slot).start()
         return carry
 

time: 58.9 us -> 55.2 us (0.937)
  Pallas kernels: 34.2 us -> 32 us
  local copies, waits for them, and re-layouts: 1.74 us -> 0.15 us
    pallas_call x1, Pallas kernels: 12.7 us -> 11.1 us  [floes(): pl.pallas_call(floe_kernel, out_shape=(jax.ShapeDtypeStruct(cell.shape, j...]
    unnamed x22 -> x20, local copies, waits for them, and re-layouts: 1.63 us -> 0.05 us
    pallas_call x1, Pallas kernels: 8.11 us -> 6.6 us  [collide(): pl.pallas_call(collide_kernel, out_shape=jax.ShapeDtypeStruct(populations...]
    pallas_call x1, Pallas kernels: 0.84 us -> 1.78 us  [prepare(): pl.pallas_call(prepare_kernel, out_shape=(shape, shape), in_specs=[hbm(),...]
  transfers between devices with their start and end apart: 8 -> 8, of which waited for: 4 -> 4; matrix products, arithmetic and copies ran while one was open for 0% -> 0% of each run, Pallas kernels for 34% -> 33%
where the time goes in v3:
time: 55.2 us; the launch traced here: 55 us
  Pallas kernels  32 us (58%)
  starting transfers between devices  15.8 us (29%)
  waiting for transfers between devices  6.18 us (11%)
  between operations  0.87 us (2%)
    ppermute x8, starting transfers between devices, shifted(): lax.ppermute(value, axis, [(i, (i + step) % count) for i in range(count)])  15.8 us
    pallas_call x1, Pallas kernels, floes(): pl.pallas_call(floe_kernel, out_shape=(jax.ShapeDtypeStruct(cell.shape, j...  11.1 us
    pallas_call x1, Pallas kernels, pick(): pl.pallas_call(functools.partial(pick_kernel, sizes), out_shape=(row, row...  6.94 us
    pallas_call x1, Pallas kernels, collide(): pl.pallas_call(collide_kernel, out_shape=jax.ShapeDtypeStruct(populations...  6.6 us
    ppermute x8, waiting for transfers between devices, shifted(): lax.ppermute(value, axis, [(i, (i + step) % count) for i in range(count)])  6.18 us
    pallas_call x1, Pallas kernels, gather(): pl.pallas_call(gather_kernel, out_shape=jax.ShapeDtypeStruct(cell.shape,...  2.5 us
    pallas_call x1, Pallas kernels, spread_out(): pl.pallas_call(spread_kernel, out_shape=jax.ShapeDtypeStruct((PADDED_COLU...  2.28 us
    pallas_call x1, Pallas kernels, prepare(): pl.pallas_call(prepare_kernel, out_shape=(shape, shape), in_specs=[hbm(),...  1.78 us
  transfers between devices with their start and end apart: 8, of which 4 were waited for; matrix products, arithmetic and copies ran while one was open for 0% of the time, Pallas kernels for 33%

profile of v3, /device:TPU:0, one launch (start us, length us, event | category | flops | bytes accessed | tf_op | source)
XLA Modules:
  0.0 55.0 jit_solution(10491168738522555507)
XLA Ops:
  0.6 0.0 copy-start.6
  0.6 0.0 copy-start.5
  0.7 0.0 copy-start.4
  0.7 1.8 %prepare.1 = (f32[256,128]{1,0:T(8,128)}, f32[256,128]{1,0:T(8,128)}) custom-call(f32[3,2048]{1,0:T(4,128)} %place.1, f32[6,2048]{1,0:T(8,128)} %velocity.1, f32[19,32,32,128]{3,2,1,0:T(8,128)} %pop_hbm.1), custom_call_target="tpu_custom_call" | custom-call | flops 100000 | bytes 2600000 | tf_op jit(solution)/shard_map/prepare/pallas_call | solution.py:124
  2.4 5.4 %collective-permute-start.1 = (f32[256,128]{1,0:T(8,128)}, f32[256,128]{1,0:T(8,128)S(1)}, u32[]{:S(2)}, u32[]{:S(2)}) collective-permute-start(f32[256,128]{1,0:T(8,128)} %get-tuple-element.24), channel_id=1, source_target_pairs={{0,120},{8,0},{16,8},{24,16},{32,24},{40,32},{48,40},{56,48},{64,5... | collective-permute-start | bytes 393224 | tf_op jit(solution)/shard_map/ppermute | solution.py:753
  7.8 0.0 collective-permute-start
  7.8 0.0 copy-done.6
  7.8 0.0 copy-done.5
  7.8 0.0 copy-done.4
  7.8 0.0 copy-start.2
  7.8 6.9 %pick.1 = (s32[1,8192]{1,0:T(1,128)S(1)}, s32[1,8192]{1,0:T(1,128)S(1)}, s32[3,32]{1,0:T(4,128)S(1)}, f32[1184,128]{1,0:T(8,128)S(1)}, f32[1184,128]{1,0:T(8,128...) custom-call(s32[64,128]{1,0:T(8,128)S(1)} %bitcast.5, s32[64,128]{1,0:T(8,128)S(1)} %bitcast.6, ...), custom_call_target="tpu_custom_call" | custom-call | flops 7000000000 | bytes 1000000 | tf_op jit(solution)/shard_map/pick/pallas_call | solution.py:330
  14.8 0.0 copy-done.2
  14.8 0.0 collective-permute-done.1.high
  14.8 1.5 %collective-permute-done.low = f32[256,128]{1,0:T(8,128)S(1)} collective-permute-done((f32[256,128]{1,0:T(8,128)}, f32[256,128]{1,0:T(8,128)S(1)}, u32[]{:S(2)}, u32[]{:S(2)}) %collective-permute-start) | collective-permute-done | bytes 131104 | tf_op jit(solution)/shard_map/ppermute | solution.py:753
  16.4 2.1 %collective-permute-start.3 = (f32[456,128]{1,0:T(8,128)S(1)}, f32[456,128]{1,0:T(8,128)S(1)}, u32[]{:S(2)}, u32[]{:S(2)}) collective-permute-start(f32[456,128]{1,0:T(8,128)S(1)} %concatenate.7), channel_id=1, source_target_pairs={{0,7},{1,0},{2,1},{3,2},{4,3},{5,4},{6,5},{7,6},{8,15},{9,8},{10,9... | collective-permute-start | bytes 700424 | tf_op jit(solution)/shard_map/ppermute | solution.py:753
  18.5 0.0 collective-permute-start.2
  18.5 2.5 %gather.1.here = f32[1,8192]{1,0:T(1,128)S(1)} custom-call(s32[3,32]{1,0:T(4,128)S(1)} %get-tuple-element.19.work, s32[1,8192]{1,0:T(1,128)S(1)} %get-tuple-element.20.cell, f32[1184,128]{1,0:T(8,128)S(1)} %get-tuple-element.22.chosen), custom_call_target="tpu_custom_call" | custom-call | flops 6000000000 | bytes 2000000 | tf_op jit(solution)/shard_map/gather/pallas_call | solution.py:373
  21.0 1.0 %collective-permute-done.3.right = f32[456,128]{1,0:T(8,128)S(1)} collective-permute-done((f32[456,128]{1,0:T(8,128)S(1)}, f32[456,128]{1,0:T(8,128)S(1)}, u32[]{:S(2)}, u32[]{:S(2)}) %collective-permute-start.3) | collective-permute-done | bytes 233504 | tf_op jit(solution)/shard_map/ppermute | solution.py:753
  22.0 3.2 %collective-permute-done.2.left = f32[456,128]{1,0:T(8,128)S(1)} collective-permute-done((f32[456,128]{1,0:T(8,128)S(1)}, f32[456,128]{1,0:T(8,128)S(1)}, u32[]{:S(2)}, u32[]{:S(2)}) %collective-permute-start.2) | collective-permute-done | bytes 233504 | tf_op jit(solution)/shard_map/ppermute | solution.py:753
  25.2 0.0 slice-start
  25.2 0.0 slice-start.1
  25.2 0.0 slice-start.2
  25.2 11.1 %floes.1 = (f32[1,8192]{1,0:T(1,128)S(1)}, f32[288,128]{1,0:T(8,128)S(1)}, f32[288,128]{1,0:T(8,128)S(1)}, f32[288,128]{1,0:T(8,128)S(1)}) custom-call(s32[1,8192]{1,0:T(1,128)S(1)} %get-tuple-element.20.cell, s32[1,8192]{1,0:T(1,128)S(1)} %get-tuple-element.21.words, f32[1,8192]{1,0:T(1,128)S(1)} %gather.1.here, f32[256,128]{1,0:T(8,128)S(1)} %copy-done.2, ...), custom_call_target="tpu_custom_call" | custom-call | flops 8000000000 | bytes 2000000 | tf_op jit(solution)/shard_map/floes/pallas_call | solution.py:494
  36.3 0.0 collective-permute-start.4
  36.3 2.9 %collective-permute-start.5 = (f32[288,128]{1,0:T(8,128)S(1)}, f32[288,128]{1,0:T(8,128)S(1)}, u32[]{:S(2)}, u32[]{:S(2)}) collective-permute-start(f32[288,128]{1,0:T(8,128)S(1)} %get-tuple-element.30), channel_id=1, source_target_pairs={{0,7},{1,0},{2,1},{3,2},{4,3},{5,4},{6,5},{7,6},{8,15},{9,8},{10,9... | collective-permute-start | bytes 442376 | tf_op jit(solution)/shard_map/ppermute | solution.py:753
  39.2 2.3 %spread.1.dense_take.dense = f32[1184,128]{1,0:T(8,128)S(1)} custom-call(s32[3,32]{1,0:T(4,128)S(1)} %get-tuple-element.19.work, s32[1,8192]{1,0:T(1,128)S(1)} %get-tuple-element.20.cell, f32[1,8192]{1,0:T(1,128)S(1)} %get-tuple-element.27.taken), custom_call_target="tpu_custom_call" | custom-call | flops 3000000000 | bytes 1000000 | tf_op jit(solution)/shard_map/spread/pallas_call | solution.py:534
  41.5 0.5 collective-permute-done.4.left
  42.0 0.0 collective-permute-done.5.right
  42.1 0.1 collective-permute-start.6
  42.2 5.3 %collective-permute-start.7 = (f32[96,128]{1,0:T(8,128)S(1)}, f32[96,128]{1,0:T(8,128)S(1)}, u32[]{:S(2)}, u32[]{:S(2)}) collective-permute-start(f32[96,128]{1,0:T(8,128)S(1)} %get-tuple-element.33), channel_id=1, source_target_pairs={{0,120},{8,0},{16,8},{24,16},{32,24},{40,32},{48,40},{56,48},{64,5... | collective-permute-start | bytes 147464 | tf_op jit(solution)/shard_map/ppermute | solution.py:753
  47.5 0.0 slice-done
  47.5 0.0 slice-done.1
  47.5 0.0 slice-done.2
  47.5 0.0 copy-start
  47.5 0.0 copy-start.1
  47.5 0.0 copy-start.3
  47.5 6.6 %collide.1 = f32[19,32,32,128]{3,2,1,0:T(8,128)} custom-call(f32[1184,128]{1,0:T(8,128)S(1)} %get-tuple-element.18.dense_dir, f32[1184,128]{1,0:T(8,128)S(1)} %spread.1.dense_take.dense, f32[256,128]{1,0:T(8,128)S(1)} %collective-permute-done.low, f32[256,128]{1,0:T(8,128)S(1)} %collective-permute-done.1.high, f32[456,128]{1,0:T(8,128)S(1)} %collective-permute-done.2.left, ...), custom_call_target="tpu_custom_call" | custom-call | flops 40000000 | bytes 24000000 | tf_op jit(solution)/shard_map/collide/pallas_call | solution.py:674
  54.2 0.0 collective-permute-done.6.low
  54.2 0.0 collective-permute-done.7.high
  54.2 0.0 copy-done
  54.2 0.0 copy-done.1
  54.2 0.0 copy-done.3
  54.2 0.7 %motion.1 = f32[6,2048]{1,0:T(8,128)} custom-call(f32[96,128]{1,0:T(8,128)S(1)} %get-tuple-element.31.own, f32[96,128]{1,0:T(8,128)S(1)} %collective-permute-done.6.low, f32[96,128]{1,0:T(8,128)S(1)} %collective-permute-done.7.high, f32[3,2048]{1,0:T(4,128)S(1)} %copy-done.1, f32[6,2048]{1,0:T(8,128)S(1)} %copy-done, f32[2,2048]{1,0:T(2,128)S(1)} %copy-done.3), custom_call_target="tpu_custom_call" | custom-call | flops 200000 | bytes 300000 | tf_op jit(solution)/shard_map/motion/pallas_call | solution.py:740
  (10 shorter events, 0.1 us)
Async XLA Ops:
  0.6 7.2 %copy-start.6 = (s32[1,1,8192]{2,1,0:T(1,128)S(1)}, s32[1,1,8192]{2,1,0:T(1,128)}, u32[]{:S(2)}) copy-start(s32[1,1,8192]{2,1,0:T(1,128)} %param.10) | copy-start | bytes 98308
  0.6 7.2 %copy-start.5 = (s32[1,1,8192]{2,1,0:T(1,128)S(1)}, s32[1,1,8192]{2,1,0:T(1,128)}, u32[]{:S(2)}) copy-start(s32[1,1,8192]{2,1,0:T(1,128)} %param.9) | copy-start | bytes 98308
  0.7 7.2 %copy-start.4 = (s32[1,1,8192]{2,1,0:T(1,128)S(1)}, s32[1,1,8192]{2,1,0:T(1,128)}, u32[]{:S(2)}) copy-start(s32[1,1,8192]{2,1,0:T(1,128)} %param.8) | copy-start | bytes 98308
  2.4 12.4 %collective-permute-start.1 = (f32[256,128]{1,0:T(8,128)}, f32[256,128]{1,0:T(8,128)S(1)}, u32[]{:S(2)}, u32[]{:S(2)}) collective-permute-start(f32[256,128]{1,0:T(8,128)} %get-tuple-element.24), channel_id=1, source_target_pairs={{0,120},{8,0},{16,8},{24,16},{32,24},{40,32},{48,40},{56,48},{64,5... | collective-permute-start | bytes 393224 | tf_op jit(solution)/shard_map/ppermute | solution.py:753
  7.8 8.5 %collective-permute-start = (f32[256,128]{1,0:T(8,128)}, f32[256,128]{1,0:T(8,128)S(1)}, u32[]{:S(2)}, u32[]{:S(2)}) collective-permute-start(f32[256,128]{1,0:T(8,128)} %get-tuple-element.23.mine), channel_id=1, source_target_pairs={{0,8},{8,16},{16,24},{24,32},{32,40},{40,48},{48,56},{56,64},{64,7... | collective-permute-start | bytes 393224 | tf_op jit(solution)/shard_map/ppermute | solution.py:753
  7.8 7.0 %copy-start.2 = (f32[256,128]{1,0:T(8,128)S(1)}, f32[256,128]{1,0:T(8,128)}, u32[]{:S(2)}) copy-start(f32[256,128]{1,0:T(8,128)} %get-tuple-element.23.mine) | copy-start | bytes 393220
  16.4 5.6 %collective-permute-start.3 = (f32[456,128]{1,0:T(8,128)S(1)}, f32[456,128]{1,0:T(8,128)S(1)}, u32[]{:S(2)}, u32[]{:S(2)}) collective-permute-start(f32[456,128]{1,0:T(8,128)S(1)} %concatenate.7), channel_id=1, source_target_pairs={{0,7},{1,0},{2,1},{3,2},{4,3},{5,4},{6,5},{7,6},{8,15},{9,8},{10,9... | collective-permute-start | bytes 700424 | tf_op jit(solution)/shard_map/ppermute | solution.py:753
  18.5 6.7 %collective-permute-start.2 = (f32[456,128]{1,0:T(8,128)S(1)}, f32[456,128]{1,0:T(8,128)S(1)}, u32[]{:S(2)}, u32[]{:S(2)}) collective-permute-start(f32[456,128]{1,0:T(8,128)S(1)} %concatenate.6), channel_id=1, source_target_pairs={{0,1},{1,2},{2,3},{3,4},{4,5},{5,6},{6,7},{7,0},{8,9},{9,10},{10,1... | collective-permute-start | bytes 700424 | tf_op jit(solution)/shard_map/ppermute | solution.py:753
  25.2 22.3 %slice-start = ((s8[9961472]{0:T(1024)(128)(4,1)}), s8[4194304]{0:T(1024)(128)(4,1)S(1)}, s32[]{:S(2)}) async-start(s8[9961472]{0:T(1024)(128)(4,1)} %bitcast.3), calls=%async_computation | async-start | bytes 8388608
  25.2 22.3 %slice-start.1 = ((s8[9961472]{0:T(1024)(128)(4,1)}), s8[4194304]{0:T(1024)(128)(4,1)S(1)}, s32[]{:S(2)}) async-start(s8[9961472]{0:T(1024)(128)(4,1)} %bitcast.3), calls=%async_computation.1 | async-start | bytes 8388608
  25.2 22.3 %slice-start.2 = ((s8[9961472]{0:T(1024)(128)(4,1)}), s8[1572864]{0:T(1024)(128)(4,1)S(1)}, s32[]{:S(2)}) async-start(s8[9961472]{0:T(1024)(128)(4,1)} %bitcast.3), calls=%async_computation.2 | async-start | bytes 3145728
  36.3 5.8 %collective-permute-start.4 = (f32[288,128]{1,0:T(8,128)S(1)}, f32[288,128]{1,0:T(8,128)S(1)}, u32[]{:S(2)}, u32[]{:S(2)}) collective-permute-start(f32[288,128]{1,0:T(8,128)S(1)} %get-tuple-element.29), channel_id=1, source_target_pairs={{0,1},{1,2},{2,3},{3,4},{4,5},{5,6},{6,7},{7,0},{8,9},{9,10},{10,1... | collective-permute-start | bytes 442376 | tf_op jit(solution)/shard_map/ppermute | solution.py:753
  36.3 5.8 %collective-permute-start.5 = (f32[288,128]{1,0:T(8,128)S(1)}, f32[288,128]{1,0:T(8,128)S(1)}, u32[]{:S(2)}, u32[]{:S(2)}) collective-permute-start(f32[288,128]{1,0:T(8,128)S(1)} %get-tuple-element.30), channel_id=1, source_target_pairs={{0,7},{1,0},{2,1},{3,2},{4,3},{5,4},{6,5},{7,6},{8,15},{9,8},{10,9... | collective-permute-start | bytes 442376 | tf_op jit(solution)/shard_map/ppermute | solution.py:753
  42.1 12.1 %collective-permute-start.6 = (f32[96,128]{1,0:T(8,128)S(1)}, f32[96,128]{1,0:T(8,128)S(1)}, u32[]{:S(2)}, u32[]{:S(2)}) collective-permute-start(f32[96,128]{1,0:T(8,128)S(1)} %get-tuple-element.32), channel_id=1, source_target_pairs={{0,8},{8,16},{16,24},{24,32},{32,40},{40,48},{48,56},{56,64},{64,7... | collective-permute-start | bytes 147464 | tf_op jit(solution)/shard_map/ppermute | solution.py:753
  42.2 12.0 %collective-permute-start.7 = (f32[96,128]{1,0:T(8,128)S(1)}, f32[96,128]{1,0:T(8,128)S(1)}, u32[]{:S(2)}, u32[]{:S(2)}) collective-permute-start(f32[96,128]{1,0:T(8,128)S(1)} %get-tuple-element.33), channel_id=1, source_target_pairs={{0,120},{8,0},{16,8},{24,16},{32,24},{40,32},{48,40},{56,48},{64,5... | collective-permute-start | bytes 147464 | tf_op jit(solution)/shard_map/ppermute | solution.py:753
  47.5 6.7 %copy-start = (f32[6,2048]{1,0:T(8,128)S(1)}, f32[6,2048]{1,0:T(8,128)}, u32[]{:S(2)}) copy-start(f32[6,2048]{1,0:T(8,128)} %velocity.1) | copy-start | bytes 147460
  47.5 6.7 %copy-start.1 = (f32[3,2048]{1,0:T(4,128)S(1)}, f32[3,2048]{1,0:T(4,128)}, u32[]{:S(2)}) copy-start(f32[3,2048]{1,0:T(4,128)} %place.1) | copy-start | bytes 73732
  47.5 6.7 %copy-start.3 = (f32[2,2048]{1,0:T(2,128)S(1)}, f32[2,2048]{1,0:T(2,128)}, u32[]{:S(2)}) copy-start(f32[2,2048]{1,0:T(2,128)} %response.1) | copy-start | bytes 49156

commit v4 on v3

--- a/solution.py
+++ b/solution.py
@@ -40,6 +40,10 @@
 MEMBERS = 2048
 GROUPS = MEMBERS // 128
 STATE_ROWS = 6 * GROUPS
+ROWS_NEAR = 9 * GROUPS
+TURNS = 6
+HEIGHT = ROWS_NEAR // TURNS
+TABLE_ROWS = 6 * HEIGHT
 FACE = 5 * WX
 EDGE_ROWS = 8
 WINDOW = 160
@@ -396,7 +400,7 @@
 
 def floe_kernel(
     cell, words, here, mine, low, high, left, right,
-    taken, loads_left, loads_mid, loads_right, table, hot, spread, payload, total,
+    taken, loads_left, loads_mid, loads_right, near, flat, table, hot, spread, payload, total,
 ):
     links = cell.shape[1]
     for ra in range(3):
@@ -407,13 +411,23 @@
                 state = right[ra * STATE_ROWS : (ra + 1) * STATE_ROWS]
             else:
                 state = (low, mine, high)[ra][0:STATE_ROWS]
-            region = ra * 3 + rb
-            lanes = slice(region * 128, (region + 1) * 128)
-            first = state.astype(jnp.bfloat16)
-            table[0:STATE_ROWS, lanes] = first
-            table[STATE_ROWS : 2 * STATE_ROWS, lanes] = (
-                state - first.astype(jnp.float32)
-            ).astype(jnp.bfloat16)
+            first_row = (ra * 3 + rb) * GROUPS
+            for c in range(6):
+                near[c * ROWS_NEAR + first_row : c * ROWS_NEAR + first_row + GROUPS] = state[
+                    c * GROUPS : (c + 1) * GROUPS
+                ]
+    for c in range(6):
+        for q in range(TURNS):
+            flat[c * HEIGHT : (c + 1) * HEIGHT, q * 128 : (q + 1) * 128] = near[
+                pl.ds(c * ROWS_NEAR + q, HEIGHT, stride=TURNS), :
+            ]
+    whole_table = flat[...]
+    top = whole_table.astype(jnp.bfloat16)
+    table[0:TABLE_ROWS] = top
+    table[TABLE_ROWS : 2 * TABLE_ROWS] = (whole_table - top.astype(jnp.float32)).astype(
+        jnp.bfloat16
+    )
+
     def first_half(t):
         slot = t % 2
         at = slice(t * CHUNK, (t + 1) * CHUNK)
@@ -424,11 +438,12 @@
         region = jnp.right_shift(place, 11)
         ra = jnp.right_shift(region * 11, 5)
         rb = region - 3 * ra
-        group = jnp.bitwise_and(jnp.right_shift(place, 7), GROUPS - 1)
-        entry = region * 128 + jnp.bitwise_and(place, 127)
-        rows = lax.broadcasted_iota(jnp.int32, (9 * 128, CHUNK), 0)
+        near_row = jnp.right_shift(place, 7)
+        group = jnp.right_shift(near_row * 171, 10)
+        entry = (near_row - TURNS * group) * 128 + jnp.bitwise_and(place, 127)
+        rows = lax.broadcasted_iota(jnp.int32, (TURNS * 128, CHUNK), 0)
         pick_floe = jnp.where(rows == entry, 1.0, 0.0).astype(jnp.bfloat16)
-        groups = lax.broadcasted_iota(jnp.int32, (GROUPS, CHUNK), 0)
+        groups = lax.broadcasted_iota(jnp.int32, (HEIGHT, CHUNK), 0)
         mask = jnp.where(groups == group, 1.0, 0.0)
 
         cx = component(0, d)
@@ -451,11 +466,11 @@
             (rx * cy - ry * cx) * scale,
         ]
         for c in range(6):
-            spread[slot, c * GROUPS : (c + 1) * GROUPS, :] = mask * coefficients[c]
+            spread[slot, c * HEIGHT : (c + 1) * HEIGHT, :] = mask * coefficients[c]
         hot[slot] = pick_floe
 
         state = product(table[...], pick_floe, NN)
-        state = state[0:STATE_ROWS] + state[STATE_ROWS : 2 * STATE_ROWS]
+        state = state[0:TABLE_ROWS] + state[TABLE_ROWS : 2 * TABLE_ROWS]
         weights = spread[slot]
         speed = jnp.sum(state * weights, axis=0, keepdims=True)
         take = (6.0 * FLOW_SCALE) * weight * speed
@@ -463,8 +478,8 @@
         taken[:, at] = take
         amount = weights * magnitude
         first = amount.astype(jnp.bfloat16)
-        payload[slot, 0:STATE_ROWS, :] = first
-        payload[slot, STATE_ROWS : 2 * STATE_ROWS, :] = (amount - first.astype(jnp.float32)).astype(
+        payload[slot, 0:TABLE_ROWS, :] = first
+        payload[slot, TABLE_ROWS : 2 * TABLE_ROWS, :] = (amount - first.astype(jnp.float32)).astype(
             jnp.bfloat16
         )
 
@@ -481,12 +496,21 @@
         first_half(t)
         second_half(t - 1)
     second_half(steps - 1)
+    flat[...] = total[0:TABLE_ROWS] + total[TABLE_ROWS : 2 * TABLE_ROWS]
+    for c in range(6):
+        for q in range(TURNS):
+            near[pl.ds(c * ROWS_NEAR + q, HEIGHT, stride=TURNS), :] = flat[
+                c * HEIGHT : (c + 1) * HEIGHT, q * 128 : (q + 1) * 128
+            ]
     for ra in range(3):
         for rb in range(3):
-            lanes = slice((ra * 3 + rb) * 128, (ra * 3 + rb + 1) * 128)
-            summed = total[0:STATE_ROWS, lanes] + total[STATE_ROWS : 2 * STATE_ROWS, lanes]
             out = (loads_left, loads_mid, loads_right)[rb]
-            out[ra * STATE_ROWS : (ra + 1) * STATE_ROWS] = summed
+            first_row = (ra * 3 + rb) * GROUPS
+            for c in range(6):
+                at = ra * STATE_ROWS + c * GROUPS
+                out[at : at + GROUPS] = near[
+                    c * ROWS_NEAR + first_row : c * ROWS_NEAR + first_row + GROUPS
+                ]
 
 
 def floes(cell, words, here, mine, low, high, left, right):
@@ -497,11 +521,13 @@
         in_specs=[whole()] * 8,
         out_specs=(whole(),) * 4,
         scratch_shapes=[
-            pltpu.VMEM((2 * STATE_ROWS, 9 * 128), jnp.bfloat16),
-            pltpu.VMEM((2, 9 * 128, CHUNK), jnp.bfloat16),
-            pltpu.VMEM((2, STATE_ROWS, CHUNK), jnp.float32),
-            pltpu.VMEM((2, 2 * STATE_ROWS, CHUNK), jnp.bfloat16),
-            pltpu.VMEM((2 * STATE_ROWS, 9 * 128), jnp.float32),
+            pltpu.VMEM((6 * ROWS_NEAR, 128), jnp.float32),
+            pltpu.VMEM((TABLE_ROWS, TURNS * 128), jnp.float32),
+            pltpu.VMEM((2 * TABLE_ROWS, TURNS * 128), jnp.bfloat16),
+            pltpu.VMEM((2, TURNS * 128, CHUNK), jnp.bfloat16),
+            pltpu.VMEM((2, TABLE_ROWS, CHUNK), jnp.float32),
+            pltpu.VMEM((2, 2 * TABLE_ROWS, CHUNK), jnp.bfloat16),
+            pltpu.VMEM((2 * TABLE_ROWS, TURNS * 128), jnp.float32),
         ],
         compiler_params=params(18),
         cost_estimate=cost(8_000_000_000, 2_000_000),

time: 55.2 us -> 52.9 us (0.958)
  Pallas kernels: 32 us -> 29.7 us
    pallas_call x1, Pallas kernels: 11.1 us -> 8.81 us  [floes(): pl.pallas_call(floe_kernel, out_shape=(jax.ShapeDtypeStruct(cell.shape, j...]
  transfers between devices with their start and end apart: 8 -> 8, of which waited for: 4 -> 4; matrix products, arithmetic and copies ran while one was open for 0% -> 0% of each run, Pallas kernels for 33% -> 35%
where the time goes in v4:
time: 52.9 us; the launch traced here: 52.7 us
  Pallas kernels  29.7 us (56%)
  starting transfers between devices  15.8 us (30%)
  waiting for transfers between devices  6.18 us (12%)
  between operations  0.87 us (2%)
    ppermute x8, starting transfers between devices, shifted(): lax.ppermute(value, axis, [(i, (i + step) % count) for i in range(count)])  15.8 us
    pallas_call x1, Pallas kernels, floes(): pl.pallas_call(floe_kernel, out_shape=(jax.ShapeDtypeStruct(cell.shape, j...  8.81 us
    pallas_call x1, Pallas kernels, pick(): pl.pallas_call(functools.partial(pick_kernel, sizes), out_shape=(row, row...  6.94 us
    pallas_call x1, Pallas kernels, collide(): pl.pallas_call(collide_kernel, out_shape=jax.ShapeDtypeStruct(populations...  6.6 us
    ppermute x8, waiting for transfers between devices, shifted(): lax.ppermute(value, axis, [(i, (i + step) % count) for i in range(count)])  6.18 us
    pallas_call x1, Pallas kernels, gather(): pl.pallas_call(gather_kernel, out_shape=jax.ShapeDtypeStruct(cell.shape,...  2.5 us
    pallas_call x1, Pallas kernels, spread_out(): pl.pallas_call(spread_kernel, out_shape=jax.ShapeDtypeStruct((PADDED_COLU...  2.29 us
    pallas_call x1, Pallas kernels, prepare(): pl.pallas_call(prepare_kernel, out_shape=(shape, shape), in_specs=[hbm(),...  1.78 us
  transfers between devices with their start and end apart: 8, of which 4 were waited for; matrix products, arithmetic and copies ran while one was open for 0% of the time, Pallas kernels for 35%

profile of v4, /device:TPU:0, one launch (start us, length us, event | category | flops | bytes accessed | tf_op | source)
XLA Modules:
  0.0 52.7 jit_solution(3472181248052018378)
XLA Ops:
  0.6 0.0 copy-start.6
  0.6 0.0 copy-start.5
  0.7 0.0 copy-start.4
  0.7 1.8 %prepare.1 = (f32[256,128]{1,0:T(8,128)}, f32[256,128]{1,0:T(8,128)}) custom-call(f32[3,2048]{1,0:T(4,128)} %place.1, f32[6,2048]{1,0:T(8,128)} %velocity.1, f32[19,32,32,128]{3,2,1,0:T(8,128)} %pop_hbm.1), custom_call_target="tpu_custom_call" | custom-call | flops 100000 | bytes 2600000 | tf_op jit(solution)/shard_map/prepare/pallas_call | solution.py:128
  2.4 5.4 %collective-permute-start.1 = (f32[256,128]{1,0:T(8,128)}, f32[256,128]{1,0:T(8,128)S(1)}, u32[]{:S(2)}, u32[]{:S(2)}) collective-permute-start(f32[256,128]{1,0:T(8,128)} %get-tuple-element.24), channel_id=1, source_target_pairs={{0,120},{8,0},{16,8},{24,16},{32,24},{40,32},{48,40},{56,48},{64,5... | collective-permute-start | bytes 393224 | tf_op jit(solution)/shard_map/ppermute | solution.py:779
  7.8 0.0 collective-permute-start
  7.8 0.0 copy-done.6
  7.8 0.0 copy-done.5
  7.8 0.0 copy-done.4
  7.8 0.0 copy-start.2
  7.8 6.9 %pick.1 = (s32[1,8192]{1,0:T(1,128)S(1)}, s32[1,8192]{1,0:T(1,128)S(1)}, s32[3,32]{1,0:T(4,128)S(1)}, f32[1184,128]{1,0:T(8,128)S(1)}, f32[1184,128]{1,0:T(8,128...) custom-call(s32[64,128]{1,0:T(8,128)S(1)} %bitcast.5, s32[64,128]{1,0:T(8,128)S(1)} %bitcast.6, ...), custom_call_target="tpu_custom_call" | custom-call | flops 7000000000 | bytes 1000000 | tf_op jit(solution)/shard_map/pick/pallas_call | solution.py:334
  14.8 0.0 copy-done.2
  14.8 0.0 collective-permute-done.1.high
  14.8 1.5 %collective-permute-done.low = f32[256,128]{1,0:T(8,128)S(1)} collective-permute-done((f32[256,128]{1,0:T(8,128)}, f32[256,128]{1,0:T(8,128)S(1)}, u32[]{:S(2)}, u32[]{:S(2)}) %collective-permute-start) | collective-permute-done | bytes 131104 | tf_op jit(solution)/shard_map/ppermute | solution.py:779
  16.4 2.1 %collective-permute-start.3 = (f32[456,128]{1,0:T(8,128)S(1)}, f32[456,128]{1,0:T(8,128)S(1)}, u32[]{:S(2)}, u32[]{:S(2)}) collective-permute-start(f32[456,128]{1,0:T(8,128)S(1)} %concatenate.7), channel_id=1, source_target_pairs={{0,7},{1,0},{2,1},{3,2},{4,3},{5,4},{6,5},{7,6},{8,15},{9,8},{10,9... | collective-permute-start | bytes 700424 | tf_op jit(solution)/shard_map/ppermute | solution.py:779
  18.5 0.0 collective-permute-start.2
  18.5 2.5 %gather.1.here = f32[1,8192]{1,0:T(1,128)S(1)} custom-call(s32[3,32]{1,0:T(4,128)S(1)} %get-tuple-element.19.work, s32[1,8192]{1,0:T(1,128)S(1)} %get-tuple-element.20.cell, f32[1184,128]{1,0:T(8,128)S(1)} %get-tuple-element.22.chosen), custom_call_target="tpu_custom_call" | custom-call | flops 6000000000 | bytes 2000000 | tf_op jit(solution)/shard_map/gather/pallas_call | solution.py:377
  21.0 1.0 %collective-permute-done.3.right = f32[456,128]{1,0:T(8,128)S(1)} collective-permute-done((f32[456,128]{1,0:T(8,128)S(1)}, f32[456,128]{1,0:T(8,128)S(1)}, u32[]{:S(2)}, u32[]{:S(2)}) %collective-permute-start.3) | collective-permute-done | bytes 233504 | tf_op jit(solution)/shard_map/ppermute | solution.py:779
  22.0 3.2 %collective-permute-done.2.left = f32[456,128]{1,0:T(8,128)S(1)} collective-permute-done((f32[456,128]{1,0:T(8,128)S(1)}, f32[456,128]{1,0:T(8,128)S(1)}, u32[]{:S(2)}, u32[]{:S(2)}) %collective-permute-start.2) | collective-permute-done | bytes 233504 | tf_op jit(solution)/shard_map/ppermute | solution.py:779
  25.2 0.0 slice-start
  25.2 0.0 slice-start.1
  25.2 0.0 slice-start.2
  25.2 8.8 %floes.1 = (f32[1,8192]{1,0:T(1,128)S(1)}, f32[288,128]{1,0:T(8,128)S(1)}, f32[288,128]{1,0:T(8,128)S(1)}, f32[288,128]{1,0:T(8,128)S(1)}) custom-call(s32[1,8192]{1,0:T(1,128)S(1)} %get-tuple-element.20.cell, s32[1,8192]{1,0:T(1,128)S(1)} %get-tuple-element.21.words, f32[1,8192]{1,0:T(1,128)S(1)} %gather.1.here, f32[256,128]{1,0:T(8,128)S(1)} %copy-done.2, ...), custom_call_target="tpu_custom_call" | custom-call | flops 8000000000 | bytes 2000000 | tf_op jit(solution)/shard_map/floes/pallas_call | solution.py:518
  34.0 0.0 collective-permute-start.4
  34.0 2.9 %collective-permute-start.5 = (f32[288,128]{1,0:T(8,128)S(1)}, f32[288,128]{1,0:T(8,128)S(1)}, u32[]{:S(2)}, u32[]{:S(2)}) collective-permute-start(f32[288,128]{1,0:T(8,128)S(1)} %get-tuple-element.30), channel_id=1, source_target_pairs={{0,7},{1,0},{2,1},{3,2},{4,3},{5,4},{6,5},{7,6},{8,15},{9,8},{10,9... | collective-permute-start | bytes 442376 | tf_op jit(solution)/shard_map/ppermute | solution.py:779
  37.0 2.3 %spread.1.dense_take.dense = f32[1184,128]{1,0:T(8,128)S(1)} custom-call(s32[3,32]{1,0:T(4,128)S(1)} %get-tuple-element.19.work, s32[1,8192]{1,0:T(1,128)S(1)} %get-tuple-element.20.cell, f32[1,8192]{1,0:T(1,128)S(1)} %get-tuple-element.27.taken), custom_call_target="tpu_custom_call" | custom-call | flops 3000000000 | bytes 1000000 | tf_op jit(solution)/shard_map/spread/pallas_call | solution.py:560
  39.3 0.5 %collective-permute-done.4.left = f32[288,128]{1,0:T(8,128)S(1)} collective-permute-done((f32[288,128]{1,0:T(8,128)S(1)}, f32[288,128]{1,0:T(8,128)S(1)}, u32[]{:S(2)}, u32[]{:S(2)}) %collective-permute-start.4) | collective-permute-done | bytes 147488 | tf_op jit(solution)/shard_map/ppermute | solution.py:779
  39.8 0.0 collective-permute-done.5.right
  39.8 0.1 collective-permute-start.6
  39.9 5.3 %collective-permute-start.7 = (f32[96,128]{1,0:T(8,128)S(1)}, f32[96,128]{1,0:T(8,128)S(1)}, u32[]{:S(2)}, u32[]{:S(2)}) collective-permute-start(f32[96,128]{1,0:T(8,128)S(1)} %get-tuple-element.33), channel_id=1, source_target_pairs={{0,120},{8,0},{16,8},{24,16},{32,24},{40,32},{48,40},{56,48},{64,5... | collective-permute-start | bytes 147464 | tf_op jit(solution)/shard_map/ppermute | solution.py:779
  45.2 0.0 slice-done
  45.2 0.0 slice-done.1
  45.2 0.0 slice-done.2
  45.2 0.0 copy-start
  45.3 0.0 copy-start.1
  45.3 0.0 copy-start.3
  45.3 6.6 %collide.1 = f32[19,32,32,128]{3,2,1,0:T(8,128)} custom-call(f32[1184,128]{1,0:T(8,128)S(1)} %get-tuple-element.18.dense_dir, f32[1184,128]{1,0:T(8,128)S(1)} %spread.1.dense_take.dense, f32[256,128]{1,0:T(8,128)S(1)} %collective-permute-done.low, f32[256,128]{1,0:T(8,128)S(1)} %collective-permute-done.1.high, f32[456,128]{1,0:T(8,128)S(1)} %collective-permute-done.2.left, ...), custom_call_target="tpu_custom_call" | custom-call | flops 40000000 | bytes 24000000 | tf_op jit(solution)/shard_map/collide/pallas_call | solution.py:700
  51.9 0.0 collective-permute-done.6.low
  51.9 0.0 collective-permute-done.7.high
  51.9 0.0 copy-done
  51.9 0.0 copy-done.1
  51.9 0.0 copy-done.3
  51.9 0.7 %motion.1 = f32[6,2048]{1,0:T(8,128)} custom-call(f32[96,128]{1,0:T(8,128)S(1)} %get-tuple-element.31.own, f32[96,128]{1,0:T(8,128)S(1)} %collective-permute-done.6.low, f32[96,128]{1,0:T(8,128)S(1)} %collective-permute-done.7.high, f32[3,2048]{1,0:T(4,128)S(1)} %copy-done.1, f32[6,2048]{1,0:T(8,128)S(1)} %copy-done, f32[2,2048]{1,0:T(2,128)S(1)} %copy-done.3), custom_call_target="tpu_custom_call" | custom-call | flops 200000 | bytes 300000 | tf_op jit(solution)/shard_map/motion/pallas_call | solution.py:766
  (10 shorter events, 0.1 us)
Async XLA Ops:
  0.6 7.2 %copy-start.6 = (s32[1,1,8192]{2,1,0:T(1,128)S(1)}, s32[1,1,8192]{2,1,0:T(1,128)}, u32[]{:S(2)}) copy-start(s32[1,1,8192]{2,1,0:T(1,128)} %param.10) | copy-start | bytes 98308
  0.6 7.2 %copy-start.5 = (s32[1,1,8192]{2,1,0:T(1,128)S(1)}, s32[1,1,8192]{2,1,0:T(1,128)}, u32[]{:S(2)}) copy-start(s32[1,1,8192]{2,1,0:T(1,128)} %param.9) | copy-start | bytes 98308
  0.7 7.2 %copy-start.4 = (s32[1,1,8192]{2,1,0:T(1,128)S(1)}, s32[1,1,8192]{2,1,0:T(1,128)}, u32[]{:S(2)}) copy-start(s32[1,1,8192]{2,1,0:T(1,128)} %param.8) | copy-start | bytes 98308
  2.4 12.4 %collective-permute-start.1 = (f32[256,128]{1,0:T(8,128)}, f32[256,128]{1,0:T(8,128)S(1)}, u32[]{:S(2)}, u32[]{:S(2)}) collective-permute-start(f32[256,128]{1,0:T(8,128)} %get-tuple-element.24), channel_id=1, source_target_pairs={{0,120},{8,0},{16,8},{24,16},{32,24},{40,32},{48,40},{56,48},{64,5... | collective-permute-start | bytes 393224 | tf_op jit(solution)/shard_map/ppermute | solution.py:779
  7.8 8.5 %collective-permute-start = (f32[256,128]{1,0:T(8,128)}, f32[256,128]{1,0:T(8,128)S(1)}, u32[]{:S(2)}, u32[]{:S(2)}) collective-permute-start(f32[256,128]{1,0:T(8,128)} %get-tuple-element.23.mine), channel_id=1, source_target_pairs={{0,8},{8,16},{16,24},{24,32},{32,40},{40,48},{48,56},{56,64},{64,7... | collective-permute-start | bytes 393224 | tf_op jit(solution)/shard_map/ppermute | solution.py:779
  7.8 7.0 %copy-start.2 = (f32[256,128]{1,0:T(8,128)S(1)}, f32[256,128]{1,0:T(8,128)}, u32[]{:S(2)}) copy-start(f32[256,128]{1,0:T(8,128)} %get-tuple-element.23.mine) | copy-start | bytes 393220
  16.4 5.6 %collective-permute-start.3 = (f32[456,128]{1,0:T(8,128)S(1)}, f32[456,128]{1,0:T(8,128)S(1)}, u32[]{:S(2)}, u32[]{:S(2)}) collective-permute-start(f32[456,128]{1,0:T(8,128)S(1)} %concatenate.7), channel_id=1, source_target_pairs={{0,7},{1,0},{2,1},{3,2},{4,3},{5,4},{6,5},{7,6},{8,15},{9,8},{10,9... | collective-permute-start | bytes 700424 | tf_op jit(solution)/shard_map/ppermute | solution.py:779
  18.5 6.7 %collective-permute-start.2 = (f32[456,128]{1,0:T(8,128)S(1)}, f32[456,128]{1,0:T(8,128)S(1)}, u32[]{:S(2)}, u32[]{:S(2)}) collective-permute-start(f32[456,128]{1,0:T(8,128)S(1)} %concatenate.6), channel_id=1, source_target_pairs={{0,1},{1,2},{2,3},{3,4},{4,5},{5,6},{6,7},{7,0},{8,9},{9,10},{10,1... | collective-permute-start | bytes 700424 | tf_op jit(solution)/shard_map/ppermute | solution.py:779
  25.2 20.1 %slice-start = ((s8[9961472]{0:T(1024)(128)(4,1)}), s8[4194304]{0:T(1024)(128)(4,1)S(1)}, s32[]{:S(2)}) async-start(s8[9961472]{0:T(1024)(128)(4,1)} %bitcast.3), calls=%async_computation | async-start | bytes 8388608
  25.2 20.1 %slice-start.1 = ((s8[9961472]{0:T(1024)(128)(4,1)}), s8[4194304]{0:T(1024)(128)(4,1)S(1)}, s32[]{:S(2)}) async-start(s8[9961472]{0:T(1024)(128)(4,1)} %bitcast.3), calls=%async_computation.1 | async-start | bytes 8388608
  25.2 20.1 %slice-start.2 = ((s8[9961472]{0:T(1024)(128)(4,1)}), s8[1572864]{0:T(1024)(128)(4,1)S(1)}, s32[]{:S(2)}) async-start(s8[9961472]{0:T(1024)(128)(4,1)} %bitcast.3), calls=%async_computation.2 | async-start | bytes 3145728
  34.0 5.8 %collective-permute-start.4 = (f32[288,128]{1,0:T(8,128)S(1)}, f32[288,128]{1,0:T(8,128)S(1)}, u32[]{:S(2)}, u32[]{:S(2)}) collective-permute-start(f32[288,128]{1,0:T(8,128)S(1)} %get-tuple-element.29), channel_id=1, source_target_pairs={{0,1},{1,2},{2,3},{3,4},{4,5},{5,6},{6,7},{7,0},{8,9},{9,10},{10,1... | collective-permute-start | bytes 442376 | tf_op jit(solution)/shard_map/ppermute | solution.py:779
  34.0 5.8 %collective-permute-start.5 = (f32[288,128]{1,0:T(8,128)S(1)}, f32[288,128]{1,0:T(8,128)S(1)}, u32[]{:S(2)}, u32[]{:S(2)}) collective-permute-start(f32[288,128]{1,0:T(8,128)S(1)} %get-tuple-element.30), channel_id=1, source_target_pairs={{0,7},{1,0},{2,1},{3,2},{4,3},{5,4},{6,5},{7,6},{8,15},{9,8},{10,9... | collective-permute-start | bytes 442376 | tf_op jit(solution)/shard_map/ppermute | solution.py:779
  39.8 12.1 %collective-permute-start.6 = (f32[96,128]{1,0:T(8,128)S(1)}, f32[96,128]{1,0:T(8,128)S(1)}, u32[]{:S(2)}, u32[]{:S(2)}) collective-permute-start(f32[96,128]{1,0:T(8,128)S(1)} %get-tuple-element.32), channel_id=1, source_target_pairs={{0,8},{8,16},{16,24},{24,32},{32,40},{40,48},{48,56},{56,64},{64,7... | collective-permute-start | bytes 147464 | tf_op jit(solution)/shard_map/ppermute | solution.py:779
  39.9 12.0 %collective-permute-start.7 = (f32[96,128]{1,0:T(8,128)S(1)}, f32[96,128]{1,0:T(8,128)S(1)}, u32[]{:S(2)}, u32[]{:S(2)}) collective-permute-start(f32[96,128]{1,0:T(8,128)S(1)} %get-tuple-element.33), channel_id=1, source_target_pairs={{0,120},{8,0},{16,8},{24,16},{32,24},{40,32},{48,40},{56,48},{64,5... | collective-permute-start | bytes 147464 | tf_op jit(solution)/shard_map/ppermute | solution.py:779
  45.2 6.7 %copy-start = (f32[6,2048]{1,0:T(8,128)S(1)}, f32[6,2048]{1,0:T(8,128)}, u32[]{:S(2)}) copy-start(f32[6,2048]{1,0:T(8,128)} %velocity.1) | copy-start | bytes 147460
  45.3 6.7 %copy-start.1 = (f32[3,2048]{1,0:T(4,128)S(1)}, f32[3,2048]{1,0:T(4,128)}, u32[]{:S(2)}) copy-start(f32[3,2048]{1,0:T(4,128)} %place.1) | copy-start | bytes 73732
  45.3 6.7 %copy-start.3 = (f32[2,2048]{1,0:T(2,128)S(1)}, f32[2,2048]{1,0:T(2,128)}, u32[]{:S(2)}) copy-start(f32[2,2048]{1,0:T(2,128)} %response.1) | copy-start | bytes 49156

commit v5 on v4

--- a/solution.py
+++ b/solution.py
@@ -290,7 +290,7 @@
         chosen[rows, :] = value
         return carry
 
-    lax.fori_loop(0, WX, select, 0, unroll=2)
+    lax.fori_loop(0, WX, select, 0, unroll=8)
 
 
 def window_adder(dense):

time: 52.9 us -> 52.9 us (level)
  transfers between devices with their start and end apart: 8 -> 8, of which waited for: 4 -> 4; matrix products, arithmetic and copies ran while one was open for 0% -> 0% of each run, Pallas kernels for 35% -> 34%
where the time goes in v5:
time: 52.9 us; the launch traced here: 52.7 us
  Pallas kernels  29.5 us (56%)
  starting transfers between devices  15.8 us (30%)
  waiting for transfers between devices  6.35 us (12%)
  between operations  0.87 us (2%)
    ppermute x8, starting transfers between devices, shifted(): lax.ppermute(value, axis, [(i, (i + step) % count) for i in range(count)])  15.8 us
    pallas_call x1, Pallas kernels, floes(): pl.pallas_call(floe_kernel, out_shape=(jax.ShapeDtypeStruct(cell.shape, j...  8.81 us
    pallas_call x1, Pallas kernels, pick(): pl.pallas_call(functools.partial(pick_kernel, sizes), out_shape=(row, row...  6.76 us
    pallas_call x1, Pallas kernels, collide(): pl.pallas_call(collide_kernel, out_shape=jax.ShapeDtypeStruct(populations...  6.6 us
    ppermute x8, waiting for transfers between devices, shifted(): lax.ppermute(value, axis, [(i, (i + step) % count) for i in range(count)])  6.35 us
    pallas_call x1, Pallas kernels, gather(): pl.pallas_call(gather_kernel, out_shape=jax.ShapeDtypeStruct(cell.shape,...  2.5 us
    pallas_call x1, Pallas kernels, spread_out(): pl.pallas_call(spread_kernel, out_shape=jax.ShapeDtypeStruct((PADDED_COLU...  2.29 us
    pallas_call x1, Pallas kernels, prepare(): pl.pallas_call(prepare_kernel, out_shape=(shape, shape), in_specs=[hbm(),...  1.78 us
  transfers between devices with their start and end apart: 8, of which 4 were waited for; matrix products, arithmetic and copies ran while one was open for 0% of the time, Pallas kernels for 34%

profile of v5, /device:TPU:0, one launch (start us, length us, event | category | flops | bytes accessed | tf_op | source)
XLA Modules:
  0.0 52.7 jit_solution(2232326444992592563)
XLA Ops:
  0.6 0.0 copy-start.6
  0.6 0.0 copy-start.5
  0.7 0.0 copy-start.4
  0.7 1.8 %prepare.1 = (f32[256,128]{1,0:T(8,128)}, f32[256,128]{1,0:T(8,128)}) custom-call(f32[3,2048]{1,0:T(4,128)} %place.1, f32[6,2048]{1,0:T(8,128)} %velocity.1, f32[19,32,32,128]{3,2,1,0:T(8,128)} %pop_hbm.1), custom_call_target="tpu_custom_call" | custom-call | flops 100000 | bytes 2600000 | tf_op jit(solution)/shard_map/prepare/pallas_call | solution.py:128
  2.4 5.4 %collective-permute-start.1 = (f32[256,128]{1,0:T(8,128)}, f32[256,128]{1,0:T(8,128)S(1)}, u32[]{:S(2)}, u32[]{:S(2)}) collective-permute-start(f32[256,128]{1,0:T(8,128)} %get-tuple-element.24), channel_id=1, source_target_pairs={{0,120},{8,0},{16,8},{24,16},{32,24},{40,32},{48,40},{56,48},{64,5... | collective-permute-start | bytes 393224 | tf_op jit(solution)/shard_map/ppermute | solution.py:779
  7.8 0.0 collective-permute-start
  7.8 0.0 copy-done.6
  7.8 0.0 copy-done.5
  7.8 0.0 copy-done.4
  7.8 0.0 copy-start.2
  7.8 6.8 %pick.1 = (s32[1,8192]{1,0:T(1,128)S(1)}, s32[1,8192]{1,0:T(1,128)S(1)}, s32[3,32]{1,0:T(4,128)S(1)}, f32[1184,128]{1,0:T(8,128)S(1)}, f32[1184,128]{1,0:T(8,128...) custom-call(s32[64,128]{1,0:T(8,128)S(1)} %bitcast.5, s32[64,128]{1,0:T(8,128)S(1)} %bitcast.6, ...), custom_call_target="tpu_custom_call" | custom-call | flops 7000000000 | bytes 1000000 | tf_op jit(solution)/shard_map/pick/pallas_call | solution.py:334
  14.6 0.0 copy-done.2
  14.6 0.0 collective-permute-done.1.high
  14.7 1.6 %collective-permute-done.low = f32[256,128]{1,0:T(8,128)S(1)} collective-permute-done((f32[256,128]{1,0:T(8,128)}, f32[256,128]{1,0:T(8,128)S(1)}, u32[]{:S(2)}, u32[]{:S(2)}) %collective-permute-start) | collective-permute-done | bytes 131104 | tf_op jit(solution)/shard_map/ppermute | solution.py:779
  16.4 2.1 %collective-permute-start.3 = (f32[456,128]{1,0:T(8,128)S(1)}, f32[456,128]{1,0:T(8,128)S(1)}, u32[]{:S(2)}, u32[]{:S(2)}) collective-permute-start(f32[456,128]{1,0:T(8,128)S(1)} %concatenate.7), channel_id=1, source_target_pairs={{0,7},{1,0},{2,1},{3,2},{4,3},{5,4},{6,5},{7,6},{8,15},{9,8},{10,9... | collective-permute-start | bytes 700424 | tf_op jit(solution)/shard_map/ppermute | solution.py:779
  18.5 0.0 collective-permute-start.2
  18.5 2.5 %gather.1.here = f32[1,8192]{1,0:T(1,128)S(1)} custom-call(s32[3,32]{1,0:T(4,128)S(1)} %get-tuple-element.19.work, s32[1,8192]{1,0:T(1,128)S(1)} %get-tuple-element.20.cell, f32[1184,128]{1,0:T(8,128)S(1)} %get-tuple-element.22.chosen), custom_call_target="tpu_custom_call" | custom-call | flops 6000000000 | bytes 2000000 | tf_op jit(solution)/shard_map/gather/pallas_call | solution.py:377
  21.0 1.0 %collective-permute-done.3.right = f32[456,128]{1,0:T(8,128)S(1)} collective-permute-done((f32[456,128]{1,0:T(8,128)S(1)}, f32[456,128]{1,0:T(8,128)S(1)}, u32[]{:S(2)}, u32[]{:S(2)}) %collective-permute-start.3) | collective-permute-done | bytes 233504 | tf_op jit(solution)/shard_map/ppermute | solution.py:779
  22.0 3.2 %collective-permute-done.2.left = f32[456,128]{1,0:T(8,128)S(1)} collective-permute-done((f32[456,128]{1,0:T(8,128)S(1)}, f32[456,128]{1,0:T(8,128)S(1)}, u32[]{:S(2)}, u32[]{:S(2)}) %collective-permute-start.2) | collective-permute-done | bytes 233504 | tf_op jit(solution)/shard_map/ppermute | solution.py:779
  25.2 0.0 slice-start
  25.2 0.0 slice-start.1
  25.2 0.0 slice-start.2
  25.2 8.8 %floes.1 = (f32[1,8192]{1,0:T(1,128)S(1)}, f32[288,128]{1,0:T(8,128)S(1)}, f32[288,128]{1,0:T(8,128)S(1)}, f32[288,128]{1,0:T(8,128)S(1)}) custom-call(s32[1,8192]{1,0:T(1,128)S(1)} %get-tuple-element.20.cell, s32[1,8192]{1,0:T(1,128)S(1)} %get-tuple-element.21.words, f32[1,8192]{1,0:T(1,128)S(1)} %gather.1.here, f32[256,128]{1,0:T(8,128)S(1)} %copy-done.2, ...), custom_call_target="tpu_custom_call" | custom-call | flops 8000000000 | bytes 2000000 | tf_op jit(solution)/shard_map/floes/pallas_call | solution.py:518
  34.0 0.0 collective-permute-start.4
  34.0 2.9 %collective-permute-start.5 = (f32[288,128]{1,0:T(8,128)S(1)}, f32[288,128]{1,0:T(8,128)S(1)}, u32[]{:S(2)}, u32[]{:S(2)}) collective-permute-start(f32[288,128]{1,0:T(8,128)S(1)} %get-tuple-element.30), channel_id=1, source_target_pairs={{0,7},{1,0},{2,1},{3,2},{4,3},{5,4},{6,5},{7,6},{8,15},{9,8},{10,9... | collective-permute-start | bytes 442376 | tf_op jit(solution)/shard_map/ppermute | solution.py:779
  37.0 2.3 %spread.1.dense_take.dense = f32[1184,128]{1,0:T(8,128)S(1)} custom-call(s32[3,32]{1,0:T(4,128)S(1)} %get-tuple-element.19.work, s32[1,8192]{1,0:T(1,128)S(1)} %get-tuple-element.20.cell, f32[1,8192]{1,0:T(1,128)S(1)} %get-tuple-element.27.taken), custom_call_target="tpu_custom_call" | custom-call | flops 3000000000 | bytes 1000000 | tf_op jit(solution)/shard_map/spread/pallas_call | solution.py:560
  39.3 0.5 %collective-permute-done.4.left = f32[288,128]{1,0:T(8,128)S(1)} collective-permute-done((f32[288,128]{1,0:T(8,128)S(1)}, f32[288,128]{1,0:T(8,128)S(1)}, u32[]{:S(2)}, u32[]{:S(2)}) %collective-permute-start.4) | collective-permute-done | bytes 147488 | tf_op jit(solution)/shard_map/ppermute | solution.py:779
  39.8 0.0 collective-permute-done.5.right
  39.8 0.1 collective-permute-start.6
  39.9 5.3 %collective-permute-start.7 = (f32[96,128]{1,0:T(8,128)S(1)}, f32[96,128]{1,0:T(8,128)S(1)}, u32[]{:S(2)}, u32[]{:S(2)}) collective-permute-start(f32[96,128]{1,0:T(8,128)S(1)} %get-tuple-element.33), channel_id=1, source_target_pairs={{0,120},{8,0},{16,8},{24,16},{32,24},{40,32},{48,40},{56,48},{64,5... | collective-permute-start | bytes 147464 | tf_op jit(solution)/shard_map/ppermute | solution.py:779
  45.2 0.0 slice-done
  45.2 0.0 slice-done.1
  45.2 0.0 slice-done.2
  45.2 0.0 copy-start
  45.3 0.0 copy-start.1
  45.3 0.0 copy-start.3
  45.3 6.6 %collide.1 = f32[19,32,32,128]{3,2,1,0:T(8,128)} custom-call(f32[1184,128]{1,0:T(8,128)S(1)} %get-tuple-element.18.dense_dir, f32[1184,128]{1,0:T(8,128)S(1)} %spread.1.dense_take.dense, f32[256,128]{1,0:T(8,128)S(1)} %collective-permute-done.low, f32[256,128]{1,0:T(8,128)S(1)} %collective-permute-done.1.high, f32[456,128]{1,0:T(8,128)S(1)} %collective-permute-done.2.left, ...), custom_call_target="tpu_custom_call" | custom-call | flops 40000000 | bytes 24000000 | tf_op jit(solution)/shard_map/collide/pallas_call | solution.py:700
  51.9 0.0 collective-permute-done.6.low
  51.9 0.0 collective-permute-done.7.high
  51.9 0.0 copy-done
  51.9 0.0 copy-done.1
  51.9 0.0 copy-done.3
  51.9 0.7 %motion.1 = f32[6,2048]{1,0:T(8,128)} custom-call(f32[96,128]{1,0:T(8,128)S(1)} %get-tuple-element.31.own, f32[96,128]{1,0:T(8,128)S(1)} %collective-permute-done.6.low, f32[96,128]{1,0:T(8,128)S(1)} %collective-permute-done.7.high, f32[3,2048]{1,0:T(4,128)S(1)} %copy-done.1, f32[6,2048]{1,0:T(8,128)S(1)} %copy-done, f32[2,2048]{1,0:T(2,128)S(1)} %copy-done.3), custom_call_target="tpu_custom_call" | custom-call | flops 200000 | bytes 300000 | tf_op jit(solution)/shard_map/motion/pallas_call | solution.py:766
  (10 shorter events, 0.1 us)
Async XLA Ops:
  0.6 7.2 %copy-start.6 = (s32[1,1,8192]{2,1,0:T(1,128)S(1)}, s32[1,1,8192]{2,1,0:T(1,128)}, u32[]{:S(2)}) copy-start(s32[1,1,8192]{2,1,0:T(1,128)} %param.10) | copy-start | bytes 98308
  0.6 7.2 %copy-start.5 = (s32[1,1,8192]{2,1,0:T(1,128)S(1)}, s32[1,1,8192]{2,1,0:T(1,128)}, u32[]{:S(2)}) copy-start(s32[1,1,8192]{2,1,0:T(1,128)} %param.9) | copy-start | bytes 98308
  0.7 7.2 %copy-start.4 = (s32[1,1,8192]{2,1,0:T(1,128)S(1)}, s32[1,1,8192]{2,1,0:T(1,128)}, u32[]{:S(2)}) copy-start(s32[1,1,8192]{2,1,0:T(1,128)} %param.8) | copy-start | bytes 98308
  2.4 12.2 %collective-permute-start.1 = (f32[256,128]{1,0:T(8,128)}, f32[256,128]{1,0:T(8,128)S(1)}, u32[]{:S(2)}, u32[]{:S(2)}) collective-permute-start(f32[256,128]{1,0:T(8,128)} %get-tuple-element.24), channel_id=1, source_target_pairs={{0,120},{8,0},{16,8},{24,16},{32,24},{40,32},{48,40},{56,48},{64,5... | collective-permute-start | bytes 393224 | tf_op jit(solution)/shard_map/ppermute | solution.py:779
  7.8 8.5 %collective-permute-start = (f32[256,128]{1,0:T(8,128)}, f32[256,128]{1,0:T(8,128)S(1)}, u32[]{:S(2)}, u32[]{:S(2)}) collective-permute-start(f32[256,128]{1,0:T(8,128)} %get-tuple-element.23.mine), channel_id=1, source_target_pairs={{0,8},{8,16},{16,24},{24,32},{32,40},{40,48},{48,56},{56,64},{64,7... | collective-permute-start | bytes 393224 | tf_op jit(solution)/shard_map/ppermute | solution.py:779
  7.8 6.8 %copy-start.2 = (f32[256,128]{1,0:T(8,128)S(1)}, f32[256,128]{1,0:T(8,128)}, u32[]{:S(2)}) copy-start(f32[256,128]{1,0:T(8,128)} %get-tuple-element.23.mine) | copy-start | bytes 393220
  16.4 5.6 %collective-permute-start.3 = (f32[456,128]{1,0:T(8,128)S(1)}, f32[456,128]{1,0:T(8,128)S(1)}, u32[]{:S(2)}, u32[]{:S(2)}) collective-permute-start(f32[456,128]{1,0:T(8,128)S(1)} %concatenate.7), channel_id=1, source_target_pairs={{0,7},{1,0},{2,1},{3,2},{4,3},{5,4},{6,5},{7,6},{8,15},{9,8},{10,9... | collective-permute-start | bytes 700424 | tf_op jit(solution)/shard_map/ppermute | solution.py:779
  18.5 6.7 %collective-permute-start.2 = (f32[456,128]{1,0:T(8,128)S(1)}, f32[456,128]{1,0:T(8,128)S(1)}, u32[]{:S(2)}, u32[]{:S(2)}) collective-permute-start(f32[456,128]{1,0:T(8,128)S(1)} %concatenate.6), channel_id=1, source_target_pairs={{0,1},{1,2},{2,3},{3,4},{4,5},{5,6},{6,7},{7,0},{8,9},{9,10},{10,1... | collective-permute-start | bytes 700424 | tf_op jit(solution)/shard_map/ppermute | solution.py:779
  25.2 20.1 %slice-start = ((s8[9961472]{0:T(1024)(128)(4,1)}), s8[4194304]{0:T(1024)(128)(4,1)S(1)}, s32[]{:S(2)}) async-start(s8[9961472]{0:T(1024)(128)(4,1)} %bitcast.3), calls=%async_computation | async-start | bytes 8388608
  25.2 20.1 %slice-start.1 = ((s8[9961472]{0:T(1024)(128)(4,1)}), s8[4194304]{0:T(1024)(128)(4,1)S(1)}, s32[]{:S(2)}) async-start(s8[9961472]{0:T(1024)(128)(4,1)} %bitcast.3), calls=%async_computation.1 | async-start | bytes 8388608
  25.2 20.1 %slice-start.2 = ((s8[9961472]{0:T(1024)(128)(4,1)}), s8[1572864]{0:T(1024)(128)(4,1)S(1)}, s32[]{:S(2)}) async-start(s8[9961472]{0:T(1024)(128)(4,1)} %bitcast.3), calls=%async_computation.2 | async-start | bytes 3145728
  34.0 5.8 %collective-permute-start.4 = (f32[288,128]{1,0:T(8,128)S(1)}, f32[288,128]{1,0:T(8,128)S(1)}, u32[]{:S(2)}, u32[]{:S(2)}) collective-permute-start(f32[288,128]{1,0:T(8,128)S(1)} %get-tuple-element.29), channel_id=1, source_target_pairs={{0,1},{1,2},{2,3},{3,4},{4,5},{5,6},{6,7},{7,0},{8,9},{9,10},{10,1... | collective-permute-start | bytes 442376 | tf_op jit(solution)/shard_map/ppermute | solution.py:779
  34.0 5.8 %collective-permute-start.5 = (f32[288,128]{1,0:T(8,128)S(1)}, f32[288,128]{1,0:T(8,128)S(1)}, u32[]{:S(2)}, u32[]{:S(2)}) collective-permute-start(f32[288,128]{1,0:T(8,128)S(1)} %get-tuple-element.30), channel_id=1, source_target_pairs={{0,7},{1,0},{2,1},{3,2},{4,3},{5,4},{6,5},{7,6},{8,15},{9,8},{10,9... | collective-permute-start | bytes 442376 | tf_op jit(solution)/shard_map/ppermute | solution.py:779
  39.8 12.1 %collective-permute-start.6 = (f32[96,128]{1,0:T(8,128)S(1)}, f32[96,128]{1,0:T(8,128)S(1)}, u32[]{:S(2)}, u32[]{:S(2)}) collective-permute-start(f32[96,128]{1,0:T(8,128)S(1)} %get-tuple-element.32), channel_id=1, source_target_pairs={{0,8},{8,16},{16,24},{24,32},{32,40},{40,48},{48,56},{56,64},{64,7... | collective-permute-start | bytes 147464 | tf_op jit(solution)/shard_map/ppermute | solution.py:779
  39.9 12.0 %collective-permute-start.7 = (f32[96,128]{1,0:T(8,128)S(1)}, f32[96,128]{1,0:T(8,128)S(1)}, u32[]{:S(2)}, u32[]{:S(2)}) collective-permute-start(f32[96,128]{1,0:T(8,128)S(1)} %get-tuple-element.33), channel_id=1, source_target_pairs={{0,120},{8,0},{16,8},{24,16},{32,24},{40,32},{48,40},{56,48},{64,5... | collective-permute-start | bytes 147464 | tf_op jit(solution)/shard_map/ppermute | solution.py:779
  45.2 6.7 %copy-start = (f32[6,2048]{1,0:T(8,128)S(1)}, f32[6,2048]{1,0:T(8,128)}, u32[]{:S(2)}) copy-start(f32[6,2048]{1,0:T(8,128)} %velocity.1) | copy-start | bytes 147460
  45.3 6.7 %copy-start.1 = (f32[3,2048]{1,0:T(4,128)S(1)}, f32[3,2048]{1,0:T(4,128)}, u32[]{:S(2)}) copy-start(f32[3,2048]{1,0:T(4,128)} %place.1) | copy-start | bytes 73732
  45.3 6.7 %copy-start.3 = (f32[2,2048]{1,0:T(2,128)S(1)}, f32[2,2048]{1,0:T(2,128)}, u32[]{:S(2)}) copy-start(f32[2,2048]{1,0:T(2,128)} %response.1) | copy-start | bytes 49156
